TPU v7x, 32 devices: a whole 2x2x4 slice. The times are simulated.
32 devices in a mesh: ctx: 16 (over z, x, core), head: 2 (over y).
Axes of the slice: x: 2, y: 2, z: 4, core: 2. Of those that a mesh axis runs over, the one named last changes fastest.
Arguments:
- queries: bfloat16 [4096, 4096], P(('ctx', 'head')), may hold values from -6 to 6
- keys: bfloat16 [4096, 1024], P(('ctx', 'head')), may hold values from -6 to 6
- values: bfloat16 [4096, 1024], P(('ctx', 'head')), may hold values from -1.5 to 1.5
- out_grad: bfloat16 [4096, 4096], P(('ctx', 'head')), may hold values from -6 to 6
- log_norm: float32 [4096, 32], P(('ctx', 'head')), may hold values from 2 to 4
- row_delta: float32 [4096, 32], P(('ctx', 'head')), may hold values from -10 to 10
- tile_pairs: int32 [16, 4, 4, 2], P('ctx'), may hold values from 0 to 1, as said below
- pair_count: int32 [16, 4], P('ctx'), may hold values from 0 to 4, as said below
Outputs:
- query_grad: bfloat16 [4096, 4096], P(('ctx', 'head'))
- key_grad: bfloat16 [4096, 1024], P(('ctx', 'head'))
- value_grad: bfloat16 [4096, 1024], P(('ctx', 'head'))
Inputs may be any that keep to these rules, and one draw needn't show every extreme that they name: `tile_pairs`: Entries past pair_count are not read.
All inputs are finite; a program needn't handle non-finite values.
Results may differ from a plain program's by a relative error of at most 0.005.
Values may be sent and summed in bfloat16 or wider, within the bound.
No kernel may reach another device: no remote copies, remote signals or barrier semaphores. Data moves between devices by JAX's collectives and lax.ppermute only.
A program may use at most 64 MiB of HBM per device.

v0:
```python
import jax
import jax.numpy as jnp
from jax import lax
from jax.sharding import PartitionSpec as P

HEAD_DIM = 128
TILE = 128
WIN = 4


def shifted(block, axis, distance):
    devices = range(lax.axis_size(axis))
    route = [(i - distance, i) for i in devices if i - distance in devices]
    return lax.ppermute(block, axis, route)


def from_behind(value, axis, steps):
    count = lax.axis_size(axis)
    pairs = [(source, (source + steps) % count) for source in range(count)]
    return lax.ppermute(value, axis, pairs)


def tile_terms(
    query_tile, grad_tile, norm_tile, delta_tile, key_tile, value_tile, allowed, scaling
):
    scores = (
        jnp.einsum("ikgd,jkd->kgij", query_tile, key_tile, preferred_element_type=jnp.float32)
        * scaling
    )
    probs = jnp.where(allowed, jnp.exp(scores - norm_tile), 0.0)
    prob_grad = jnp.einsum(
        "ikgd,jkd->kgij", grad_tile, value_tile, preferred_element_type=jnp.float32
    )
    score_grad = (scaling * probs * (prob_grad - delta_tile)).astype(jnp.bfloat16)
    probs_low = probs.astype(jnp.bfloat16)
    query_term = jnp.einsum(
        "kgij,jkd->ikgd", score_grad, key_tile, preferred_element_type=jnp.float32
    )
    key_term = jnp.einsum(
        "kgij,ikgd->jkd", score_grad, query_tile, preferred_element_type=jnp.float32
    )
    value_term = jnp.einsum(
        "kgij,ikgd->jkd", probs_low, grad_tile, preferred_element_type=jnp.float32
    )
    return (query_term, key_term, value_term)


def add_rows(total, term, start):
    current = lax.dynamic_slice_in_dim(total, start, term.shape[0], 0)
    return lax.dynamic_update_slice_in_dim(total, current + term, start, 0)


def per_device(queries, keys, values, out_grad, log_norm, row_delta, tile_pairs, pair_count):
    query_rows, key_rows, value_rows, grad_rows = (
        lax.all_to_all(queries, "head", split_axis=1, concat_axis=0, tiled=True),
        lax.all_to_all(keys, "head", split_axis=1, concat_axis=0, tiled=True),
        lax.all_to_all(values, "head", split_axis=1, concat_axis=0, tiled=True),
        lax.all_to_all(out_grad, "head", split_axis=1, concat_axis=0, tiled=True),
    )
    norm_rows, delta_rows = (
        lax.all_to_all(log_norm, "head", split_axis=1, concat_axis=0, tiled=True),
        lax.all_to_all(row_delta, "head", split_axis=1, concat_axis=0, tiled=True),
    )
    block_len = query_rows.shape[0]
    local_heads = norm_rows.shape[1]
    local_kv = key_rows.shape[1] // HEAD_DIM
    group_size = local_heads // local_kv
    list_len = tile_pairs.shape[2]
    scaling = HEAD_DIM ** (-0.5)
    query_four = query_rows.reshape(block_len, local_kv, group_size, HEAD_DIM)
    grad_four = grad_rows.reshape(block_len, local_kv, group_size, HEAD_DIM)
    norm_cols = jnp.transpose(norm_rows.reshape(block_len, local_kv, group_size), (1, 2, 0))[
        ..., None
    ]
    delta_cols = jnp.transpose(delta_rows.reshape(block_len, local_kv, group_size), (1, 2, 0))[
        ..., None
    ]
    positions = jnp.arange(TILE, dtype=jnp.int32)
    lower_tri = positions[None, :] <= positions[:, None]
    query_total = jnp.zeros((block_len, local_kv, group_size, HEAD_DIM), jnp.float32)
    key_now, value_now = (key_rows, value_rows)
    key_total = jnp.zeros((block_len, local_kv * HEAD_DIM), jnp.float32)
    value_total = jnp.zeros((block_len, local_kv * HEAD_DIM), jnp.float32)
    for cycle_step in range(WIN):
        if cycle_step > 0:
            key_now, value_now = shifted((key_now, value_now), "ctx", 1)
        key_three = key_now.reshape(block_len, local_kv, HEAD_DIM)
        value_three = value_now.reshape(block_len, local_kv, HEAD_DIM)
        pair_list = tile_pairs[0, cycle_step]
        live_count = pair_count[0, cycle_step]
        causal = cycle_step == 0

        def slot_body(
            slot,
            state,
            pair_list=pair_list,
            live_count=live_count,
            causal=causal,
            key_three=key_three,
            value_three=value_three,
        ):
            q_total, k_step, v_step = state
            q_start = pair_list[slot, 0] * TILE
            k_start = pair_list[slot, 1] * TILE
            allowed = jnp.broadcast_to(slot < live_count, (TILE, TILE))
            if causal:
                allowed = allowed & ((q_start != k_start) | lower_tri)
            query_term, key_term, value_term = tile_terms(
                lax.dynamic_slice_in_dim(query_four, q_start, TILE, 0),
                lax.dynamic_slice_in_dim(grad_four, q_start, TILE, 0),
                lax.dynamic_slice_in_dim(norm_cols, q_start, TILE, 2),
                lax.dynamic_slice_in_dim(delta_cols, q_start, TILE, 2),
                lax.dynamic_slice_in_dim(key_three, k_start, TILE, 0),
                lax.dynamic_slice_in_dim(value_three, k_start, TILE, 0),
                allowed,
                scaling,
            )
            return (
                add_rows(q_total, query_term, q_start),
                add_rows(k_step, key_term, k_start),
                add_rows(v_step, value_term, k_start),
            )

        step_start = (
            query_total,
            jnp.zeros((block_len, local_kv, HEAD_DIM), jnp.float32),
            jnp.zeros((block_len, local_kv, HEAD_DIM), jnp.float32),
        )
        query_total, key_step, value_step = lax.fori_loop(0, list_len, slot_body, step_start)
        key_term = key_step.reshape(block_len, local_kv * HEAD_DIM)
        value_term = value_step.reshape(block_len, local_kv * HEAD_DIM)
        if cycle_step == 0:
            key_total, value_total = (key_term, value_term)
        else:
            key_total, value_total = from_behind((key_total, value_total), "ctx", 1)
            key_total = key_total + key_term
            value_total = value_total + value_term
    key_total, value_total = (
        from_behind(key_total.astype(jnp.bfloat16), "ctx", -(WIN - 1)).astype(key_total.dtype),
        from_behind(value_total.astype(jnp.bfloat16), "ctx", -(WIN - 1)).astype(value_total.dtype),
    )
    query_grad = query_total.reshape(block_len, local_heads * HEAD_DIM).astype(jnp.bfloat16)
    return (
        lax.all_to_all(query_grad, "head", split_axis=0, concat_axis=1, tiled=True),
        lax.all_to_all(
            key_total.astype(jnp.bfloat16), "head", split_axis=0, concat_axis=1, tiled=True
        ),
        lax.all_to_all(
            value_total.astype(jnp.bfloat16), "head", split_axis=0, concat_axis=1, tiled=True
        ),
    )


def solution(mesh):
    in_specs = (
        P(("ctx", "head"), None),
        P(("ctx", "head"), None),
        P(("ctx", "head"), None),
        P(("ctx", "head"), None),
        P(("ctx", "head"), None),
        P(("ctx", "head"), None),
        P("ctx", None, None, None),
        P("ctx", None),
    )
    out_specs = (P(("ctx", "head"), None), P(("ctx", "head"), None), P(("ctx", "head"), None))
    return jax.shard_map(
        per_device, mesh=mesh, in_specs=in_specs, out_specs=out_specs, check_vma=False
    )
```

profile of v0, /device:TPU:0, one launch (start us, length us, event | category | flops | bytes accessed | tf_op | source)
XLA Modules:
  0.0 262.3 jit_solution(9477888267651087087)
XLA Ops:
  0.6 8.2 %all_to_all.156 = f32[128,2,16]{0,2,1:T(8,128)S(1)} all-to-all(f32[128,2,16]{0,2,1:T(8,128)} %bitcast.464), channel_id=1, replica_groups=mesh['ctx'=16,'head'=2] {'head'}, dimensions={1} | all-to-all | bytes 32768 | tf_op jit(solution)/shard_map/all_to_all | solution.py:61
  8.9 3.2 %all-to-all-start.5 = ((f32[128,2,16]{0,2,1:T(8,128)}), f32[128,2,16]{0,2,1:T(8,128)S(1)}, u32[]{:S(2)}, u32[]{:S(2)}) async-start(f32[128,2,16]{0,2,1:T(8,128)} %bitcast.465), calls=%async_computation.5 | async-start | bytes 32768 | tf_op jit(solution)/shard_map/all_to_all | solution.py:62
  16.0 3.4 %all-to-all-start = ((bf16[128,2,512]{0,2,1:T(8,128)(2,1)}), bf16[128,2,512]{0,2,1:T(8,128)(2,1)S(1)}, u32[]{:S(2)}, u32[]{:S(2)}) async-start(bf16[128,2,512]{0,2,1:T(8,128)(2,1)} %bitcast.55), calls=%async_computation | async-start | bytes 524288 | tf_op jit(solution)/shard_map/all_to_all | solution.py:56
  21.2 3.4 %all-to-all-done = bf16[128,2,512]{0,2,1:T(8,128)(2,1)S(1)} async-done(((bf16[128,2,512]{0,2,1:T(8,128)(2,1)}), bf16[128,2,512]{0,2,1:T(8,128)(2,1)S(1)}, u32[]{:S(2)}, u32[]{:S(2)}) %all-to-all-start) | async-done | bytes 262176 | tf_op jit(solution)/shard_map/all_to_all | solution.py:56
  24.6 3.4 %all-to-all-start.3 = ((bf16[128,2,512]{0,2,1:T(8,128)(2,1)}), bf16[128,2,512]{0,2,1:T(8,128)(2,1)S(1)}, u32[]{:S(2)}, u32[]{:S(2)}) async-start(bf16[128,2,512]{0,2,1:T(8,128)(2,1)} %bitcast.63), calls=%async_computation.3 | async-start | bytes 524288 | tf_op jit(solution)/shard_map/all_to_all | solution.py:57
  29.1 4.1 %all-to-all-done.3 = bf16[128,2,512]{0,2,1:T(8,128)(2,1)S(1)} async-done(((bf16[128,2,512]{0,2,1:T(8,128)(2,1)}), bf16[128,2,512]{0,2,1:T(8,128)(2,1)S(1)}, u32[]{:S(2)}, u32[]{:S(2)}) %all-to-all-start.3) | async-done | bytes 262176 | tf_op jit(solution)/shard_map/all_to_all | solution.py:57
  33.2 3.6 %all-to-all-start.1 = ((bf16[128,2,2048]{2,0,1:T(8,128)(2,1)}), bf16[128,2,2048]{2,0,1:T(8,128)(2,1)S(1)}, u32[]{:S(2)}, u32[]{:S(2)}) async-start(bf16[128,2,2048]{2,0,1:T(8,128)(2,1)} %bitcast.328), calls=%async_computation.1 | async-start | bytes 2097152 | tf_op jit(solution)/shard_map/all_to_all | solution.py:55
  37.9 8.4 %all-to-all-done.1 = bf16[128,2,2048]{2,0,1:T(8,128)(2,1)S(1)} async-done(((bf16[128,2,2048]{2,0,1:T(8,128)(2,1)}), bf16[128,2,2048]{2,0,1:T(8,128)(2,1)S(1)}, u32[]{:S(2)}, u32[]{:S(2)}) %all-to-all-start.1) | async-done | bytes 1048608 | tf_op jit(solution)/shard_map/all_to_all | solution.py:55
  46.2 3.6 %all-to-all-start.4 = ((bf16[128,2,2048]{2,0,1:T(8,128)(2,1)}), bf16[128,2,2048]{2,0,1:T(8,128)(2,1)S(1)}, u32[]{:S(2)}, u32[]{:S(2)}) async-start(bf16[128,2,2048]{2,0,1:T(8,128)(2,1)} %bitcast.327), calls=%async_computation.4 | async-start | bytes 2097152 | tf_op jit(solution)/shard_map/all_to_all | solution.py:58
  52.1 4.5 %collective-permute-start.1 = (bf16[256,512]{1,0:T(8,128)(2,1)S(1)}, bf16[256,512]{1,0:T(8,128)(2,1)}, u32[]{:S(2)}, u32[]{:S(2)}) collective-permute-start(bf16[256,512]{1,0:T(8,128)(2,1)S(1)} %bitcast.454), channel_id=1, source_target_pairs={{0,2},{2,4},{4,6},{6,8},{8,10},{10,12},{12,14},{14,16},{16,18},{18... | collective-permute-start | bytes 786440 | tf_op jit(solution)/shard_map/ppermute | solution.py:14
  64.5 3.5 %collective-permute-start.3 = (bf16[256,512]{1,0:T(8,128)(2,1)}, bf16[256,512]{1,0:T(8,128)(2,1)}, u32[]{:S(2)}, u32[]{:S(2)}) collective-permute-start(bf16[256,512]{1,0:T(8,128)(2,1)} %collective-permute-done.1), channel_id=1, source_target_pairs={{0,2},{2,4},{4,6},{6,8},{8,10},{10,12},{12,14},{14,16},{16,18},{18... | collective-permute-start | bytes 786440 | tf_op jit(solution)/shard_map/ppermute | solution.py:14
  71.7 30.7 %while.72 = (s32[]{:T(128)}, f32[256,4,4,128]{0,3,2,1:T(8,128)}, f32[256,4,128]{0,2,1:T(8,128)S(1)}, f32[256,4,128]{0,2,1:T(8,128)S(1)}, s32[4,2]{0,1:T(2,128)S(...) while((s32[]{:T(128)}, f32[256,4,4,128]{0,3,2,1:T(8,128)}, ...), condition=%wide.region_1.2_spmd.clone, body=%wide.region_0.1_spmd.clone.sunk | while | flops 338083840 | bytes 10961213 | solution.py:129
  76.1 2.6 fusion.235
  106.4 30.2 %while.69 = (s32[]{:T(128)}, f32[256,4,4,128]{0,3,2,1:T(8,128)}, f32[256,4,128]{0,2,1:T(8,128)S(1)}, f32[256,4,128]{0,2,1:T(8,128)S(1)}, s32[4,2]{0,1:T(2,128)S(...) while((s32[]{:T(128)}, f32[256,4,4,128]{0,3,2,1:T(8,128)}, ...), condition=%wide.region_3.4_spmd, body=%wide.region_2.3_spmd.sunk | while | flops 338034688 | bytes 10404155 | solution.py:129
  139.0 2.7 %collective-permute-start.4 = (bf16[256,512]{1,0:T(8,128)(2,1)}, bf16[256,512]{1,0:T(8,128)(2,1)}, u32[]{:S(2)}, u32[]{:S(2)}) collective-permute-start(bf16[256,512]{1,0:T(8,128)(2,1)} %collective-permute-done.2), channel_id=1, source_target_pairs={{0,2},{2,4},{4,6},{6,8},{8,10},{10,12},{12,14},{14,16},{16,18},{18... | collective-permute-start | bytes 786440 | tf_op jit(solution)/shard_map/ppermute | solution.py:14
  143.4 2.6 collective-permute-start.5
  151.9 30.0 %while.70 = (s32[]{:T(128)}, f32[256,4,4,128]{0,3,2,1:T(8,128)}, f32[256,4,128]{0,2,1:T(8,128)S(1)}, f32[256,4,128]{0,2,1:T(8,128)S(1)}, s32[4,2]{0,1:T(2,128)S(...) while((s32[]{:T(128)}, f32[256,4,4,128]{0,3,2,1:T(8,128)}, ...), condition=%wide.region_5.6_spmd, body=%wide.region_4.5_spmd.sunk | while | flops 338034688 | bytes 10404155 | solution.py:129
  190.9 30.0 %while.71 = (s32[]{:T(128)}, f32[256,4,4,128]{0,3,2,1:T(8,128)}, f32[256,4,128]{0,2,1:T(8,128)S(1)}, f32[256,4,128]{0,2,1:T(8,128)S(1)}, s32[4,2]{0,1:T(2,128)S(...) while((s32[]{:T(128)}, f32[256,4,4,128]{0,3,2,1:T(8,128)}, ...), condition=%wide.region_7.8_spmd, body=%wide.region_6.7_spmd.sunk | while | flops 338034688 | bytes 10404155 | solution.py:129
  226.1 3.6 %all-to-all-start.6 = ((bf16[2,128,2048]{2,1,0:T(8,128)(2,1)}), bf16[2,128,2048]{2,1,0:T(8,128)(2,1)S(1)}, u32[]{:S(2)}, u32[]{:S(2)}) async-start(bf16[2,128,2048]{2,1,0:T(8,128)(2,1)} %copy.350), calls=%async_computation.6 | async-start | bytes 2097152 | tf_op jit(solution)/shard_map/all_to_all | solution.py:144
  230.9 2.6 collective-permute-start.13
  234.7 9.4 %all-to-all-done.6 = bf16[2,128,2048]{2,1,0:T(8,128)(2,1)S(1)} async-done(((bf16[2,128,2048]{2,1,0:T(8,128)(2,1)}), bf16[2,128,2048]{2,1,0:T(8,128)(2,1)S(1)}, u32[]{:S(2)}, u32[]{:S(2)}) %all-to-all-start.6) | async-done | bytes 1048608 | tf_op jit(solution)/shard_map/all_to_all | solution.py:144
  244.0 3.4 %all-to-all-start.8 = ((bf16[2,128,512]{2,1,0:T(8,128)(2,1)}), bf16[2,128,512]{2,1,0:T(8,128)(2,1)S(1)}, u32[]{:S(2)}, u32[]{:S(2)}) async-start(bf16[2,128,512]{2,1,0:T(8,128)(2,1)} %bitcast.97), calls=%async_computation.8 | async-start | bytes 524288 | tf_op jit(solution)/shard_map/all_to_all | solution.py:148
  247.5 5.1 %all-to-all-done.8 = bf16[2,128,512]{2,1,0:T(8,128)(2,1)S(1)} async-done(((bf16[2,128,512]{2,1,0:T(8,128)(2,1)}), bf16[2,128,512]{2,1,0:T(8,128)(2,1)S(1)}, u32[]{:S(2)}, u32[]{:S(2)}) %all-to-all-start.8) | async-done | bytes 262176 | tf_op jit(solution)/shard_map/all_to_all | solution.py:148
  252.6 3.4 %all-to-all-start.7 = ((bf16[2,128,512]{2,1,0:T(8,128)(2,1)}), bf16[2,128,512]{2,1,0:T(8,128)(2,1)S(1)}, u32[]{:S(2)}, u32[]{:S(2)}) async-start(bf16[2,128,512]{2,1,0:T(8,128)(2,1)} %bitcast.90), calls=%async_computation.7 | async-start | bytes 524288 | tf_op jit(solution)/shard_map/all_to_all | solution.py:145
  (213 shorter events, 144.7 us)
Async XLA Ops:
  0.6 27.4 %copy-start.2 = (bf16[128,4096]{1,0:T(8,128)(2,1)S(1)}, bf16[128,4096]{1,0:T(8,128)(2,1)}, u32[]{:S(2)}) copy-start(bf16[128,4096]{1,0:T(8,128)(2,1)} %param.16) | copy-start | bytes 3145732
  8.9 7.1 %all-to-all-start.5 = ((f32[128,2,16]{0,2,1:T(8,128)}), f32[128,2,16]{0,2,1:T(8,128)S(1)}, u32[]{:S(2)}, u32[]{:S(2)}) async-start(f32[128,2,16]{0,2,1:T(8,128)} %bitcast.465), calls=%async_computation.5 | async-start | bytes 32768 | tf_op jit(solution)/shard_map/all_to_all | solution.py:62
  16.0 8.6 %all-to-all-start = ((bf16[128,2,512]{0,2,1:T(8,128)(2,1)}), bf16[128,2,512]{0,2,1:T(8,128)(2,1)S(1)}, u32[]{:S(2)}, u32[]{:S(2)}) async-start(bf16[128,2,512]{0,2,1:T(8,128)(2,1)} %bitcast.55), calls=%async_computation | async-start | bytes 524288 | tf_op jit(solution)/shard_map/all_to_all | solution.py:56
  24.6 8.6 %all-to-all-start.3 = ((bf16[128,2,512]{0,2,1:T(8,128)(2,1)}), bf16[128,2,512]{0,2,1:T(8,128)(2,1)S(1)}, u32[]{:S(2)}, u32[]{:S(2)}) async-start(bf16[128,2,512]{0,2,1:T(8,128)(2,1)} %bitcast.63), calls=%async_computation.3 | async-start | bytes 524288 | tf_op jit(solution)/shard_map/all_to_all | solution.py:57
  33.2 13.1 %all-to-all-start.1 = ((bf16[128,2,2048]{2,0,1:T(8,128)(2,1)}), bf16[128,2,2048]{2,0,1:T(8,128)(2,1)S(1)}, u32[]{:S(2)}, u32[]{:S(2)}) async-start(bf16[128,2,2048]{2,0,1:T(8,128)(2,1)} %bitcast.328), calls=%async_computation.1 | async-start | bytes 2097152 | tf_op jit(solution)/shard_map/all_to_all | solution.py:55
  37.9 19.4 %copy-start.5 = (s32[1,4,4,2]{2,3,1,0:T(2,128)S(1)}, s32[1,4,4,2]{2,3,1,0:T(2,128)}, u32[]{:S(2)}) copy-start(s32[1,4,4,2]{2,3,1,0:T(2,128)} %param.22) | copy-start | bytes 388
  46.2 22.8 %all-to-all-start.4 = ((bf16[128,2,2048]{2,0,1:T(8,128)(2,1)}), bf16[128,2,2048]{2,0,1:T(8,128)(2,1)S(1)}, u32[]{:S(2)}, u32[]{:S(2)}) async-start(bf16[128,2,2048]{2,0,1:T(8,128)(2,1)} %bitcast.327), calls=%async_computation.4 | async-start | bytes 2097152 | tf_op jit(solution)/shard_map/all_to_all | solution.py:58
  50.1 8.8 %collective-permute-start = (bf16[256,512]{1,0:T(8,128)(2,1)S(1)}, bf16[256,512]{1,0:T(8,128)(2,1)}, u32[]{:S(2)}, u32[]{:S(2)}) collective-permute-start(bf16[256,512]{1,0:T(8,128)(2,1)S(1)} %bitcast.456), channel_id=1, source_target_pairs={{0,2},{2,4},{4,6},{6,8},{8,10},{10,12},{12,14},{14,16},{16,18},{18... | collective-permute-start | bytes 786440 | tf_op jit(solution)/shard_map/ppermute | solution.py:14
  52.1 10.6 %collective-permute-start.1 = (bf16[256,512]{1,0:T(8,128)(2,1)S(1)}, bf16[256,512]{1,0:T(8,128)(2,1)}, u32[]{:S(2)}, u32[]{:S(2)}) collective-permute-start(bf16[256,512]{1,0:T(8,128)(2,1)S(1)} %bitcast.454), channel_id=1, source_target_pairs={{0,2},{2,4},{4,6},{6,8},{8,10},{10,12},{12,14},{14,16},{16,18},{18... | collective-permute-start | bytes 786440 | tf_op jit(solution)/shard_map/ppermute | solution.py:14
  60.7 77.2 %collective-permute-start.2 = (bf16[256,512]{1,0:T(8,128)(2,1)}, bf16[256,512]{1,0:T(8,128)(2,1)}, u32[]{:S(2)}, u32[]{:S(2)}) collective-permute-start(bf16[256,512]{1,0:T(8,128)(2,1)} %collective-permute-done), channel_id=1, source_target_pairs={{0,2},{2,4},{4,6},{6,8},{8,10},{10,12},{12,14},{14,16},{16,18},{18... | collective-permute-start | bytes 786440 | tf_op jit(solution)/shard_map/ppermute | solution.py:14
  64.5 77.1 %collective-permute-start.3 = (bf16[256,512]{1,0:T(8,128)(2,1)}, bf16[256,512]{1,0:T(8,128)(2,1)}, u32[]{:S(2)}, u32[]{:S(2)}) collective-permute-start(bf16[256,512]{1,0:T(8,128)(2,1)} %collective-permute-done.1), channel_id=1, source_target_pairs={{0,2},{2,4},{4,6},{6,8},{8,10},{10,12},{12,14},{14,16},{16,18},{18... | collective-permute-start | bytes 786440 | tf_op jit(solution)/shard_map/ppermute | solution.py:14
  103.5 42.6 %collective-permute-start.10 = (f32[256,512]{1,0:T(8,128)}, f32[256,512]{1,0:T(8,128)}, u32[]{:S(2)}, u32[]{:S(2)}) collective-permute-start(f32[256,512]{1,0:T(8,128)} %copy.355), channel_id=1, source_target_pairs={{0,2},{2,4},{4,6},{6,8},{8,10},{10,12},{12,14},{14,16},{16,18},{18... | collective-permute-start | bytes 1572872 | tf_op jit(solution)/shard_map/ppermute | solution.py:20
  104.5 43.6 %collective-permute-start.6 = (f32[256,512]{1,0:T(8,128)}, f32[256,512]{1,0:T(8,128)}, u32[]{:S(2)}, u32[]{:S(2)}) collective-permute-start(f32[256,512]{1,0:T(8,128)} %copy.351), channel_id=1, source_target_pairs={{0,2},{2,4},{4,6},{6,8},{8,10},{10,12},{12,14},{14,16},{16,18},{18... | collective-permute-start | bytes 1572872 | tf_op jit(solution)/shard_map/ppermute | solution.py:20
  139.0 44.2 %collective-permute-start.4 = (bf16[256,512]{1,0:T(8,128)(2,1)}, bf16[256,512]{1,0:T(8,128)(2,1)}, u32[]{:S(2)}, u32[]{:S(2)}) collective-permute-start(bf16[256,512]{1,0:T(8,128)(2,1)} %collective-permute-done.2), channel_id=1, source_target_pairs={{0,2},{2,4},{4,6},{6,8},{8,10},{10,12},{12,14},{14,16},{16,18},{18... | collective-permute-start | bytes 786440 | tf_op jit(solution)/shard_map/ppermute | solution.py:14
  143.4 40.8 %collective-permute-start.5 = (bf16[256,512]{1,0:T(8,128)(2,1)}, bf16[256,512]{1,0:T(8,128)(2,1)}, u32[]{:S(2)}, u32[]{:S(2)}) collective-permute-start(bf16[256,512]{1,0:T(8,128)(2,1)} %collective-permute-done.3), channel_id=1, source_target_pairs={{0,2},{2,4},{4,6},{6,8},{8,10},{10,12},{12,14},{14,16},{16,18},{18... | collective-permute-start | bytes 786440 | tf_op jit(solution)/shard_map/ppermute | solution.py:14
  148.1 37.9 %collective-permute-start.11 = (f32[256,512]{1,0:T(8,128)}, f32[256,512]{1,0:T(8,128)}, u32[]{:S(2)}, u32[]{:S(2)}) collective-permute-start(f32[256,512]{1,0:T(8,128)} %add.289), channel_id=1, source_target_pairs={{0,2},{2,4},{4,6},{6,8},{8,10},{10,12},{12,14},{14,16},{16,18},{18... | collective-permute-start | bytes 1572872 | tf_op jit(solution)/shard_map/ppermute | solution.py:20
  150.0 38.1 %collective-permute-start.7 = (f32[256,512]{1,0:T(8,128)}, f32[256,512]{1,0:T(8,128)}, u32[]{:S(2)}, u32[]{:S(2)}) collective-permute-start(f32[256,512]{1,0:T(8,128)} %add.286), channel_id=1, source_target_pairs={{0,2},{2,4},{4,6},{6,8},{8,10},{10,12},{12,14},{14,16},{16,18},{18... | collective-permute-start | bytes 1572872 | tf_op jit(solution)/shard_map/ppermute | solution.py:20
  188.1 41.6 %collective-permute-start.12 = (f32[256,512]{1,0:T(8,128)}, f32[256,512]{1,0:T(8,128)}, u32[]{:S(2)}, u32[]{:S(2)}) collective-permute-start(f32[256,512]{1,0:T(8,128)} %add.290), channel_id=1, source_target_pairs={{0,2},{2,4},{4,6},{6,8},{8,10},{10,12},{12,14},{14,16},{16,18},{18... | collective-permute-start | bytes 1572872 | tf_op jit(solution)/shard_map/ppermute | solution.py:20
  190.1 43.4 %collective-permute-start.8 = (f32[256,512]{1,0:T(8,128)}, f32[256,512]{1,0:T(8,128)}, u32[]{:S(2)}, u32[]{:S(2)}) collective-permute-start(f32[256,512]{1,0:T(8,128)} %add.287), channel_id=1, source_target_pairs={{0,2},{2,4},{4,6},{6,8},{8,10},{10,12},{12,14},{14,16},{16,18},{18... | collective-permute-start | bytes 1572872 | tf_op jit(solution)/shard_map/ppermute | solution.py:20
  226.1 17.9 %all-to-all-start.6 = ((bf16[2,128,2048]{2,1,0:T(8,128)(2,1)}), bf16[2,128,2048]{2,1,0:T(8,128)(2,1)S(1)}, u32[]{:S(2)}, u32[]{:S(2)}) async-start(bf16[2,128,2048]{2,1,0:T(8,128)(2,1)} %copy.350), calls=%async_computation.6 | async-start | bytes 2097152 | tf_op jit(solution)/shard_map/all_to_all | solution.py:144
  230.9 13.2 %collective-permute-start.13 = (bf16[256,512]{1,0:T(8,128)(2,1)S(1)}, bf16[256,512]{1,0:T(8,128)(2,1)}, u32[]{:S(2)}, u32[]{:S(2)}) collective-permute-start(bf16[256,512]{1,0:T(8,128)(2,1)S(1)} %add_convert_fusion), channel_id=1, source_target_pairs={{0,26},{2,28},{4,30},{6,0},{8,2},{10,4},{12,6},{14,8},{16,10},{18,... | collective-permute-start | bytes 786440 | tf_op jit(solution)/shard_map/ppermute | solution.py:20
  234.6 12.9 %collective-permute-start.9 = (bf16[256,512]{1,0:T(8,128)(2,1)S(1)}, bf16[256,512]{1,0:T(8,128)(2,1)}, u32[]{:S(2)}, u32[]{:S(2)}) collective-permute-start(bf16[256,512]{1,0:T(8,128)(2,1)S(1)} %add_convert_fusion.1), channel_id=1, source_target_pairs={{0,26},{2,28},{4,30},{6,0},{8,2},{10,4},{12,6},{14,8},{16,10},{18,... | collective-permute-start | bytes 786440 | tf_op jit(solution)/shard_map/ppermute | solution.py:20
  244.0 8.6 %all-to-all-start.8 = ((bf16[2,128,512]{2,1,0:T(8,128)(2,1)}), bf16[2,128,512]{2,1,0:T(8,128)(2,1)S(1)}, u32[]{:S(2)}, u32[]{:S(2)}) async-start(bf16[2,128,512]{2,1,0:T(8,128)(2,1)} %bitcast.97), calls=%async_computation.8 | async-start | bytes 524288 | tf_op jit(solution)/shard_map/all_to_all | solution.py:148
  252.6 8.6 %all-to-all-start.7 = ((bf16[2,128,512]{2,1,0:T(8,128)(2,1)}), bf16[2,128,512]{2,1,0:T(8,128)(2,1)S(1)}, u32[]{:S(2)}, u32[]{:S(2)}) async-start(bf16[2,128,512]{2,1,0:T(8,128)(2,1)} %bitcast.90), calls=%async_computation.7 | async-start | bytes 524288 | tf_op jit(solution)/shard_map/all_to_all | solution.py:145
  (4 other events, 36.0 us)
where the time goes:
time: 265 us; the launch traced here: 262 us
  matrix products  74.7 us (28%)
  starting transfers between devices  52.1 us (20%)
  local copies, waits for them, and re-layouts  47.8 us (18%)
  waiting for transfers between devices  34.5 us (13%)
  loops' own time  31.8 us (12%)
  other arithmetic  12 us (5%)
  blocking collectives  8.23 us (3%)
    dot_general x16, matrix products, tile_terms(): jnp.einsum('kgij,jkd->ikgd', score_grad, key_tile, preferred_element_type...  40.7 us
    another operation x4, loops' own time, per_device(): lax.fori_loop(0, list_len, slot_body, step_start)  31.8 us
    ppermute x6, starting transfers between devices, shifted(): return lax.ppermute(block, axis, route)  17.2 us
    dot_general x16, matrix products, tile_terms(): jnp.einsum('ikgd,jkd->kgij', grad_tile, value_tile, preferred_element_typ...  16.5 us
    dynamic_slice x16, local copies, waits for them, and re-layouts, slot_body(): k_start = pair_list[slot, 1] * TILE  9.88 us
    all_to_all x1, waiting for transfers between devices, per_device(): lax.all_to_all(query_grad, 'head', split_axis=0, concat_axis=1, tiled=True)  9.36 us
    ppermute x6, local copies, waits for them, and re-layouts, shifted(): return lax.ppermute(block, axis, route)  9.32 us
    all_to_all x1, waiting for transfers between devices, per_device(): lax.all_to_all(queries, 'head', split_axis=1, concat_axis=0, tiled=True)  8.35 us
  transfers between devices with their start and end apart: 22, of which 7 were waited for; matrix products, arithmetic and copies ran while one was open for 51% of the time, Pallas kernels for 0%

commit v1 on v0

v1 whole, which is shorter than its diff:
```python
import functools

import jax
import jax.numpy as jnp
from jax import lax
from jax.experimental import pallas as pl
from jax.experimental.pallas import tpu as pltpu
from jax.sharding import PartitionSpec as P

HEAD_DIM = 128
TILE = 128
WIN = 4
LOG2E = 1.4426950408889634
FAR = 1e30
NT = (((1,), (1,)), ((), ()))
NN = (((1,), (0,)), ((), ()))


def dot(a, b, dims):
    return lax.dot_general(a, b, dims, preferred_element_type=jnp.float32)


def swap(value, axis):
    return lax.ppermute(value, axis, [(i, i ^ 1) for i in range(lax.axis_size(axis))])


def routed(value, route, backwards=False):
    count = lax.axis_size("ctx")
    pairs = [(c, route(c)) for c in range(count) if route(c) < count]
    if backwards:
        pairs = [(b, a) for a, b in pairs]
    return lax.ppermute(value, "ctx", pairs)


def two_on(c):
    return c + 2


def one_or_three_on(c):
    return c + 1 if c % 2 == 0 else c + 3


def kernel(tiles, group, slots, split, *refs):
    place, pairs, counts = refs[:3]
    refs = refs[3:]
    if split:
        q_mine, q_far, g_mine, g_far, k_mine, v_mine, kv_far = refs[:7]
        refs = refs[7:]
        q_tile = lambda t: (q_mine if t == 0 else q_far)
        g_tile = lambda t: (g_mine if t == 0 else g_far)
    else:
        q_all, g_all, kv_own = refs[:3]
        refs = refs[3:]
        q_tile = lambda t: q_all.at[t]
        g_tile = lambda t: g_all.at[t]
    rows_ref, kv_two, kv_core, kv_odd = refs[:4]
    refs = refs[4:]
    dq_refs = refs[:2] if split else refs[:1]
    refs = refs[len(dq_refs) :]
    d_own, d_two, d_core, d_odd, live, k_rows, v_rows, k_cols, dk_sum, dv_sum = refs
    scale = HEAD_DIM**-0.5
    odd = place[1]
    step_of = (0, 2, 1 + 2 * odd, 3 - 2 * odd)
    block = tiles * TILE
    chunk = 2 * TILE
    chunks = WIN * block // chunk

    def clear(i, _):
        live[i] = 0
        return _

    lax.fori_loop(0, WIN * tiles * tiles, clear, 0)
    for b in range(WIN):
        step = step_of[b]

        def mark(slot, _, b=b, step=step):
            at = (step * slots + slot) * 2
            q_at, k_at = pairs[at], pairs[at + 1]
            if split:
                q_at, k_at = (q_at + place[0]) % 2, (k_at + place[0]) % 2
            live[(b * tiles + k_at) * tiles + q_at] = 1
            return _

        lax.fori_loop(0, counts[step], mark, 0)

    for b, ref in enumerate((None, kv_two, kv_core, kv_odd)):
        for t in range(tiles):
            at = pl.ds(b * block + t * TILE, TILE)
            if b == 0 and split:
                k, v = (k_mine[...], v_mine[...]) if t == 0 else (kv_far[0], kv_far[1])
            else:
                source = kv_own if b == 0 else ref
                k, v = source[t, 0], source[t, 1]
            k_rows[at, :] = k
            v_rows[at, :] = v
            k_cols[:, at] = k.T
    below = lax.broadcasted_iota(jnp.int32, (TILE, 2 * TILE), 0)
    across = lax.broadcasted_iota(jnp.int32, (TILE, 2 * TILE), 1) % TILE
    causal = below <= across

    for t in range(tiles):
        for pair in range(group // 2):
            first = t == 0 and pair == 0
            cut = pl.ds(pair * 2 * HEAD_DIM, HEAD_DIM), pl.ds((pair * 2 + 1) * HEAD_DIM, HEAD_DIM)
            q_two = jnp.concatenate([q_tile(t)[:, cut[0]], q_tile(t)[:, cut[1]]], axis=0)
            g_two = jnp.concatenate([g_tile(t)[:, cut[0]], g_tile(t)[:, cut[1]]], axis=0)
            norm = [rows_ref[t, 0, 0, pl.ds(pair * 2 + i, 1), :] for i in range(2)]
            delta = [rows_ref[t, 1, 0, pl.ds(pair * 2 + i, 1), :] for i in range(2)]
            norm = jnp.concatenate(norm, axis=1) * LOG2E
            delta = jnp.concatenate(delta, axis=1)

            def one_chunk(n, dq, t=t, first=first, q_two=q_two, g_two=g_two, norm=norm, delta=delta):
                at = pl.ds(n * chunk if isinstance(n, int) else pl.multiple_of(n * chunk, chunk), chunk)
                scores = dot(k_rows[at, :], q_two, NT) * (scale * LOG2E)
                prob_grad = dot(v_rows[at, :], g_two, NT)
                probs, grads = [], []
                for half in range(2):
                    k_at = n * 2 + half
                    part = slice(half * TILE, (half + 1) * TILE)
                    shift = jnp.where(live[k_at * tiles + t] > 0, norm, FAR)
                    power = scores[part] - shift
                    if not isinstance(n, int):
                        power = jnp.where(causal | (k_at != t), power, -FAR)
                    elif k_at == t:
                        power = jnp.where(causal, power, -FAR)
                    prob = jnp.exp2(power)
                    probs.append(prob.astype(jnp.bfloat16))
                    grads.append((prob * (prob_grad[part] - delta)).astype(jnp.bfloat16))
                probs = jnp.concatenate(probs, axis=0)
                grads = jnp.concatenate(grads, axis=0)
                dv = dot(probs, g_two, NN)
                dk = dot(grads, q_two, NN)
                if first:
                    dv_sum[at, :] = dv
                    dk_sum[at, :] = dk
                else:
                    dv_sum[at, :] += dv
                    dk_sum[at, :] += dk
                return dq + dot(k_cols[:, at], grads, NN)

            dq = jnp.zeros((HEAD_DIM, 2 * TILE), jnp.float32)
            if chunks <= 4:
                for n in range(chunks):
                    dq = one_chunk(n, dq)
            else:
                dq = lax.fori_loop(0, chunks, one_chunk, dq)
            dq = ((dq * scale).T).astype(jnp.bfloat16)
            out = dq_refs[t] if split else dq_refs[0].at[t]
            out[:, cut[0]] = dq[:TILE]
            out[:, cut[1]] = dq[TILE:]

    for b, ref in enumerate((d_own, d_two, d_core, d_odd)):
        for t in range(tiles):
            at = pl.ds(b * block + t * TILE, TILE)
            ref[t, 0] = (dk_sum[at, :] * scale).astype(ref.dtype)
            ref[t, 1] = dv_sum[at, :].astype(ref.dtype)


def per_device(queries, keys, values, out_grad, log_norm, row_delta, tile_pairs, pair_count):
    heads = lax.axis_size("head")
    mine = lax.axis_index("head")
    odd = lax.axis_index("ctx") % 2
    rows = queries.shape[0]
    width = queries.shape[1] // heads
    kv_width = keys.shape[1] // heads
    local_kv = kv_width // HEAD_DIM
    group = width // kv_width
    tiles = heads * rows // TILE
    slots = tile_pairs.shape[2]
    split = heads == 2 and rows == TILE
    small = jnp.stack([log_norm.T, row_delta.T])
    small = small.reshape(2, heads, local_kv, group, rows)

    if split:
        def other(x):
            return lax.dynamic_slice_in_dim(x, (1 - mine) * (x.shape[1] // 2), x.shape[1] // 2, 1)

        kv_mine = jnp.stack(
            [
                lax.dynamic_slice_in_dim(x, mine * kv_width, kv_width, 1)
                for x in (keys, values)
            ]
        )
        kv_far = swap(jnp.stack([other(keys), other(values)]), "head")
        kv_own = jnp.stack([kv_mine, kv_far])
        qg_far = swap(jnp.stack([other(queries), other(out_grad)]), "head")
        small_mine = lax.dynamic_index_in_dim(small, mine, 1, keepdims=False)
        small_far = swap(lax.dynamic_index_in_dim(small, 1 - mine, 1, keepdims=False), "head")
        small_all = jnp.stack([small_mine, small_far])
    else:
        def spread(x, split_at):
            got = lax.all_to_all(x, "head", split_axis=split_at, concat_axis=0)
            return got

        kv = jnp.stack([keys, values]).reshape(2, rows, heads, kv_width)
        kv_own = spread(kv, 2)
        q_all = spread(queries.reshape(rows, heads, width), 1)
        g_all = spread(out_grad.reshape(rows, heads, width), 1)
        small_all = spread(small, 1)
        per = rows // TILE
        kv_own = jnp.swapaxes(kv_own.reshape(heads, 2, per, TILE, kv_width), 1, 2)
        kv_own = kv_own.reshape(tiles, 2, TILE, kv_width)
        q_all = q_all.reshape(tiles, TILE, width)
        g_all = g_all.reshape(tiles, TILE, width)
        small_all = small_all.reshape(heads, 2, local_kv, group, per, TILE)
        small_all = jnp.moveaxis(small_all, 4, 1).reshape(tiles, 2, local_kv, group, TILE)

    kv_two = routed(kv_own, two_on)
    kv_odd = routed(kv_own, one_or_three_on)
    kv_core = swap(kv_two, "ctx")

    place = jnp.stack([mine, odd]).astype(jnp.int32)
    kv_spec = pl.BlockSpec((tiles, 2, TILE, HEAD_DIM), lambda h, *_: (0, 0, 0, h))
    wide = group * HEAD_DIM
    if split:
        head_args = (queries, qg_far, out_grad, qg_far, keys, values, kv_far)
        q_own = pl.BlockSpec((rows, wide), lambda h, place, *_: (0, place[0] * local_kv + h))
        k_own = pl.BlockSpec((rows, HEAD_DIM), lambda h, place, *_: (0, place[0] * local_kv + h))
        head_specs = [
            q_own,
            pl.BlockSpec((None, rows, wide), lambda h, *_: (0, 0, h)),
            q_own,
            pl.BlockSpec((None, rows, wide), lambda h, *_: (1, 0, h)),
            k_own,
            k_own,
            pl.BlockSpec((2, rows, HEAD_DIM), lambda h, *_: (0, 0, h)),
        ]
        dq_shapes = [jax.ShapeDtypeStruct((rows, width), jnp.bfloat16)] * 2
        dq_specs = [pl.BlockSpec((rows, wide), lambda h, *_: (0, h))] * 2
    else:
        head_args = (q_all, g_all, kv_own)
        all_spec = pl.BlockSpec((tiles, TILE, wide), lambda h, *_: (0, 0, h))
        head_specs = [all_spec, all_spec, kv_spec]
        dq_shapes = [jax.ShapeDtypeStruct((tiles, TILE, width), jnp.bfloat16)]
        dq_specs = [all_spec]
    small_spec = pl.BlockSpec((tiles, 2, 1, group, TILE), lambda h, *_: (0, 0, h, 0, 0))
    d_shape = (tiles, 2, TILE, kv_width)
    keys_all = WIN * tiles * TILE
    results = pl.pallas_call(
        functools.partial(kernel, tiles, group, slots, split),
        out_shape=dq_shapes
        + [jax.ShapeDtypeStruct(d_shape, t) for t in (jnp.float32, jnp.float32, jnp.bfloat16, jnp.bfloat16)],
        grid_spec=pltpu.PrefetchScalarGridSpec(
            num_scalar_prefetch=3,
            grid=(local_kv,),
            in_specs=head_specs + [small_spec, kv_spec, kv_spec, kv_spec],
            out_specs=dq_specs + [kv_spec] * 4,
            scratch_shapes=[
                pltpu.SMEM((WIN * tiles * tiles,), jnp.int32),
                pltpu.VMEM((keys_all, HEAD_DIM), jnp.bfloat16),
                pltpu.VMEM((keys_all, HEAD_DIM), jnp.bfloat16),
                pltpu.VMEM((HEAD_DIM, keys_all), jnp.bfloat16),
                pltpu.VMEM((keys_all, HEAD_DIM), jnp.float32),
                pltpu.VMEM((keys_all, HEAD_DIM), jnp.float32),
            ],
        ),
        compiler_params=pltpu.CompilerParams(vmem_limit_bytes=48 * 1024 * 1024),
        name="attention_grads",
    )(
        place,
        tile_pairs.reshape(-1),
        pair_count.reshape(-1),
        *head_args,
        small_all,
        kv_two,
        kv_core,
        kv_odd,
    )
    d_own, d_two, d_core, d_odd = results[-4:]
    from_odd = routed(d_odd, one_or_three_on, backwards=True)
    d_two = d_two + swap(d_core, "ctx").astype(jnp.float32)
    from_two = routed(d_two.astype(jnp.bfloat16), two_on, backwards=True)
    d_all = (d_own + from_odd.astype(jnp.float32) + from_two.astype(jnp.float32)).astype(jnp.bfloat16)

    if split:
        dq_mine, dq_other = results[:2]
        dq_far = swap(dq_other, "head")
        d_far = swap(d_all[1], "head")

        def whole(near, far):
            return jnp.where(
                mine == 0, jnp.concatenate([near, far], -1), jnp.concatenate([far, near], -1)
            )

        d_both = whole(d_all[0], d_far)
        return whole(dq_mine, dq_far), d_both[0], d_both[1]
    dq = results[0].reshape(heads, rows, width)
    dq = lax.all_to_all(dq, "head", split_axis=0, concat_axis=1).reshape(queries.shape)
    d_all = jnp.swapaxes(d_all.reshape(heads, rows // TILE, 2, TILE, kv_width), 1, 2)
    d_all = d_all.reshape(heads, 2, rows, kv_width)
    d_all = lax.all_to_all(d_all, "head", split_axis=0, concat_axis=2).reshape(2, *keys.shape)
    return dq, d_all[0], d_all[1]


def solution(mesh):
    rows = P(("ctx", "head"), None)
    return jax.shard_map(
        per_device,
        mesh=mesh,
        in_specs=(rows,) * 6 + (P("ctx", None, None, None), P("ctx", None)),
        out_specs=(rows,) * 3,
        check_vma=False,
    )
```

time: 265 us -> 85.5 us (0.32)
  matrix products: 74.7 us -> 0 us
  local copies, waits for them, and re-layouts: 47.8 us -> 4.4 us
  starting transfers between devices: 52.1 us -> 16.2 us
  loops' own time: 31.8 us -> 0 us
  Pallas kernels: 0 us -> 19.6 us
  blocking collectives: 8.23 us -> 0 us
  other arithmetic: 12 us -> 5.03 us
  waiting for transfers between devices: 34.5 us -> 37.8 us
    dot_general x80 -> x0, matrix products: 74.7 us -> none  [the longest x16 40.7 us: tile_terms(): jnp.einsum('kgij,jkd->ikgd', score_grad, key_tile, preferred_element_type...]
    ppermute x14 -> x11, waiting for transfers between devices: 0.04 us -> 37.8 us  [the longest x4 21.4 us: routed(): return lax.ppermute(value, 'ctx', pairs)]
    all_to_all x8 -> x0, waiting for transfers between devices: 34.5 us -> none  [the longest x1 9.36 us: per_device(): lax.all_to_all(query_grad, 'head', split_axis=0, concat_axis=1, tiled=True)]
    another operation x4 -> x0, loops' own time: 31.8 us -> none  [per_device(): lax.fori_loop(0, list_len, slot_body, step_start)]
    all_to_all x8 -> x0, starting transfers between devices: 27.8 us -> none  [the longest x1 3.58 us: per_device(): lax.all_to_all(queries, 'head', split_axis=1, concat_axis=0, tiled=True)]
    pallas_call x0 -> x1, Pallas kernels: none -> 19.6 us  [per_device(): pl.pallas_call(functools.partial(kernel, tiles, group, slots, split), out...]
    dynamic_slice x20 -> x0, local copies, waits for them, and re-layouts: 14.1 us -> none  [the longest x16 9.88 us: slot_body(): k_start = pair_list[slot, 1] * TILE]
    ppermute x6 -> x0, local copies, waits for them, and re-layouts: 9.32 us -> none  [shifted(): return lax.ppermute(block, axis, route)]
  transfers between devices with their start and end apart: 22 -> 11, of which waited for: 7 -> 6; matrix products, arithmetic and copies ran while one was open for 51% -> 7% of each run, Pallas kernels for 0% -> 0%
where the time goes in v1:
time: 85.5 us; the launch traced here: 83.9 us
  waiting for transfers between devices  37.8 us (44%)
  Pallas kernels  19.6 us (23%)
  starting transfers between devices  16.2 us (19%)
  other arithmetic  5.03 us (6%)
  local copies, waits for them, and re-layouts  4.4 us (5%)
    ppermute x4, waiting for transfers between devices, routed(): return lax.ppermute(value, 'ctx', pairs)  21.4 us
    pallas_call x1, Pallas kernels, per_device(): pl.pallas_call(functools.partial(kernel, tiles, group, slots, split), out...  19.6 us
    ppermute x7, waiting for transfers between devices, swap(): lax.ppermute(value, axis, [(i, i ^ 1) for i in range(lax.axis_size(axis))])  16.4 us
    ppermute x7, starting transfers between devices, swap(): lax.ppermute(value, axis, [(i, i ^ 1) for i in range(lax.axis_size(axis))])  8.32 us
    ppermute x4, starting transfers between devices, routed(): return lax.ppermute(value, 'ctx', pairs)  7.86 us
  transfers between devices with their start and end apart: 11, of which 6 were waited for; matrix products, arithmetic and copies ran while one was open for 7% of the time, Pallas kernels for 0%

profile of v1, /device:TPU:0, one launch (start us, length us, event | category | flops | bytes accessed | tf_op | source)
XLA Modules:
  0.0 83.9 jit_solution(747797254766228553)
XLA Ops:
  0.6 1.2 %dynamic-slice_bitcast_fusion.2 = (bf16[1,128,512]{2,1,0:T(8,128)(2,1)S(1)}, bf16[1,128,512]{2,1,0:T(8,128)(2,1)S(1)}, bf16[1,128,512]{2,1,0:T(8,128)(2,1)S(1)}, bf16[1,128,512]{2,1,0:T(8,128)(2,1)S(1)}) fusion(bf16[128,1024]{1,0:T(8,128)(2,1)} %refs_8_.1, s32[]{:T(128)S(6)} %select_n.48, s32[]{:T(128)S(6)} %select_n.45, bf16[128,1024]{1,0:T(8,128)(2,1)} %refs_7_.1), kind=kLoop, calls=%fused_computation.14 | loop fusion | bytes 1048584 | tf_op jit(solution)/shard_map/stack | solution.py:178
  1.9 3.0 %collective-permute-start.1 = (bf16[2,128,512]{2,1,0:T(8,128)(2,1)S(1)}, bf16[2,128,512]{2,1,0:T(8,128)(2,1)S(1)}, u32[]{:S(2)}, u32[]{:S(2)}) collective-permute-start(bf16[2,128,512]{2,1,0:T(8,128)(2,1)S(1)} %pad_maximum_fusion.2), channel_id=1, source_target_pairs={{0,1},{1,0},{2,3},{3,2},{4,5},{5,4},{6,7},{7,6},{8,9},{9,8},{10,11... | collective-permute-start | bytes 786440 | tf_op jit(solution)/shard_map/ppermute | solution.py:24
  4.9 1.1 %dynamic-slice_bitcast_fusion = (bf16[1,128,2048]{2,1,0:T(8,128)(2,1)S(1)}, bf16[1,128,2048]{2,1,0:T(8,128)(2,1)S(1)}) fusion(bf16[128,4096]{1,0:T(8,128)(2,1)} %refs_5_.1, s32[]{:T(128)S(6)} %select_n.44, bf16[128,4096]{1,0:T(8,128)(2,1)S(1)} %copy-done.7), kind=kLoop, calls=%fused_computation.6 | loop fusion | bytes 2097156 | tf_op jit(solution)/shard_map/stack | solution.py:186
  6.1 1.1 %pad_maximum_fusion = bf16[2,128,2048]{2,1,0:T(8,128)(2,1)} fusion(bf16[1,128,2048]{2,1,0:T(8,128)(2,1)S(1)} %get-tuple-element.25, bf16[1,128,2048]{2,1,0:T(8,128)(2,1)S(1)} %get-tuple-element.26), kind=kLoop, calls=%fused_computation | loop fusion | flops 524288 | bytes 2097152 | tf_op jit(solution)/shard_map/stack | solution.py:186
  7.4 4.7 %collective-permute-done.1.refs_9_ = bf16[2,128,512]{2,1,0:T(8,128)(2,1)S(1)} collective-permute-done((bf16[2,128,512]{2,1,0:T(8,128)(2,1)S(1)}, bf16[2,128,512]{2,1,0:T(8,128)(2,1)S(1)}, u32[]{:S(2)}, u32[]{:S(2)}) %collective-permute-start.1) | collective-permute-done | bytes 262176 | tf_op jit(solution)/shard_map/ppermute | solution.py:24
  12.1 0.9 %pad_maximum_fusion.1 = bf16[2,2,128,512]{3,2,1,0:T(8,128)(2,1)} fusion(bf16[1,2,128,512]{3,2,1,0:T(8,128)(2,1)S(1)} %bitcast.41, bf16[1,2,128,512]{3,2,1,0:T(8,128)(2,1)S(1)} %maximum_bitcast_fusion), kind=kLoop, calls=%fused_computation.4 | loop fusion | flops 262144 | bytes 1048576 | tf_op jit(solution)/shard_map/stack | solution.py:185
  12.9 4.0 %collective-permute-start.3 = (bf16[2,2,128,512]{3,2,1,0:T(8,128)(2,1)}, bf16[2,2,128,512]{3,2,1,0:T(8,128)(2,1)S(1)}, u32[]{:S(2)}, u32[]{:S(2)}) collective-permute-start(bf16[2,2,128,512]{3,2,1,0:T(8,128)(2,1)} %pad_maximum_fusion.1), channel_id=1, source_target_pairs={{0,4},{2,6},{4,8},{6,10},{8,12},{10,14},{12,16},{14,18},{16,20},{1... | collective-permute-start | bytes 1572872 | tf_op jit(solution)/shard_map/ppermute | solution.py:32
  16.9 1.3 %collective-permute-start.5 = (bf16[2,2,128,512]{3,2,1,0:T(8,128)(2,1)}, bf16[2,2,128,512]{3,2,1,0:T(8,128)(2,1)S(1)}, u32[]{:S(2)}, u32[]{:S(2)}) collective-permute-start(bf16[2,2,128,512]{3,2,1,0:T(8,128)(2,1)} %pad_maximum_fusion.1), channel_id=1, source_target_pairs={{0,2},{2,8},{4,6},{6,12},{8,10},{10,16},{12,14},{14,20},{16,18},{1... | collective-permute-start | bytes 1572872 | tf_op jit(solution)/shard_map/ppermute | solution.py:32
  18.2 8.1 %collective-permute-done.3.refs_11_ = bf16[2,2,128,512]{3,2,1,0:T(8,128)(2,1)S(1)} collective-permute-done((bf16[2,2,128,512]{3,2,1,0:T(8,128)(2,1)}, bf16[2,2,128,512]{3,2,1,0:T(8,128)(2,1)S(1)}, u32[]{:S(2)}, u32[]{:S(2)}) %collective-permute-start.3) | collective-permute-done | bytes 524320 | tf_op jit(solution)/shard_map/ppermute | solution.py:32
  26.4 1.6 %collective-permute-start.2 = (f32[2,4,4,128]{3,2,1,0:T(4,128)S(1)}, f32[2,4,4,128]{3,2,1,0:T(4,128)S(1)}, u32[]{:S(2)}, u32[]{:S(2)}) collective-permute-start(f32[2,4,4,128]{3,2,1,0:T(4,128)S(1)} %get-tuple-element.24), channel_id=1, source_target_pairs={{0,1},{1,0},{2,3},{3,2},{4,5},{5,4},{6,7},{7,6},{8,9},{9,8},{10,11... | collective-permute-start | bytes 49160 | tf_op jit(solution)/shard_map/ppermute | solution.py:24
  28.2 5.8 %collective-permute-done.2 = f32[2,4,4,128]{3,2,1,0:T(4,128)S(1)} collective-permute-done((f32[2,4,4,128]{3,2,1,0:T(4,128)S(1)}, f32[2,4,4,128]{3,2,1,0:T(4,128)S(1)}, u32[]{:S(2)}, u32[]{:S(2)}) %collective-permute-start.2) | collective-permute-done | bytes 16416 | tf_op jit(solution)/shard_map/ppermute | solution.py:24
  34.1 0.9 %copy-done.6 = bf16[2,128,2048]{2,1,0:T(8,128)(2,1)} copy-done((bf16[2,128,2048]{2,1,0:T(8,128)(2,1)}, bf16[2,128,2048]{2,1,0:T(8,128)(2,1)S(1)}, u32[]{:S(2)}) %copy-start.6) | copy-done | bytes 1048600
  35.1 19.6 %attention_grads.1 = (bf16[128,2048]{1,0:T(8,128)(2,1)S(1)}, bf16[128,2048]{1,0:T(8,128)(2,1)S(1)}, f32[2,2,128,512]{3,2,1,0:T(8,128)S(1)}, f32[2,2,128,512]{3,2...) custom-call(s32[2]{0:T(128)S(1)} %pad_add_fusion.refs_0_, s32[32]{0:T(128)S(1)} %reshape.18.refs_1_, ...), custom_call_target="tpu_custom_call" | custom-call | tf_op jit(solution)/shard_map/attention_grads/pallas_call | solution.py:239
  54.8 1.3 %collective-permute-start.7 = (bf16[2,2,128,512]{3,2,1,0:T(8,128)(2,1)}, bf16[2,2,128,512]{3,2,1,0:T(8,128)(2,1)S(1)}, u32[]{:S(2)}, u32[]{:S(2)}) collective-permute-start(bf16[2,2,128,512]{3,2,1,0:T(8,128)(2,1)} %get-tuple-element.12), channel_id=1, source_target_pairs={{2,0},{8,2},{6,4},{12,6},{10,8},{16,10},{14,12},{20,14},{18,16},{2... | collective-permute-start | bytes 1572872 | tf_op jit(solution)/shard_map/ppermute | solution.py:32
  56.1 0.6 collective-permute-done.8
  56.7 1.4 %add_convert_fusion.1 = bf16[2,2,128,512]{3,2,1,0:T(8,128)(2,1)S(1)} fusion(f32[2,2,128,512]{3,2,1,0:T(8,128)} %get-tuple-element.13, bf16[2,2,128,512]{3,2,1,0:T(8,128)(2,1)S(1)} %collective-permute-done.8), kind=kLoop, calls=%fused_computation.3 | loop fusion | flops 786432 | bytes 2097152 | tf_op jit(solution)/shard_map/convert_element_type | solution.py:272
  58.1 1.3 %collective-permute-start.9 = (bf16[2,2,128,512]{3,2,1,0:T(8,128)(2,1)S(1)}, bf16[2,2,128,512]{3,2,1,0:T(8,128)(2,1)S(1)}, u32[]{:S(2)}, u32[]{:S(2)}) collective-permute-start(bf16[2,2,128,512]{3,2,1,0:T(8,128)(2,1)S(1)} %add_convert_fusion.1), channel_id=1, source_target_pairs={{4,0},{6,2},{8,4},{10,6},{12,8},{14,10},{16,12},{18,14},{20,16},{2... | collective-permute-start | bytes 1572872 | tf_op jit(solution)/shard_map/ppermute | solution.py:32
  59.4 1.8 %collective-permute-start.6 = (bf16[128,2048]{1,0:T(8,128)(2,1)}, bf16[128,2048]{1,0:T(8,128)(2,1)S(1)}, u32[]{:S(2)}, u32[]{:S(2)}) collective-permute-start(bf16[128,2048]{1,0:T(8,128)(2,1)} %copy-done.5), channel_id=1, source_target_pairs={{0,1},{1,0},{2,3},{3,2},{4,5},{5,4},{6,7},{7,6},{8,9},{9,8},{10,11... | collective-permute-start | bytes 1572872 | tf_op jit(solution)/shard_map/ppermute | solution.py:24
  61.2 13.3 %collective-permute-done.9 = bf16[2,2,128,512]{3,2,1,0:T(8,128)(2,1)S(1)} collective-permute-done((bf16[2,2,128,512]{3,2,1,0:T(8,128)(2,1)S(1)}, bf16[2,2,128,512]{3,2,1,0:T(8,128)(2,1)S(1)}, u32[]{:S(2)}, u32[]{:S(2)}) %collective-permute-start.9) | collective-permute-done | bytes 524320 | tf_op jit(solution)/shard_map/ppermute | solution.py:32
  74.5 0.2 add_convert_fusion
  74.8 1.6 %collective-permute-start.10 = (bf16[2,128,512]{2,1,0:T(8,128)(2,1)S(1)}, bf16[2,128,512]{2,1,0:T(8,128)(2,1)S(1)}, u32[]{:S(2)}, u32[]{:S(2)}) collective-permute-start(bf16[2,128,512]{2,1,0:T(8,128)(2,1)S(1)} %get-tuple-element.18), channel_id=1, source_target_pairs={{0,1},{1,0},{2,3},{3,2},{4,5},{5,4},{6,7},{7,6},{8,9},{9,8},{10,11... | collective-permute-start | bytes 786440 | tf_op jit(solution)/shard_map/ppermute | solution.py:24
  76.5 1.2 %maximum_select_fusion = bf16[128,4096]{1,0:T(8,128)(2,1)} fusion(bf16[128,2048]{1,0:T(8,128)(2,1)S(1)} %collective-permute-done.6, bf16[128,2048]{1,0:T(8,128)(2,1)S(1)} %copy-done.3, pred[]{:T(512)S(6)} %eq.6), kind=kLoop, calls=%fused_computation.1 | loop fusion | flops 4718592 | bytes 2097153 | tf_op jit(solution)/shard_map/jit(_where)/select_n | solution.py:281
  77.7 5.3 %collective-permute-done.10 = bf16[2,128,512]{2,1,0:T(8,128)(2,1)S(1)} collective-permute-done((bf16[2,128,512]{2,1,0:T(8,128)(2,1)S(1)}, bf16[2,128,512]{2,1,0:T(8,128)(2,1)S(1)}, u32[]{:S(2)}, u32[]{:S(2)}) %collective-permute-start.10) | collective-permute-done | bytes 262176 | tf_op jit(solution)/shard_map/ppermute | solution.py:24
  83.1 0.8 slice_bitcast_fusion
  (38 shorter events, 0.9 us)
Async XLA Ops:
  0.6 4.3 %copy-start.7 = (bf16[128,4096]{1,0:T(8,128)(2,1)S(1)}, bf16[128,4096]{1,0:T(8,128)(2,1)}, u32[]{:S(2)}) copy-start(bf16[128,4096]{1,0:T(8,128)(2,1)} %refs_3_.1) | copy-start | bytes 3145732
  1.9 10.2 %collective-permute-start.1 = (bf16[2,128,512]{2,1,0:T(8,128)(2,1)S(1)}, bf16[2,128,512]{2,1,0:T(8,128)(2,1)S(1)}, u32[]{:S(2)}, u32[]{:S(2)}) collective-permute-start(bf16[2,128,512]{2,1,0:T(8,128)(2,1)S(1)} %pad_maximum_fusion.2), channel_id=1, source_target_pairs={{0,1},{1,0},{2,3},{3,2},{4,5},{5,4},{6,7},{7,6},{8,9},{9,8},{10,11... | collective-permute-start | bytes 786440 | tf_op jit(solution)/shard_map/ppermute | solution.py:24
  7.1 19.2 %copy-start.8 = (f32[128,32]{0,1:T(8,128)S(1)}, f32[128,32]{0,1:T(8,128)}, u32[]{:S(2)}) copy-start(f32[128,32]{0,1:T(8,128)} %param.12) | copy-start | bytes 49156
  7.1 19.2 %copy-start.9 = (f32[128,32]{0,1:T(8,128)S(1)}, f32[128,32]{0,1:T(8,128)}, u32[]{:S(2)}) copy-start(f32[128,32]{0,1:T(8,128)} %param.13) | copy-start | bytes 49156
  7.1 20.9 %copy-start.10 = (s32[1,4,4,2]{2,3,1,0:T(2,128)S(1)}, s32[1,4,4,2]{2,3,1,0:T(2,128)}, u32[]{:S(2)}) copy-start(s32[1,4,4,2]{2,3,1,0:T(2,128)} %param.14) | copy-start | bytes 388
  7.1 27.9 %copy-start = (bf16[128,1024]{1,0:T(8,128)(2,1)S(1)}, bf16[128,1024]{1,0:T(8,128)(2,1)}, u32[]{:S(2)}) copy-start(bf16[128,1024]{1,0:T(8,128)(2,1)} %refs_7_.1) | copy-start | bytes 786436
  7.1 27.9 %copy-start.1 = (bf16[128,1024]{1,0:T(8,128)(2,1)S(1)}, bf16[128,1024]{1,0:T(8,128)(2,1)}, u32[]{:S(2)}) copy-start(bf16[128,1024]{1,0:T(8,128)(2,1)} %refs_8_.1) | copy-start | bytes 786436
  7.2 27.9 %copy-start.4 = (s32[1,4]{1,0:T(1,128)S(1)}, s32[1,4]{1,0:T(1,128)}, u32[]{:S(2)}) copy-start(s32[1,4]{1,0:T(1,128)} %param.15) | copy-start | bytes 52
  7.2 26.9 %collective-permute-start = (bf16[2,128,2048]{2,1,0:T(8,128)(2,1)}, bf16[2,128,2048]{2,1,0:T(8,128)(2,1)S(1)}, u32[]{:S(2)}, u32[]{:S(2)}) collective-permute-start(bf16[2,128,2048]{2,1,0:T(8,128)(2,1)} %pad_maximum_fusion), channel_id=1, source_target_pairs={{0,1},{1,0},{2,3},{3,2},{4,5},{5,4},{6,7},{7,6},{8,9},{9,8},{10,11... | collective-permute-start | bytes 3145736 | tf_op jit(solution)/shard_map/ppermute | solution.py:24
  12.9 13.4 %collective-permute-start.3 = (bf16[2,2,128,512]{3,2,1,0:T(8,128)(2,1)}, bf16[2,2,128,512]{3,2,1,0:T(8,128)(2,1)S(1)}, u32[]{:S(2)}, u32[]{:S(2)}) collective-permute-start(bf16[2,2,128,512]{3,2,1,0:T(8,128)(2,1)} %pad_maximum_fusion.1), channel_id=1, source_target_pairs={{0,4},{2,6},{4,8},{6,10},{8,12},{10,14},{12,16},{14,18},{16,20},{1... | collective-permute-start | bytes 1572872 | tf_op jit(solution)/shard_map/ppermute | solution.py:32
  16.9 17.2 %collective-permute-start.5 = (bf16[2,2,128,512]{3,2,1,0:T(8,128)(2,1)}, bf16[2,2,128,512]{3,2,1,0:T(8,128)(2,1)S(1)}, u32[]{:S(2)}, u32[]{:S(2)}) collective-permute-start(bf16[2,2,128,512]{3,2,1,0:T(8,128)(2,1)} %pad_maximum_fusion.1), channel_id=1, source_target_pairs={{0,2},{2,8},{4,6},{6,12},{8,10},{10,16},{12,14},{14,20},{16,18},{1... | collective-permute-start | bytes 1572872 | tf_op jit(solution)/shard_map/ppermute | solution.py:32
  26.3 7.8 %collective-permute-start.4 = (bf16[2,2,128,512]{3,2,1,0:T(8,128)(2,1)S(1)}, bf16[2,2,128,512]{3,2,1,0:T(8,128)(2,1)S(1)}, u32[]{:S(2)}, u32[]{:S(2)}) collective-permute-start(bf16[2,2,128,512]{3,2,1,0:T(8,128)(2,1)S(1)} %collective-permute-done.3.refs_11_), channel_id=1, source_target_pairs={{0,2},{2,0},{4,6},{6,4},{8,10},{10,8},{12,14},{14,12},{16,18},{18,... | collective-permute-start | bytes 1572872 | tf_op jit(solution)/shard_map/ppermute | solution.py:24
  26.4 7.7 %collective-permute-start.2 = (f32[2,4,4,128]{3,2,1,0:T(4,128)S(1)}, f32[2,4,4,128]{3,2,1,0:T(4,128)S(1)}, u32[]{:S(2)}, u32[]{:S(2)}) collective-permute-start(f32[2,4,4,128]{3,2,1,0:T(4,128)S(1)} %get-tuple-element.24), channel_id=1, source_target_pairs={{0,1},{1,0},{2,3},{3,2},{4,5},{5,4},{6,7},{7,6},{8,9},{9,8},{10,11... | collective-permute-start | bytes 49160 | tf_op jit(solution)/shard_map/ppermute | solution.py:24
  34.1 1.0 %copy-start.6 = (bf16[2,128,2048]{2,1,0:T(8,128)(2,1)}, bf16[2,128,2048]{2,1,0:T(8,128)(2,1)S(1)}, u32[]{:S(2)}) copy-start(bf16[2,128,2048]{2,1,0:T(8,128)(2,1)S(1)} %collective-permute-done.refs_4_.refs_6_) | copy-start | bytes 3145732
  54.7 3.4 %copy-start.2 = (bf16[128,2048]{1,0:T(8,128)(2,1)}, bf16[128,2048]{1,0:T(8,128)(2,1)S(1)}, u32[]{:S(2)}) copy-start(bf16[128,2048]{1,0:T(8,128)(2,1)S(1)} %get-tuple-element.9) | copy-start | bytes 1572868
  54.7 3.4 %copy-start.5 = (bf16[128,2048]{1,0:T(8,128)(2,1)}, bf16[128,2048]{1,0:T(8,128)(2,1)S(1)}, u32[]{:S(2)}) copy-start(bf16[128,2048]{1,0:T(8,128)(2,1)S(1)} %get-tuple-element.10) | copy-start | bytes 1572868
  54.7 2.0 %collective-permute-start.8 = (bf16[2,2,128,512]{3,2,1,0:T(8,128)(2,1)S(1)}, bf16[2,2,128,512]{3,2,1,0:T(8,128)(2,1)S(1)}, u32[]{:S(2)}, u32[]{:S(2)}) collective-permute-start(bf16[2,2,128,512]{3,2,1,0:T(8,128)(2,1)S(1)} %get-tuple-element.14), channel_id=1, source_target_pairs={{0,2},{2,0},{4,6},{6,4},{8,10},{10,8},{12,14},{14,12},{16,18},{18,... | collective-permute-start | bytes 1572872 | tf_op jit(solution)/shard_map/ppermute | solution.py:24
  54.8 6.4 %collective-permute-start.7 = (bf16[2,2,128,512]{3,2,1,0:T(8,128)(2,1)}, bf16[2,2,128,512]{3,2,1,0:T(8,128)(2,1)S(1)}, u32[]{:S(2)}, u32[]{:S(2)}) collective-permute-start(bf16[2,2,128,512]{3,2,1,0:T(8,128)(2,1)} %get-tuple-element.12), channel_id=1, source_target_pairs={{2,0},{8,2},{6,4},{12,6},{10,8},{16,10},{14,12},{20,14},{18,16},{2... | collective-permute-start | bytes 1572872 | tf_op jit(solution)/shard_map/ppermute | solution.py:32
  58.1 16.4 %collective-permute-start.9 = (bf16[2,2,128,512]{3,2,1,0:T(8,128)(2,1)S(1)}, bf16[2,2,128,512]{3,2,1,0:T(8,128)(2,1)S(1)}, u32[]{:S(2)}, u32[]{:S(2)}) collective-permute-start(bf16[2,2,128,512]{3,2,1,0:T(8,128)(2,1)S(1)} %add_convert_fusion.1), channel_id=1, source_target_pairs={{4,0},{6,2},{8,4},{10,6},{12,8},{14,10},{16,12},{18,14},{20,16},{2... | collective-permute-start | bytes 1572872 | tf_op jit(solution)/shard_map/ppermute | solution.py:32
  59.4 17.0 %collective-permute-start.6 = (bf16[128,2048]{1,0:T(8,128)(2,1)}, bf16[128,2048]{1,0:T(8,128)(2,1)S(1)}, u32[]{:S(2)}, u32[]{:S(2)}) collective-permute-start(bf16[128,2048]{1,0:T(8,128)(2,1)} %copy-done.5), channel_id=1, source_target_pairs={{0,1},{1,0},{2,3},{3,2},{4,5},{5,4},{6,7},{7,6},{8,9},{9,8},{10,11... | collective-permute-start | bytes 1572872 | tf_op jit(solution)/shard_map/ppermute | solution.py:24
  74.8 1.7 %copy-start.3 = (bf16[128,2048]{1,0:T(8,128)(2,1)S(1)}, bf16[128,2048]{1,0:T(8,128)(2,1)}, u32[]{:S(2)}) copy-start(bf16[128,2048]{1,0:T(8,128)(2,1)} %copy-done.2) | copy-start | bytes 1572868
  74.8 8.1 %collective-permute-start.10 = (bf16[2,128,512]{2,1,0:T(8,128)(2,1)S(1)}, bf16[2,128,512]{2,1,0:T(8,128)(2,1)S(1)}, u32[]{:S(2)}, u32[]{:S(2)}) collective-permute-start(bf16[2,128,512]{2,1,0:T(8,128)(2,1)S(1)} %get-tuple-element.18), channel_id=1, source_target_pairs={{0,1},{1,0},{2,3},{3,2},{4,5},{5,4},{6,7},{7,6},{8,9},{9,8},{10,11... | collective-permute-start | bytes 786440 | tf_op jit(solution)/shard_map/ppermute | solution.py:24

commit v2 on v1

v2 whole, which is shorter than its diff:
```python
import functools

import jax
import jax.numpy as jnp
from jax import lax
from jax.experimental import pallas as pl
from jax.experimental.pallas import tpu as pltpu
from jax.sharding import PartitionSpec as P

HEAD_DIM = 128
TILE = 128
WIN = 4
LOG2E = 1.4426950408889634
FAR = 1e30
PARTS = 2
TOUCH_COST = 6000000000
VMEM_LIMIT = 60 * 1024 * 1024
FIRST_COST, SECOND_COST, DQ_COST, PACK_COST = 1000, 1000, 15000000000, 1000
NT = (((1,), (1,)), ((), ()))
NN = (((1,), (0,)), ((), ()))


def dot(a, b, dims):
    return lax.dot_general(a, b, dims, preferred_element_type=jnp.float32)


def swap(value, axis):
    return lax.ppermute(value, axis, [(i, i ^ 1) for i in range(lax.axis_size(axis))])


def routed(value, route, backwards=False):
    count = lax.axis_size("ctx")
    pairs = [(c, route(c)) for c in range(count) if route(c) < count]
    if backwards:
        pairs = [(b, a) for a, b in pairs]
    return lax.ppermute(value, "ctx", pairs)


def two_on(c):
    return c + 2


def one_or_three_on(c):
    return c + 1 if c % 2 == 0 else c + 3


def mark_live(tiles, slots, turn, steps, pairs, counts, live):
    def clear(i, _):
        live[i] = 0
        return _

    lax.fori_loop(0, WIN * tiles * tiles, clear, 0)
    for b, step in steps:

        def mark(slot, _, b=b, step=step):
            q_at, k_at = pairs[0, step, 0, slot], pairs[0, step, 1, slot]
            if tiles == 2:
                q_at, k_at = (q_at + turn) % 2, (k_at + turn) % 2
            live[(b * tiles + k_at) * tiles + q_at] = 1
            return _

        lax.fori_loop(0, counts[0, step], mark, 0)


def block_kernel(tiles, group, slots, *refs):
    pairs, counts, q_all, g_all, rows_ref, kv_own, kv_two, kv_core, kv_odd = refs[:9]
    dq_ref, d_own, d_two, d_core, d_odd, live, k_rows, v_rows, k_cols, dk_sum, dv_sum = refs[9:]
    scale = HEAD_DIM**-0.5
    odd = lax.axis_index("ctx") % 2
    block = tiles * TILE
    chunk = 2 * TILE
    steps = enumerate((0, 2, 1 + 2 * odd, 3 - 2 * odd))
    mark_live(tiles, slots, 0, steps, pairs, counts, live)
    for b, ref in enumerate((kv_own, kv_two, kv_core, kv_odd)):
        for t in range(tiles):
            at = pl.ds(b * block + t * TILE, TILE)
            k_rows[at, :] = ref[t, 0]
            v_rows[at, :] = ref[t, 1]
            k_cols[:, at] = ref[t, 0].T
    below = lax.broadcasted_iota(jnp.int32, (TILE, 2 * TILE), 0)
    across = lax.broadcasted_iota(jnp.int32, (TILE, 2 * TILE), 1) % TILE
    causal = below <= across

    for t in range(tiles):
        for pair in range(group // 2):
            first = t == 0 and pair == 0
            cut = pl.ds(pair * 2 * HEAD_DIM, HEAD_DIM), pl.ds((pair * 2 + 1) * HEAD_DIM, HEAD_DIM)
            q_two = jnp.concatenate([q_all[t, :, cut[0]], q_all[t, :, cut[1]]], axis=0)
            g_two = jnp.concatenate([g_all[t, :, cut[0]], g_all[t, :, cut[1]]], axis=0)
            norm = [rows_ref[t, 0, 0, pl.ds(pair * 2 + i, 1), :] for i in range(2)]
            delta = [rows_ref[t, 1, 0, pl.ds(pair * 2 + i, 1), :] for i in range(2)]
            norm = jnp.concatenate(norm, axis=1) * LOG2E
            delta = jnp.concatenate(delta, axis=1)

            def one_chunk(n, dq, t=t, first=first, q_two=q_two, g_two=g_two, norm=norm, delta=delta):
                at = pl.ds(pl.multiple_of(n * chunk, chunk), chunk)
                scores = dot(k_rows[at, :], q_two, NT) * (scale * LOG2E)
                prob_grad = dot(v_rows[at, :], g_two, NT)
                probs, grads = [], []
                for half in range(2):
                    k_at = n * 2 + half
                    part = slice(half * TILE, (half + 1) * TILE)
                    shift = jnp.where(live[k_at * tiles + t] > 0, norm, FAR)
                    power = jnp.where(causal | (k_at != t), scores[part] - shift, -FAR)
                    prob = jnp.exp2(power)
                    probs.append(prob.astype(jnp.bfloat16))
                    grads.append((prob * (prob_grad[part] - delta)).astype(jnp.bfloat16))
                probs = jnp.concatenate(probs, axis=0)
                grads = jnp.concatenate(grads, axis=0)
                dv = dot(probs, g_two, NN)
                dk = dot(grads, q_two, NN)
                if first:
                    dv_sum[at, :] = dv
                    dk_sum[at, :] = dk
                else:
                    dv_sum[at, :] += dv
                    dk_sum[at, :] += dk
                return dq + dot(k_cols[:, at], grads, NN)

            dq = jnp.zeros((HEAD_DIM, 2 * TILE), jnp.float32)
            dq = lax.fori_loop(0, WIN * block // chunk, one_chunk, dq)
            dq = ((dq * scale).T).astype(jnp.bfloat16)
            dq_ref[t, :, cut[0]] = dq[:TILE]
            dq_ref[t, :, cut[1]] = dq[TILE:]

    for b, ref in enumerate((d_own, d_two, d_core, d_odd)):
        for t in range(tiles):
            at = pl.ds(b * block + t * TILE, TILE)
            ref[t, 0] = (dk_sum[at, :] * scale).astype(ref.dtype)
            ref[t, 1] = dv_sum[at, :].astype(ref.dtype)


def pair_kernel(group, slots, blocks, n_unused, *refs):
    refs = list(refs)
    mine, pairs, counts, q_mine, q_far, g_mine, g_far, rows_mine, rows_far = refs[:9]
    del refs[:9]
    sources = {}
    for b in blocks:
        sources[b] = tuple(refs[: 3 if b == 0 else 2])
        del refs[: len(sources[b])]
    del refs[:n_unused]
    dq_outs = (refs.pop(0), refs.pop(0))
    outs = {b: (refs.pop(0), refs.pop(0)) for b in blocks}
    live, k_cols, prob_all, grad_all = refs[-4:]
    scale = HEAD_DIM**-0.5
    odd = lax.axis_index("ctx") % 2
    block = 2 * TILE
    units = [(t, pair) for t in range(2) for pair in range(group // 2)]
    step_of = (0, 2, 1 + 2 * odd, 3 - 2 * odd)
    mark_live(2, slots, mine[0], [(b, step_of[b]) for b in blocks], pairs, counts, live)

    below = lax.broadcasted_iota(jnp.int32, (TILE, 2 * TILE), 0)
    across = lax.broadcasted_iota(jnp.int32, (TILE, 2 * TILE), 1) % TILE
    causal = below <= across
    sides = ((q_mine, g_mine), (q_far, g_far))

    def heads_of(ref):
        return [ref[:, i * HEAD_DIM : (i + 1) * HEAD_DIM] for i in range(group)]

    q_all = jnp.concatenate([x for q, g in sides for x in heads_of(q)], axis=0)
    g_all = jnp.concatenate([x for q, g in sides for x in heads_of(g)], axis=0)
    far = rows_far[...].astype(jnp.float32)
    far = far[:, 0:1] + far[:, 1:2] + far[:, 2:3]
    rows = []
    for t, pair in units:
        at = slice(pair * block, (pair + 1) * block)
        norm, delta = [(rows_mine[i, :, at], far[i, :, at])[t] for i in range(2)]
        rows.append((norm * LOG2E, delta))

    for n, b in enumerate(blocks):
        if b == 0:
            k_mine, v_mine, kv_far = sources[b]
            k = jnp.concatenate([k_mine[...], kv_far[0]], axis=0)
            v = jnp.concatenate([v_mine[...], kv_far[1]], axis=0)
        else:
            kv_near, kv_far = sources[b]
            k = jnp.concatenate([kv_near[0], kv_far[0]], axis=0)
            v = jnp.concatenate([kv_near[1], kv_far[1]], axis=0)
        at = slice(n * block, (n + 1) * block)
        k_cols[:, at] = k.T
        for u, (t, pair) in enumerate(units):
            cut = slice(u * block, (u + 1) * block)
            norm, delta = rows[u]
            scores = dot(k, q_all[cut], NT) * (scale * LOG2E)
            prob_grad = dot(v, g_all[cut], NT)
            for k_at in range(2):
                part = slice(k_at * TILE, (k_at + 1) * TILE)
                shift = jnp.where(live[(b * 2 + k_at) * 2 + t] > 0, norm, FAR)
                power = scores[part] - shift
                if b == 0 and k_at == t:
                    power = jnp.where(causal, power, -FAR)
                prob = jnp.exp2(power)
                to = slice(n * block + k_at * TILE, n * block + (k_at + 1) * TILE)
                prob_all[to, cut] = prob.astype(jnp.bfloat16)
                grad_all[to, cut] = (prob * (prob_grad[part] - delta)).astype(jnp.bfloat16)
        dv = dot(prob_all[at, :], g_all, NN)
        dk = dot(grad_all[at, :], q_all, NN) * scale
        for t, out in enumerate(outs[b]):
            part = slice(t * TILE, (t + 1) * TILE)
            out[0] = dk[part].astype(out.dtype)
            out[1] = dv[part].astype(out.dtype)

    for u, (t, pair) in enumerate(units):
        cut = slice(u * block, (u + 1) * block)
        dq = dot(k_cols[...], grad_all[:, cut], NN)
        dq = (dq * scale).T.astype(jnp.bfloat16)
        for i in range(2):
            head = pair * 2 + i
            dq_outs[t][:, head * HEAD_DIM : (head + 1) * HEAD_DIM] = dq[i * TILE : (i + 1) * TILE]


def by_blocks(queries, keys, values, out_grad, log_norm, row_delta, tile_pairs, pair_count):
    heads = lax.axis_size("head")
    rows = queries.shape[0]
    width = queries.shape[1] // heads
    kv_width = keys.shape[1] // heads
    local_kv = kv_width // HEAD_DIM
    group = width // kv_width
    tiles = heads * rows // TILE
    per = rows // TILE

    def spread(x, split_at):
        return lax.all_to_all(x, "head", split_axis=split_at, concat_axis=0)

    kv_own = spread(jnp.stack([keys, values]).reshape(2, rows, heads, kv_width), 2)
    kv_own = jnp.swapaxes(kv_own.reshape(heads, 2, per, TILE, kv_width), 1, 2)
    kv_own = kv_own.reshape(tiles, 2, TILE, kv_width)
    q_all = spread(queries.reshape(rows, heads, width), 1).reshape(tiles, TILE, width)
    g_all = spread(out_grad.reshape(rows, heads, width), 1).reshape(tiles, TILE, width)
    small = jnp.stack([log_norm.T, row_delta.T]).reshape(2, heads, local_kv, group, rows)
    small = spread(small, 1).reshape(heads, 2, local_kv, group, per, TILE)
    small = jnp.moveaxis(small, 4, 1).reshape(tiles, 2, local_kv, group, TILE)

    kv_two = routed(kv_own, two_on)
    kv_odd = routed(kv_own, one_or_three_on)
    kv_core = swap(kv_two, "ctx")

    kv_spec = pl.BlockSpec((tiles, 2, TILE, HEAD_DIM), lambda h, *_: (0, 0, 0, h))
    q_spec = pl.BlockSpec((tiles, TILE, group * HEAD_DIM), lambda h, *_: (0, 0, h))
    small_spec = pl.BlockSpec((tiles, 2, 1, group, TILE), lambda h, *_: (0, 0, h, 0, 0))
    keys_all = WIN * tiles * TILE
    kinds = (jnp.float32, jnp.float32, jnp.bfloat16, jnp.bfloat16)
    dq, d_own, d_two, d_core, d_odd = pl.pallas_call(
        functools.partial(block_kernel, tiles, group, tile_pairs.shape[2]),
        out_shape=[jax.ShapeDtypeStruct(q_all.shape, jnp.bfloat16)]
        + [jax.ShapeDtypeStruct(kv_own.shape, t) for t in kinds],
        grid_spec=pltpu.PrefetchScalarGridSpec(
            num_scalar_prefetch=2,
            grid=(local_kv,),
            in_specs=[q_spec, q_spec, small_spec] + [kv_spec] * 4,
            out_specs=[q_spec] + [kv_spec] * 4,
            scratch_shapes=[
                pltpu.SMEM((WIN * tiles * tiles,), jnp.int32),
                pltpu.VMEM((keys_all, HEAD_DIM), jnp.bfloat16),
                pltpu.VMEM((keys_all, HEAD_DIM), jnp.bfloat16),
                pltpu.VMEM((HEAD_DIM, keys_all), jnp.bfloat16),
                pltpu.VMEM((keys_all, HEAD_DIM), jnp.float32),
                pltpu.VMEM((keys_all, HEAD_DIM), jnp.float32),
            ],
        ),
        compiler_params=pltpu.CompilerParams(vmem_limit_bytes=48 * 1024 * 1024),
        name="block_grads",
    )(jnp.swapaxes(tile_pairs, 2, 3), pair_count, q_all, g_all, small, kv_own, kv_two, kv_core, kv_odd)
    d_all = home(d_own, d_two, d_core, d_odd)
    dq = lax.all_to_all(dq.reshape(heads, rows, width), "head", split_axis=0, concat_axis=1)
    d_all = jnp.swapaxes(d_all.reshape(heads, per, 2, TILE, kv_width), 1, 2)
    d_all = d_all.reshape(heads, 2, rows, kv_width)
    d_all = lax.all_to_all(d_all, "head", split_axis=0, concat_axis=2).reshape(2, *keys.shape)
    return dq.reshape(queries.shape), d_all[0], d_all[1]


def home(d_own, d_two, d_core, d_odd):
    from_odd = routed(d_odd, one_or_three_on, backwards=True)
    d_two = d_two + swap(d_core, "ctx").astype(jnp.float32)
    from_two = routed(d_two.astype(jnp.bfloat16), two_on, backwards=True)
    total = d_own + from_odd.astype(jnp.float32) + from_two.astype(jnp.float32)
    return total.astype(jnp.bfloat16)


def then(value, *before):
    return lax.optimization_barrier((value, *before))[0]


def pack_kernel(heads, mine, q_far, g_far, norm, delta, *outs):
    *parts, rows = outs
    size = parts[0].shape[2]
    tile = q_far.shape[0]
    for p, part in enumerate(parts):
        cut = slice(p * size, (p + 1) * size)
        part[0, :tile] = q_far[:, cut]
        part[1, :tile] = g_far[:, cut]
    for i, ref in enumerate((norm, delta)):
        both = ref[...]
        low_side = mine[0] == 0
        own = jnp.where(low_side, both[:heads], both[heads:])
        other = jnp.where(low_side, both[heads:], both[:heads])
        high = other.astype(jnp.bfloat16)
        rest = other - high.astype(jnp.float32)
        middle = rest.astype(jnp.bfloat16)
        low = (rest - middle.astype(jnp.float32)).astype(jnp.bfloat16)
        for h in range(heads):
            rows[i, :, h * tile : (h + 1) * tile] = own[h : h + 1]
        pad = jnp.zeros((13, tile), jnp.float32)
        per = size // tile
        for h in range(heads):
            three = [x[h : h + 1].astype(jnp.float32) for x in (high, middle, low)]
            block = jnp.concatenate(three + [pad], axis=0).astype(jnp.bfloat16)
            at = h % per
            parts[h // per][i, tile:, at * tile : (at + 1) * tile] = block


def fill_kernel(mine, got, before, half):
    half[...] = got[...]


def touch_kernel(x_ref, y_ref, mark):
    mark[0] = 1


def touch(x, cost):
    return pl.pallas_call(
        touch_kernel,
        out_shape=jax.ShapeDtypeStruct(x.shape, x.dtype),
        in_specs=[pl.BlockSpec(memory_space=pl.ANY)],
        out_specs=pl.BlockSpec(memory_space=pl.ANY),
        input_output_aliases={0: 0},
        scratch_shapes=[pltpu.SMEM((1,), jnp.int32)],
        cost_estimate=pl.CostEstimate(flops=cost, bytes_accessed=1, transcendentals=0),
        name="arrived",
    )(x)


def by_pairs(queries, keys, values, out_grad, log_norm, row_delta, tile_pairs, pair_count):
    mine = lax.axis_index("head")
    rows = queries.shape[0]
    width = queries.shape[1] // 2
    kv_width = keys.shape[1] // 2
    local_kv = kv_width // HEAD_DIM
    group = width // kv_width
    kvs = local_kv // PARTS
    wide = group * HEAD_DIM
    lists = (mine.reshape(1), jnp.swapaxes(tile_pairs, 2, 3), pair_count)

    def cut(x, side):
        size = x.shape[1] // 2
        return lax.dynamic_slice_in_dim(x, side * size, size, 1)

    kv_near = jnp.stack([cut(keys, mine), cut(values, mine)])
    kv_far = swap(jnp.stack([cut(keys, 1 - mine), cut(values, 1 - mine)]), "head")
    kv_far = touch(kv_far, TOUCH_COST)
    pack_spec = pl.BlockSpec((rows, width), lambda i, mine: (0, 1 - mine[0]))
    whole_spec = pl.BlockSpec((2 * local_kv * group, rows), lambda i, mine: (0, 0))
    packed = [(2, rows + 16, kvs * wide)] * PARTS
    *qg_send, small = pl.pallas_call(
        functools.partial(pack_kernel, local_kv * group),
        out_shape=[jax.ShapeDtypeStruct(s, jnp.bfloat16) for s in packed]
        + [jax.ShapeDtypeStruct((2, 1, width), jnp.float32)],
        grid_spec=pltpu.PrefetchScalarGridSpec(
            num_scalar_prefetch=1,
            grid=(1,),
            in_specs=[pack_spec, pack_spec, whole_spec, whole_spec],
            out_specs=[pl.BlockSpec(s, lambda i, mine: (0, 0, 0)) for s in packed + [(2, 1, width)]],
        ),
        compiler_params=pltpu.CompilerParams(vmem_limit_bytes=VMEM_LIMIT),
        cost_estimate=pl.CostEstimate(flops=PACK_COST, bytes_accessed=1, transcendentals=0),
        name="pack_sends",
    )(lists[0], queries, out_grad, log_norm.T, row_delta.T)
    qg_far = [swap(x, "head") for x in qg_send]
    near_two, near_odd = routed(kv_near, two_on), routed(kv_near, one_or_three_on)
    far_two, far_odd = routed(kv_far, two_on), routed(kv_far, one_or_three_on)
    near_core = swap(near_two, "ctx")

    def attend(part, blocks, sources, before, cost):
        first = part * kvs

        def at_mine(h, mine, *_):
            return (0, mine[0] * local_kv + first + h)

        q_own = pl.BlockSpec((rows, wide), at_mine)
        k_own = pl.BlockSpec((rows, HEAD_DIM), at_mine)
        far = lambda i: pl.BlockSpec((None, rows, wide), lambda h, *_: (i, 0, h))
        kv_spec = pl.BlockSpec((2, rows, HEAD_DIM), lambda h, *_: (0, 0, first + h))
        dq_spec = pl.BlockSpec((rows, wide), lambda h, *_: (0, h))
        carry_spec = pl.BlockSpec((None, HEAD_DIM, 2 * group * TILE), lambda h, *_: (h, 0, 0))
        args = [queries, qg_far[part], out_grad, qg_far[part], small, qg_far[part]]
        specs = [
            q_own,
            far(0),
            q_own,
            far(1),
            pl.BlockSpec((2, 1, wide), lambda h, *_: (0, 0, first + h)),
            pl.BlockSpec((2, 16, wide), lambda h, *_: (0, rows // 16, h)),
        ]
        for b in blocks:
            args += sources[b]
            specs += [k_own, k_own, kv_spec] if b == 0 else [kv_spec, kv_spec]
        dq_shapes = [queries.shape, (rows, width)]
        outs = [jax.ShapeDtypeStruct(s, jnp.bfloat16) for s in dq_shapes]
        out_specs = [q_own, pl.BlockSpec((rows, wide), lambda h, *_: (0, first + h))]
        kinds = (jnp.float32, jnp.float32, jnp.bfloat16, jnp.bfloat16)
        outs += [jax.ShapeDtypeStruct((2, rows, kv_width), kinds[b]) for b in blocks for _ in range(2)]
        out_specs += [kv_spec] * (2 * len(blocks))
        alias, n_args = {}, len(args)
        if before is not None:
            for i, array in enumerate(before):
                alias[len(lists) + len(args)] = i
                args.append(array)
        specs += [pl.BlockSpec(memory_space=pl.ANY)] * (len(args) - n_args)
        keys_all = len(blocks) * 2 * TILE
        return pl.pallas_call(
            functools.partial(
                pair_kernel,
                group,
                tile_pairs.shape[2],
                blocks,
                len(args) - n_args,
            ),
            out_shape=outs,
            grid_spec=pltpu.PrefetchScalarGridSpec(
                num_scalar_prefetch=3,
                grid=(kvs,),
                in_specs=specs,
                out_specs=out_specs,
                scratch_shapes=[
                    pltpu.SMEM((WIN * 4,), jnp.int32),
                    pltpu.VMEM((HEAD_DIM, keys_all), jnp.bfloat16),
                    pltpu.VMEM((keys_all, 2 * group * TILE), jnp.bfloat16),
                    pltpu.VMEM((keys_all, 2 * group * TILE), jnp.bfloat16),
                ],
            ),
            input_output_aliases=alias,
            compiler_params=pltpu.CompilerParams(vmem_limit_bytes=VMEM_LIMIT),
            cost_estimate=pl.CostEstimate(flops=cost, bytes_accessed=1, transcendentals=0),
            name="grads_" + "".join(map(str, blocks)) + "_part" + str(part),
        )(*lists, *args)

    sources = {
        0: (keys, values, kv_far),
        1: (near_two, far_two),
        2: (near_core, swap(far_two, "ctx")),
        3: (near_odd, far_odd),
    }
    done = None
    for part, cost in enumerate((FIRST_COST, SECOND_COST)):
        done = attend(part, (0, 1, 2, 3), sources, done, cost)
    dq_near, dq_far, *sums = done
    own_sums, sums = sums[:2], sums[2:]

    def wide_sum(*terms):
        return sum(x.astype(jnp.float32) for x in terms).astype(jnp.bfloat16)

    totals = []
    for t in (1, 0):
        two = wide_sum(sums[t], swap(sums[2 + t], "ctx"))
        two = routed(two, two_on, backwards=True)
        odd = routed(sums[4 + t], one_or_three_on, backwards=True)
        totals.append(wide_sum(own_sums[t], odd, two))
    far, near = totals

    def whole(near, far):
        return jnp.where(mine == 0, jnp.concatenate(near + far, -1), jnp.concatenate(far + near, -1))

    both = whole([near], [swap(far, "head")])
    half = pl.BlockSpec((rows, width), lambda i, mine: (0, 1 - mine[0]))
    dq = pl.pallas_call(
        fill_kernel,
        out_shape=jax.ShapeDtypeStruct(queries.shape, jnp.bfloat16),
        grid_spec=pltpu.PrefetchScalarGridSpec(
            num_scalar_prefetch=1,
            grid=(1,),
            in_specs=[
                pl.BlockSpec((rows, width), lambda i, mine: (0, 0)),
                pl.BlockSpec(memory_space=pl.ANY),
            ],
            out_specs=half,
        ),
        input_output_aliases={2: 0},
        cost_estimate=pl.CostEstimate(flops=DQ_COST, bytes_accessed=1, transcendentals=0),
        name="fill_in",
    )(lists[0], swap(dq_far, "head"), dq_near)
    return dq, both[0], both[1]


def per_device(queries, keys, values, out_grad, log_norm, row_delta, tile_pairs, pair_count):
    heads = lax.axis_size("head")
    local_kv = keys.shape[1] // heads // HEAD_DIM
    group = queries.shape[1] // keys.shape[1]
    paired = heads == 2 and queries.shape[0] == TILE and local_kv % PARTS == 0 and group % 2 == 0
    form = by_pairs if paired else by_blocks
    return form(queries, keys, values, out_grad, log_norm, row_delta, tile_pairs, pair_count)


def solution(mesh):
    rows = P(("ctx", "head"), None)
    return jax.shard_map(
        per_device,
        mesh=mesh,
        in_specs=(rows,) * 6 + (P("ctx", None, None, None), P("ctx", None)),
        out_specs=(rows,) * 3,
        check_vma=False,
    )
```

time: 85.5 us -> 74.7 us (0.87)
  waiting for transfers between devices: 37.8 us -> 17.6 us
  starting transfers between devices: 16.2 us -> 27.3 us
  other arithmetic: 5.03 us -> 1.67 us
  Pallas kernels: 19.6 us -> 21.2 us
    ppermute x4 -> x8, waiting for transfers between devices: 21.4 us -> 9.58 us  [routed(): return lax.ppermute(value, 'ctx', pairs)]
    ppermute x4 -> x8, starting transfers between devices: 7.86 us -> 16.8 us  [routed(): return lax.ppermute(value, 'ctx', pairs)]
    ppermute x7 -> x9, waiting for transfers between devices: 16.4 us -> 8.05 us  [swap(): lax.ppermute(value, axis, [(i, i ^ 1) for i in range(lax.axis_size(axis))])]
    ppermute x7 -> x9, starting transfers between devices: 8.32 us -> 10.4 us  [swap(): lax.ppermute(value, axis, [(i, i ^ 1) for i in range(lax.axis_size(axis))])]
    unnamed x23 -> x28, local copies, waits for them, and re-layouts: 1.11 us -> 3.2 us
    another operation x7 -> x2, other arithmetic: 2.07 us -> 0.05 us  [the longest x1 0.03 us: by_pairs(): jnp.stack([cut(keys, 1 - mine), cut(values, 1 - mine)])]
    pallas_call x1 -> x5, Pallas kernels: 19.6 us -> 21.2 us  [the longest x2 17 us: attend(): pl.pallas_call(functools.partial(pair_kernel, group, tile_pairs.shape[2],...]
    select_n x2 -> x1, other arithmetic: 1.35 us -> 0.14 us  [whole(): jnp.where(mine == 0, jnp.concatenate(near + far, -1), jnp.concatenate(far...]
  transfers between devices with their start and end apart: 11 -> 17, of which waited for: 6 -> 7; matrix products, arithmetic and copies ran while one was open for 7% -> 2% of each run, Pallas kernels for 0% -> 17%
where the time goes in v2:
time: 74.7 us; the launch traced here: 73.8 us
  starting transfers between devices  27.3 us (37%)
  Pallas kernels  21.2 us (28%)
  waiting for transfers between devices  17.6 us (24%)
  local copies, waits for them, and re-layouts  5.16 us (7%)
  other arithmetic  1.67 us (2%)
  between operations  0.9 us (1%)
    pallas_call x2, Pallas kernels, attend(): pl.pallas_call(functools.partial(pair_kernel, group, tile_pairs.shape[2],...  17 us
    ppermute x8, starting transfers between devices, routed(): return lax.ppermute(value, 'ctx', pairs)  16.8 us
    ppermute x9, starting transfers between devices, swap(): lax.ppermute(value, axis, [(i, i ^ 1) for i in range(lax.axis_size(axis))])  10.4 us
    ppermute x8, waiting for transfers between devices, routed(): return lax.ppermute(value, 'ctx', pairs)  9.58 us
    ppermute x9, waiting for transfers between devices, swap(): lax.ppermute(value, axis, [(i, i ^ 1) for i in range(lax.axis_size(axis))])  8.05 us
    unnamed x28, local copies, waits for them, and re-layouts  3.2 us
    pallas_call x1, Pallas kernels, by_pairs(): pl.pallas_call(functools.partial(pack_kernel, local_kv * group), out_shap...  2.3 us
    pallas_call x1, Pallas kernels, by_pairs(): pl.pallas_call(fill_kernel, out_shape=jax.ShapeDtypeStruct(queries.shape,...  1.93 us
  transfers between devices with their start and end apart: 17, of which 7 were waited for; matrix products, arithmetic and copies ran while one was open for 2% of the time, Pallas kernels for 17%

profile of v2, /device:TPU:0, one launch (start us, length us, event | category | flops | bytes accessed | tf_op | source)
XLA Modules:
  0.0 73.8 jit_solution(4844598792205146132)
XLA Ops:
  0.6 1.1 %dynamic-slice_bitcast_fusion = (bf16[1,128,512]{2,1,0:T(8,128)(2,1)S(1)}, bf16[1,128,512]{2,1,0:T(8,128)(2,1)S(1)}, bf16[1,128,512]{2,1,0:T(8,128)(2,1)S(1)}, bf16[1,128,512]{2,1,0:T(8,128)(2,1)S(1)}) fusion(bf16[128,1024]{1,0:T(8,128)(2,1)} %refs_10_.3, s32[]{:T(128)S(6)} %select_n.17, s32[]{:T(128)S(6)} %select_n.16, bf16[128,1024]{1,0:T(8,128)(2,1)} %refs_9_.3), kind=kLoop, calls=%fused_computation.9 | loop fusion | bytes 1048584 | tf_op jit(solution)/shard_map/stack | solution.py:348
  1.8 3.0 %collective-permute-start.1 = (bf16[2,128,512]{2,1,0:T(8,128)(2,1)S(1)}, bf16[2,128,512]{2,1,0:T(8,128)(2,1)S(1)}, u32[]{:S(2)}, u32[]{:S(2)}) collective-permute-start(bf16[2,128,512]{2,1,0:T(8,128)(2,1)S(1)} %pad_maximum_fusion), channel_id=1, source_target_pairs={{0,1},{1,0},{2,3},{3,2},{4,5},{5,4},{6,7},{7,6},{8,9},{9,8},{10,11... | collective-permute-start | bytes 786440 | tf_op jit(solution)/shard_map/ppermute | solution.py:28
  4.9 3.4 %collective-permute-start.2 = (bf16[2,128,512]{2,1,0:T(8,128)(2,1)S(1)}, bf16[2,128,512]{2,1,0:T(8,128)(2,1)S(1)}, u32[]{:S(2)}, u32[]{:S(2)}) collective-permute-start(bf16[2,128,512]{2,1,0:T(8,128)(2,1)S(1)} %pad_maximum_fusion.1), channel_id=1, source_target_pairs={{0,4},{2,6},{4,8},{6,10},{8,12},{10,14},{12,16},{14,18},{16,20},{1... | collective-permute-start | bytes 786440 | tf_op jit(solution)/shard_map/ppermute | solution.py:36
  8.3 1.3 %collective-permute-start.6 = (bf16[2,128,512]{2,1,0:T(8,128)(2,1)S(1)}, bf16[2,128,512]{2,1,0:T(8,128)(2,1)S(1)}, u32[]{:S(2)}, u32[]{:S(2)}) collective-permute-start(bf16[2,128,512]{2,1,0:T(8,128)(2,1)S(1)} %pad_maximum_fusion.1), channel_id=1, source_target_pairs={{0,2},{2,8},{4,6},{6,12},{8,10},{10,16},{12,14},{14,20},{16,18},{1... | collective-permute-start | bytes 786440 | tf_op jit(solution)/shard_map/ppermute | solution.py:36
  9.6 2.3 %pack_sends.1 = (bf16[2,144,1024]{2,1,0:T(8,128)(2,1)}, bf16[2,144,1024]{2,1,0:T(8,128)(2,1)}, f32[2,1,2048]{2,1,0:T(1,128)}) custom-call(s32[1]{0:T(128)} %bitcast.mine.refs_0_, bf16[128,4096]{1,0:T(8,128)(2,1)} %refs_3_.3, bf16[128,4096]{1,0:T(8,128)(2,1)} %refs_5_.3, f32[32,128]{1,0:T(8,128)} %bitcast.16, f32[32,128]{1,0:T(8,128)} %bitcast.17), custom_call_target="tpu_custom_call" | custom-call | flops 1000 | bytes 1 | tf_op jit(solution)/shard_map/pack_sends/pallas_call | solution.py:354
  12.4 1.5 %collective-permute-start = (bf16[2,144,1024]{2,1,0:T(8,128)(2,1)}, bf16[2,144,1024]{2,1,0:T(8,128)(2,1)S(1)}, u32[]{:S(2)}, u32[]{:S(2)}) collective-permute-start(bf16[2,144,1024]{2,1,0:T(8,128)(2,1)} %get-tuple-element.26), channel_id=1, source_target_pairs={{0,1},{1,0},{2,3},{3,2},{4,5},{5,4},{6,7},{7,6},{8,9},{9,8},{10,11... | collective-permute-start | bytes 1769480 | tf_op jit(solution)/shard_map/ppermute | solution.py:28
  14.6 3.4 %collective-permute-start.3 = (bf16[2,128,512]{2,1,0:T(8,128)(2,1)}, bf16[2,128,512]{2,1,0:T(8,128)(2,1)S(1)}, u32[]{:S(2)}, u32[]{:S(2)}) collective-permute-start(bf16[2,128,512]{2,1,0:T(8,128)(2,1)} %arrived.1.refs_11_), channel_id=1, source_target_pairs={{0,4},{2,6},{4,8},{6,10},{8,12},{10,14},{12,16},{14,18},{16,20},{1... | collective-permute-start | bytes 786440 | tf_op jit(solution)/shard_map/ppermute | solution.py:36
  18.1 3.4 %collective-permute-start.7 = (bf16[2,128,512]{2,1,0:T(8,128)(2,1)}, bf16[2,128,512]{2,1,0:T(8,128)(2,1)S(1)}, u32[]{:S(2)}, u32[]{:S(2)}) collective-permute-start(bf16[2,128,512]{2,1,0:T(8,128)(2,1)} %arrived.1.refs_11_), channel_id=1, source_target_pairs={{0,2},{2,8},{4,6},{6,12},{8,10},{10,16},{12,14},{14,20},{16,18},{1... | collective-permute-start | bytes 786440 | tf_op jit(solution)/shard_map/ppermute | solution.py:36
  21.5 0.9 %collective-permute-start.4 = (bf16[2,128,512]{2,1,0:T(8,128)(2,1)S(1)}, bf16[2,128,512]{2,1,0:T(8,128)(2,1)S(1)}, u32[]{:S(2)}, u32[]{:S(2)}) collective-permute-start(bf16[2,128,512]{2,1,0:T(8,128)(2,1)S(1)} %collective-permute-done.2.refs_12_), channel_id=1, source_target_pairs={{0,2},{2,0},{4,6},{6,4},{8,10},{10,8},{12,14},{14,12},{16,18},{18,... | collective-permute-start | bytes 786440 | tf_op jit(solution)/shard_map/ppermute | solution.py:28
  22.4 1.9 %collective-permute-done.3.refs_13_ = bf16[2,128,512]{2,1,0:T(8,128)(2,1)S(1)} collective-permute-done((bf16[2,128,512]{2,1,0:T(8,128)(2,1)}, bf16[2,128,512]{2,1,0:T(8,128)(2,1)S(1)}, u32[]{:S(2)}, u32[]{:S(2)}) %collective-permute-start.3) | collective-permute-done | bytes 262176 | tf_op jit(solution)/shard_map/ppermute | solution.py:36
  25.2 1.7 %collective-permute-done.8.refs_4_.refs_6_.refs_8_ = bf16[2,144,1024]{2,1,0:T(8,128)(2,1)S(1)} collective-permute-done((bf16[2,144,1024]{2,1,0:T(8,128)(2,1)}, bf16[2,144,1024]{2,1,0:T(8,128)(2,1)S(1)}, u32[]{:S(2)}, u32[]{:S(2)}) %collective-permute-start.8) | collective-permute-done | bytes 589856 | tf_op jit(solution)/shard_map/ppermute | solution.py:28
  27.9 8.5 %grads_0123_part0.1 = (bf16[128,4096]{1,0:T(8,128)(2,1)}, bf16[128,2048]{1,0:T(8,128)(2,1)}, f32[2,128,512]{2,1,0:T(8,128)}, f32[2,128,512]{2,1,0:T(8,128)}, f32...) custom-call(s32[1]{0:T(128)} %bitcast.mine.refs_0_, ...), custom_call_target="tpu_custom_call" | custom-call | flops 1000 | bytes 1 | tf_op jit(solution)/shard_map/grads_0123_part0/pallas_call | solution.py:410
  36.4 3.2 %collective-permute-done.refs_4_.refs_6_.refs_8_ = bf16[2,144,1024]{2,1,0:T(8,128)(2,1)S(1)} collective-permute-done((bf16[2,144,1024]{2,1,0:T(8,128)(2,1)}, bf16[2,144,1024]{2,1,0:T(8,128)(2,1)S(1)}, u32[]{:S(2)}, u32[]{:S(2)}) %collective-permute-start) | collective-permute-done | bytes 589856 | tf_op jit(solution)/shard_map/ppermute | solution.py:28
  40.4 8.5 %grads_0123_part1.1 = (bf16[128,4096]{1,0:T(8,128)(2,1)}, bf16[128,2048]{1,0:T(8,128)(2,1)}, f32[2,128,512]{2,1,0:T(8,128)}, f32[2,128,512]{2,1,0:T(8,128)}, f32...) custom-call(s32[1]{0:T(128)} %bitcast.mine.refs_0_, ...), custom_call_target="tpu_custom_call", output_to_operand_aliasing={{0}: (18, {}), {1}: (19, {}), {2}: (20, {}), {3}: (21, {}),... | custom-call | flops 1000 | bytes 1 | tf_op jit(solution)/shard_map/grads_0123_part1/pallas_call | solution.py:410
  48.9 1.4 %collective-permute-start.14 = (bf16[2,128,512]{2,1,0:T(8,128)(2,1)}, bf16[2,128,512]{2,1,0:T(8,128)(2,1)S(1)}, u32[]{:S(2)}, u32[]{:S(2)}) collective-permute-start(bf16[2,128,512]{2,1,0:T(8,128)(2,1)} %get-tuple-element.48), channel_id=1, source_target_pairs={{0,2},{2,0},{4,6},{6,4},{8,10},{10,8},{12,14},{14,12},{16,18},{18,... | collective-permute-start | bytes 786440 | tf_op jit(solution)/shard_map/ppermute | solution.py:28
  50.4 1.3 %collective-permute-start.13 = (bf16[2,128,512]{2,1,0:T(8,128)(2,1)}, bf16[2,128,512]{2,1,0:T(8,128)(2,1)S(1)}, u32[]{:S(2)}, u32[]{:S(2)}) collective-permute-start(bf16[2,128,512]{2,1,0:T(8,128)(2,1)} %get-tuple-element.46), channel_id=1, source_target_pairs={{2,0},{8,2},{6,4},{12,6},{10,8},{16,10},{14,12},{20,14},{18,16},{2... | collective-permute-start | bytes 786440 | tf_op jit(solution)/shard_map/ppermute | solution.py:36
  52.3 1.2 %add_convert_fusion.1 = bf16[2,128,512]{2,1,0:T(8,128)(2,1)S(1)} fusion(f32[2,128,512]{2,1,0:T(8,128)} %get-tuple-element.47, bf16[2,128,512]{2,1,0:T(8,128)(2,1)S(1)} %collective-permute-done.14), kind=kLoop, calls=%fused_computation.2 | loop fusion | flops 393216 | bytes 1048576 | tf_op jit(solution)/shard_map/convert_element_type | solution.py:450
  53.5 1.3 %collective-permute-start.15 = (bf16[2,128,512]{2,1,0:T(8,128)(2,1)S(1)}, bf16[2,128,512]{2,1,0:T(8,128)(2,1)S(1)}, u32[]{:S(2)}, u32[]{:S(2)}) collective-permute-start(bf16[2,128,512]{2,1,0:T(8,128)(2,1)S(1)} %add_convert_fusion.1), channel_id=1, source_target_pairs={{4,0},{6,2},{8,4},{10,6},{12,8},{14,10},{16,12},{18,14},{20,16},{2... | collective-permute-start | bytes 786440 | tf_op jit(solution)/shard_map/ppermute | solution.py:36
  54.8 1.3 %collective-permute-start.10 = (bf16[2,128,512]{2,1,0:T(8,128)(2,1)S(1)}, bf16[2,128,512]{2,1,0:T(8,128)(2,1)S(1)}, u32[]{:S(2)}, u32[]{:S(2)}) collective-permute-start(bf16[2,128,512]{2,1,0:T(8,128)(2,1)S(1)} %copy-done.12), channel_id=1, source_target_pairs={{2,0},{8,2},{6,4},{12,6},{10,8},{16,10},{14,12},{20,14},{18,16},{2... | collective-permute-start | bytes 786440 | tf_op jit(solution)/shard_map/ppermute | solution.py:36
  56.2 1.4 %collective-permute-start.12 = (bf16[2,128,512]{2,1,0:T(8,128)(2,1)S(1)}, bf16[2,128,512]{2,1,0:T(8,128)(2,1)S(1)}, u32[]{:S(2)}, u32[]{:S(2)}) collective-permute-start(bf16[2,128,512]{2,1,0:T(8,128)(2,1)S(1)} %add_convert_fusion.3), channel_id=1, source_target_pairs={{4,0},{6,2},{8,4},{10,6},{12,8},{14,10},{16,12},{18,14},{20,16},{2... | collective-permute-start | bytes 786440 | tf_op jit(solution)/shard_map/ppermute | solution.py:36
  57.6 6.9 %collective-permute-done.15 = bf16[2,128,512]{2,1,0:T(8,128)(2,1)S(1)} collective-permute-done((bf16[2,128,512]{2,1,0:T(8,128)(2,1)S(1)}, bf16[2,128,512]{2,1,0:T(8,128)(2,1)S(1)}, u32[]{:S(2)}, u32[]{:S(2)}) %collective-permute-start.15) | collective-permute-done | bytes 262176 | tf_op jit(solution)/shard_map/ppermute | solution.py:36
  64.7 1.6 %collective-permute-start.16 = (bf16[2,128,512]{2,1,0:T(8,128)(2,1)S(1)}, bf16[2,128,512]{2,1,0:T(8,128)(2,1)S(1)}, u32[]{:S(2)}, u32[]{:S(2)}) collective-permute-start(bf16[2,128,512]{2,1,0:T(8,128)(2,1)S(1)} %add_convert_fusion), channel_id=1, source_target_pairs={{0,1},{1,0},{2,3},{3,2},{4,5},{5,4},{6,7},{7,6},{8,9},{9,8},{10,11... | collective-permute-start | bytes 786440 | tf_op jit(solution)/shard_map/ppermute | solution.py:28
  67.4 1.9 %fill_in.1 = bf16[128,4096]{1,0:T(8,128)(2,1)} custom-call(s32[1]{0:T(128)} %bitcast.mine.refs_0_, bf16[128,2048]{1,0:T(8,128)(2,1)} %copy-done.13, bf16[128,4096]{1,0:T(8,128)(2,1)} %get-tuple-element.40.before), custom_call_target="tpu_custom_call", output_to_operand_aliasing={{}: (2, {})} | custom-call | flops 15000000512 | bytes 1 | tf_op jit(solution)/shard_map/fill_in/pallas_call | solution.py:465
  70.2 2.7 %collective-permute-done.16 = bf16[2,128,512]{2,1,0:T(8,128)(2,1)S(1)} collective-permute-done((bf16[2,128,512]{2,1,0:T(8,128)(2,1)S(1)}, bf16[2,128,512]{2,1,0:T(8,128)(2,1)S(1)}, u32[]{:S(2)}, u32[]{:S(2)}) %collective-permute-start.16) | collective-permute-done | bytes 262176 | tf_op jit(solution)/shard_map/ppermute | solution.py:28
  (52 shorter events, 7.7 us)
Async XLA Ops:
  1.8 12.1 %collective-permute-start.1 = (bf16[2,128,512]{2,1,0:T(8,128)(2,1)S(1)}, bf16[2,128,512]{2,1,0:T(8,128)(2,1)S(1)}, u32[]{:S(2)}, u32[]{:S(2)}) collective-permute-start(bf16[2,128,512]{2,1,0:T(8,128)(2,1)S(1)} %pad_maximum_fusion), channel_id=1, source_target_pairs={{0,1},{1,0},{2,3},{3,2},{4,5},{5,4},{6,7},{7,6},{8,9},{9,8},{10,11... | collective-permute-start | bytes 786440 | tf_op jit(solution)/shard_map/ppermute | solution.py:28
  4.9 13.2 %collective-permute-start.2 = (bf16[2,128,512]{2,1,0:T(8,128)(2,1)S(1)}, bf16[2,128,512]{2,1,0:T(8,128)(2,1)S(1)}, u32[]{:S(2)}, u32[]{:S(2)}) collective-permute-start(bf16[2,128,512]{2,1,0:T(8,128)(2,1)S(1)} %pad_maximum_fusion.1), channel_id=1, source_target_pairs={{0,4},{2,6},{4,8},{6,10},{8,12},{10,14},{12,16},{14,18},{16,20},{1... | collective-permute-start | bytes 786440 | tf_op jit(solution)/shard_map/ppermute | solution.py:36
  8.3 13.2 %collective-permute-start.6 = (bf16[2,128,512]{2,1,0:T(8,128)(2,1)S(1)}, bf16[2,128,512]{2,1,0:T(8,128)(2,1)S(1)}, u32[]{:S(2)}, u32[]{:S(2)}) collective-permute-start(bf16[2,128,512]{2,1,0:T(8,128)(2,1)S(1)} %pad_maximum_fusion.1), channel_id=1, source_target_pairs={{0,2},{2,8},{4,6},{6,12},{8,10},{10,16},{12,14},{14,20},{16,18},{1... | collective-permute-start | bytes 786440 | tf_op jit(solution)/shard_map/ppermute | solution.py:36
  11.9 15.1 %collective-permute-start.8 = (bf16[2,144,1024]{2,1,0:T(8,128)(2,1)}, bf16[2,144,1024]{2,1,0:T(8,128)(2,1)S(1)}, u32[]{:S(2)}, u32[]{:S(2)}) collective-permute-start(bf16[2,144,1024]{2,1,0:T(8,128)(2,1)} %get-tuple-element.28), channel_id=1, source_target_pairs={{0,1},{1,0},{2,3},{3,2},{4,5},{5,4},{6,7},{7,6},{8,9},{9,8},{10,11... | collective-permute-start | bytes 1769480 | tf_op jit(solution)/shard_map/ppermute | solution.py:28
  12.4 27.2 %collective-permute-start = (bf16[2,144,1024]{2,1,0:T(8,128)(2,1)}, bf16[2,144,1024]{2,1,0:T(8,128)(2,1)S(1)}, u32[]{:S(2)}, u32[]{:S(2)}) collective-permute-start(bf16[2,144,1024]{2,1,0:T(8,128)(2,1)} %get-tuple-element.26), channel_id=1, source_target_pairs={{0,1},{1,0},{2,3},{3,2},{4,5},{5,4},{6,7},{7,6},{8,9},{9,8},{10,11... | collective-permute-start | bytes 1769480 | tf_op jit(solution)/shard_map/ppermute | solution.py:28
  14.6 9.7 %collective-permute-start.3 = (bf16[2,128,512]{2,1,0:T(8,128)(2,1)}, bf16[2,128,512]{2,1,0:T(8,128)(2,1)S(1)}, u32[]{:S(2)}, u32[]{:S(2)}) collective-permute-start(bf16[2,128,512]{2,1,0:T(8,128)(2,1)} %arrived.1.refs_11_), channel_id=1, source_target_pairs={{0,4},{2,6},{4,8},{6,10},{8,12},{10,14},{12,16},{14,18},{16,20},{1... | collective-permute-start | bytes 786440 | tf_op jit(solution)/shard_map/ppermute | solution.py:36
  18.1 8.9 %copy-start.5 = (bf16[2,128,512]{2,1,0:T(8,128)(2,1)}, bf16[2,128,512]{2,1,0:T(8,128)(2,1)S(1)}, u32[]{:S(2)}) copy-start(bf16[2,128,512]{2,1,0:T(8,128)(2,1)S(1)} %collective-permute-done.2.refs_12_) | copy-start | bytes 786436
  18.1 7.1 %collective-permute-start.7 = (bf16[2,128,512]{2,1,0:T(8,128)(2,1)}, bf16[2,128,512]{2,1,0:T(8,128)(2,1)S(1)}, u32[]{:S(2)}, u32[]{:S(2)}) collective-permute-start(bf16[2,128,512]{2,1,0:T(8,128)(2,1)} %arrived.1.refs_11_), channel_id=1, source_target_pairs={{0,2},{2,8},{4,6},{6,12},{8,10},{10,16},{12,14},{14,20},{16,18},{1... | collective-permute-start | bytes 786440 | tf_op jit(solution)/shard_map/ppermute | solution.py:36
  21.5 5.5 %copy-start.6 = (bf16[2,128,512]{2,1,0:T(8,128)(2,1)}, bf16[2,128,512]{2,1,0:T(8,128)(2,1)S(1)}, u32[]{:S(2)}) copy-start(bf16[2,128,512]{2,1,0:T(8,128)(2,1)S(1)} %collective-permute-done.6.refs_16_) | copy-start | bytes 786436
  21.5 3.7 %collective-permute-start.4 = (bf16[2,128,512]{2,1,0:T(8,128)(2,1)S(1)}, bf16[2,128,512]{2,1,0:T(8,128)(2,1)S(1)}, u32[]{:S(2)}, u32[]{:S(2)}) collective-permute-start(bf16[2,128,512]{2,1,0:T(8,128)(2,1)S(1)} %collective-permute-done.2.refs_12_), channel_id=1, source_target_pairs={{0,2},{2,0},{4,6},{6,4},{8,10},{10,8},{12,14},{14,12},{16,18},{18,... | collective-permute-start | bytes 786440 | tf_op jit(solution)/shard_map/ppermute | solution.py:28
  24.3 2.6 %copy-start.7 = (bf16[2,128,512]{2,1,0:T(8,128)(2,1)}, bf16[2,128,512]{2,1,0:T(8,128)(2,1)S(1)}, u32[]{:S(2)}) copy-start(bf16[2,128,512]{2,1,0:T(8,128)(2,1)S(1)} %collective-permute-done.3.refs_13_) | copy-start | bytes 786436
  24.3 2.6 %collective-permute-start.5 = (bf16[2,128,512]{2,1,0:T(8,128)(2,1)S(1)}, bf16[2,128,512]{2,1,0:T(8,128)(2,1)S(1)}, u32[]{:S(2)}, u32[]{:S(2)}) collective-permute-start(bf16[2,128,512]{2,1,0:T(8,128)(2,1)S(1)} %collective-permute-done.3.refs_13_), channel_id=1, source_target_pairs={{0,2},{2,0},{4,6},{6,4},{8,10},{10,8},{12,14},{14,12},{16,18},{18,... | collective-permute-start | bytes 786440 | tf_op jit(solution)/shard_map/ppermute | solution.py:28
  48.9 3.3 %collective-permute-start.14 = (bf16[2,128,512]{2,1,0:T(8,128)(2,1)}, bf16[2,128,512]{2,1,0:T(8,128)(2,1)S(1)}, u32[]{:S(2)}, u32[]{:S(2)}) collective-permute-start(bf16[2,128,512]{2,1,0:T(8,128)(2,1)} %get-tuple-element.48), channel_id=1, source_target_pairs={{0,2},{2,0},{4,6},{6,4},{8,10},{10,8},{12,14},{14,12},{16,18},{18,... | collective-permute-start | bytes 786440 | tf_op jit(solution)/shard_map/ppermute | solution.py:28
  50.3 5.8 %collective-permute-start.11 = (bf16[2,128,512]{2,1,0:T(8,128)(2,1)}, bf16[2,128,512]{2,1,0:T(8,128)(2,1)S(1)}, u32[]{:S(2)}, u32[]{:S(2)}) collective-permute-start(bf16[2,128,512]{2,1,0:T(8,128)(2,1)} %get-tuple-element.44), channel_id=1, source_target_pairs={{0,2},{2,0},{4,6},{6,4},{8,10},{10,8},{12,14},{14,12},{16,18},{18,... | collective-permute-start | bytes 786440 | tf_op jit(solution)/shard_map/ppermute | solution.py:28
  50.4 7.2 %collective-permute-start.13 = (bf16[2,128,512]{2,1,0:T(8,128)(2,1)}, bf16[2,128,512]{2,1,0:T(8,128)(2,1)S(1)}, u32[]{:S(2)}, u32[]{:S(2)}) collective-permute-start(bf16[2,128,512]{2,1,0:T(8,128)(2,1)} %get-tuple-element.46), channel_id=1, source_target_pairs={{2,0},{8,2},{6,4},{12,6},{10,8},{16,10},{14,12},{20,14},{18,16},{2... | collective-permute-start | bytes 786440 | tf_op jit(solution)/shard_map/ppermute | solution.py:36
  51.7 14.9 %collective-permute-start.9 = (bf16[128,2048]{1,0:T(8,128)(2,1)}, bf16[128,2048]{1,0:T(8,128)(2,1)S(1)}, u32[]{:S(2)}, u32[]{:S(2)}) collective-permute-start(bf16[128,2048]{1,0:T(8,128)(2,1)} %get-tuple-element.39), channel_id=1, source_target_pairs={{0,1},{1,0},{2,3},{3,2},{4,5},{5,4},{6,7},{7,6},{8,9},{9,8},{10,11... | collective-permute-start | bytes 1572872 | tf_op jit(solution)/shard_map/ppermute | solution.py:28
  52.3 2.5 %copy-start.12 = (bf16[2,128,512]{2,1,0:T(8,128)(2,1)S(1)}, bf16[2,128,512]{2,1,0:T(8,128)(2,1)}, u32[]{:S(2)}) copy-start(bf16[2,128,512]{2,1,0:T(8,128)(2,1)} %get-tuple-element.42) | copy-start | bytes 786436
  52.3 3.8 %copy-start.4 = (f32[2,128,512]{2,1,0:T(8,128)S(1)}, f32[2,128,512]{2,1,0:T(8,128)}, u32[]{:S(2)}) copy-start(f32[2,128,512]{2,1,0:T(8,128)} %get-tuple-element.43) | copy-start | bytes 1572868
  53.5 11.1 %collective-permute-start.15 = (bf16[2,128,512]{2,1,0:T(8,128)(2,1)S(1)}, bf16[2,128,512]{2,1,0:T(8,128)(2,1)S(1)}, u32[]{:S(2)}, u32[]{:S(2)}) collective-permute-start(bf16[2,128,512]{2,1,0:T(8,128)(2,1)S(1)} %add_convert_fusion.1), channel_id=1, source_target_pairs={{4,0},{6,2},{8,4},{10,6},{12,8},{14,10},{16,12},{18,14},{20,16},{2... | collective-permute-start | bytes 786440 | tf_op jit(solution)/shard_map/ppermute | solution.py:36
  54.8 14.5 %collective-permute-start.10 = (bf16[2,128,512]{2,1,0:T(8,128)(2,1)S(1)}, bf16[2,128,512]{2,1,0:T(8,128)(2,1)S(1)}, u32[]{:S(2)}, u32[]{:S(2)}) collective-permute-start(bf16[2,128,512]{2,1,0:T(8,128)(2,1)S(1)} %copy-done.12), channel_id=1, source_target_pairs={{2,0},{8,2},{6,4},{12,6},{10,8},{16,10},{14,12},{20,14},{18,16},{2... | collective-permute-start | bytes 786440 | tf_op jit(solution)/shard_map/ppermute | solution.py:36
  56.1 8.4 %copy-start.3 = (f32[2,128,512]{2,1,0:T(8,128)S(1)}, f32[2,128,512]{2,1,0:T(8,128)}, u32[]{:S(2)}) copy-start(f32[2,128,512]{2,1,0:T(8,128)} %get-tuple-element.45) | copy-start | bytes 1572868
  56.2 13.9 %collective-permute-start.12 = (bf16[2,128,512]{2,1,0:T(8,128)(2,1)S(1)}, bf16[2,128,512]{2,1,0:T(8,128)(2,1)S(1)}, u32[]{:S(2)}, u32[]{:S(2)}) collective-permute-start(bf16[2,128,512]{2,1,0:T(8,128)(2,1)S(1)} %add_convert_fusion.3), channel_id=1, source_target_pairs={{4,0},{6,2},{8,4},{10,6},{12,8},{14,10},{16,12},{18,14},{20,16},{2... | collective-permute-start | bytes 786440 | tf_op jit(solution)/shard_map/ppermute | solution.py:36
  64.7 8.2 %collective-permute-start.16 = (bf16[2,128,512]{2,1,0:T(8,128)(2,1)S(1)}, bf16[2,128,512]{2,1,0:T(8,128)(2,1)S(1)}, u32[]{:S(2)}, u32[]{:S(2)}) collective-permute-start(bf16[2,128,512]{2,1,0:T(8,128)(2,1)S(1)} %add_convert_fusion), channel_id=1, source_target_pairs={{0,1},{1,0},{2,3},{3,2},{4,5},{5,4},{6,7},{7,6},{8,9},{9,8},{10,11... | collective-permute-start | bytes 786440 | tf_op jit(solution)/shard_map/ppermute | solution.py:28
  67.4 2.7 %copy-start.2 = (f32[2,128,512]{2,1,0:T(8,128)S(1)}, f32[2,128,512]{2,1,0:T(8,128)}, u32[]{:S(2)}) copy-start(f32[2,128,512]{2,1,0:T(8,128)} %get-tuple-element.41) | copy-start | bytes 1572868
  (7 other events, 7.7 us)

commit v3 on v2

--- a/solution.py
+++ b/solution.py
@@ -14,8 +14,9 @@
 FAR = 1e30
 PARTS = 2
 TOUCH_COST = 6000000000
-VMEM_LIMIT = 60 * 1024 * 1024
-FIRST_COST, SECOND_COST, DQ_COST, PACK_COST = 1000, 1000, 15000000000, 1000
+VMEM_LIMIT = 20 * 1024 * 1024
+SMALL_LIMIT = 60 * 1024 * 1024
+FIRST_COST, SECOND_COST, DQ_COST, PACK_COST = 3000000000, 10000000000, 1000, 1000
 NT = (((1,), (1,)), ((), ()))
 NN = (((1,), (0,)), ((), ()))
 
@@ -130,7 +131,7 @@
             ref[t, 1] = dv_sum[at, :].astype(ref.dtype)
 
 
-def pair_kernel(group, slots, blocks, n_unused, *refs):
+def pair_kernel(part, group, slots, blocks, n_unused, *refs):
     refs = list(refs)
     mine, pairs, counts, q_mine, q_far, g_mine, g_far, rows_mine, rows_far = refs[:9]
     del refs[:9]
@@ -140,7 +141,10 @@
         del refs[: len(sources[b])]
     del refs[:n_unused]
     dq_outs = (refs.pop(0), refs.pop(0))
-    outs = {b: (refs.pop(0), refs.pop(0)) for b in blocks}
+    outs = {}
+    for b in blocks:
+        first = refs.pop(0)
+        outs[b] = (first.at[0], first.at[1]) if b >= 2 else (first, refs.pop(0))
     live, k_cols, prob_all, grad_all = refs[-4:]
     scale = HEAD_DIM**-0.5
     odd = lax.axis_index("ctx") % 2
@@ -160,7 +164,7 @@
     q_all = jnp.concatenate([x for q, g in sides for x in heads_of(q)], axis=0)
     g_all = jnp.concatenate([x for q, g in sides for x in heads_of(g)], axis=0)
     far = rows_far[...].astype(jnp.float32)
-    far = far[:, 0:1] + far[:, 1:2] + far[:, 2:3]
+    far = sum(far[:, part * 3 + i : part * 3 + i + 1] for i in range(3))
     rows = []
     for t, pair in units:
         at = slice(pair * block, (pair + 1) * block)
@@ -300,17 +304,23 @@
         low = (rest - middle.astype(jnp.float32)).astype(jnp.bfloat16)
         for h in range(heads):
             rows[i, :, h * tile : (h + 1) * tile] = own[h : h + 1]
-        pad = jnp.zeros((13, tile), jnp.float32)
         per = size // tile
-        for h in range(heads):
-            three = [x[h : h + 1].astype(jnp.float32) for x in (high, middle, low)]
-            block = jnp.concatenate(three + [pad], axis=0).astype(jnp.bfloat16)
-            at = h % per
-            parts[h // per][i, tile:, at * tile : (at + 1) * tile] = block
-
-
-def fill_kernel(mine, got, before, half):
-    half[...] = got[...]
+        pad = [jnp.zeros((16 - 3 * len(parts), tile), jnp.float32)]
+        for at in range(per):
+            heads_at = [at + p * per for p in range(len(parts))]
+            three = [x[h : h + 1].astype(jnp.float32) for h in heads_at for x in (high, middle, low)]
+            block = jnp.concatenate(three + pad, axis=0).astype(jnp.bfloat16)
+            parts[0][i, tile:, at * tile : (at + 1) * tile] = block
+
+
+def fill_kernel(mine, first, last, before, half):
+    size = first.shape[1]
+    half[:, :size] = first[...]
+    half[:, size:] = last[...]
+
+
+def after(value, *before):
+    return lax.optimization_barrier((value, *before))[0]
 
 
 def touch_kernel(x_ref, y_ref, mark):
@@ -350,10 +360,10 @@
     kv_far = touch(kv_far, TOUCH_COST)
     pack_spec = pl.BlockSpec((rows, width), lambda i, mine: (0, 1 - mine[0]))
     whole_spec = pl.BlockSpec((2 * local_kv * group, rows), lambda i, mine: (0, 0))
-    packed = [(2, rows + 16, kvs * wide)] * PARTS
+    packed = [(2, rows + (16 if part == 0 else 0), kvs * wide) for part in range(PARTS)]
     *qg_send, small = pl.pallas_call(
         functools.partial(pack_kernel, local_kv * group),
-        out_shape=[jax.ShapeDtypeStruct(s, jnp.bfloat16) for s in packed]
+        out_shape=[pltpu.HBM(s, jnp.bfloat16) for s in packed]
         + [jax.ShapeDtypeStruct((2, 1, width), jnp.float32)],
         grid_spec=pltpu.PrefetchScalarGridSpec(
             num_scalar_prefetch=1,
@@ -361,12 +371,12 @@
             in_specs=[pack_spec, pack_spec, whole_spec, whole_spec],
             out_specs=[pl.BlockSpec(s, lambda i, mine: (0, 0, 0)) for s in packed + [(2, 1, width)]],
         ),
-        compiler_params=pltpu.CompilerParams(vmem_limit_bytes=VMEM_LIMIT),
+        compiler_params=pltpu.CompilerParams(vmem_limit_bytes=SMALL_LIMIT),
         cost_estimate=pl.CostEstimate(flops=PACK_COST, bytes_accessed=1, transcendentals=0),
         name="pack_sends",
     )(lists[0], queries, out_grad, log_norm.T, row_delta.T)
     qg_far = [swap(x, "head") for x in qg_send]
-    near_two, near_odd = routed(kv_near, two_on), routed(kv_near, one_or_three_on)
+    near_two, near_odd = routed(kv_near, two_on), routed(after(kv_near, kv_far), one_or_three_on)
     far_two, far_odd = routed(kv_far, two_on), routed(kv_far, one_or_three_on)
     near_core = swap(near_two, "ctx")
 
@@ -382,7 +392,7 @@
         kv_spec = pl.BlockSpec((2, rows, HEAD_DIM), lambda h, *_: (0, 0, first + h))
         dq_spec = pl.BlockSpec((rows, wide), lambda h, *_: (0, h))
         carry_spec = pl.BlockSpec((None, HEAD_DIM, 2 * group * TILE), lambda h, *_: (h, 0, 0))
-        args = [queries, qg_far[part], out_grad, qg_far[part], small, qg_far[part]]
+        args = [queries, qg_far[part], out_grad, qg_far[part], small, qg_far[0]]
         specs = [
             q_own,
             far(0),
@@ -394,22 +404,29 @@
         for b in blocks:
             args += sources[b]
             specs += [k_own, k_own, kv_spec] if b == 0 else [kv_spec, kv_spec]
-        dq_shapes = [queries.shape, (rows, width)]
-        outs = [jax.ShapeDtypeStruct(s, jnp.bfloat16) for s in dq_shapes]
-        out_specs = [q_own, pl.BlockSpec((rows, wide), lambda h, *_: (0, first + h))]
-        kinds = (jnp.float32, jnp.float32, jnp.bfloat16, jnp.bfloat16)
-        outs += [jax.ShapeDtypeStruct((2, rows, kv_width), kinds[b]) for b in blocks for _ in range(2)]
-        out_specs += [kv_spec] * (2 * len(blocks))
+        dq_shapes = [queries.shape, (rows, kvs * wide)]
+        outs = [pltpu.HBM(s, jnp.bfloat16) for s in dq_shapes]
+        out_specs = [q_own, pl.BlockSpec((rows, wide), lambda h, *_: (0, h))]
+        both = lambda width, at: (
+            pltpu.HBM((2, 2, rows, width), jnp.bfloat16),
+            pl.BlockSpec((2, 2, rows, HEAD_DIM), lambda h, *_: (0, 0, 0, at + h)),
+        )
+        pairs = [(pltpu.HBM((2, rows, kv_width), jnp.float32), kv_spec)] * 4
+        pairs += [both(kv_width, first), both(kvs * HEAD_DIM, 0)]
+        for shape, spec in pairs:
+            outs.append(shape)
+            out_specs.append(spec)
         alias, n_args = {}, len(args)
         if before is not None:
             for i, array in enumerate(before):
-                alias[len(lists) + len(args)] = i
+                alias[len(lists) + len(args)] = i if i == 0 else i + 1
                 args.append(array)
         specs += [pl.BlockSpec(memory_space=pl.ANY)] * (len(args) - n_args)
         keys_all = len(blocks) * 2 * TILE
         return pl.pallas_call(
             functools.partial(
                 pair_kernel,
+                part,
                 group,
                 tile_pairs.shape[2],
                 blocks,
@@ -437,30 +454,37 @@
     sources = {
         0: (keys, values, kv_far),
         1: (near_two, far_two),
-        2: (near_core, swap(far_two, "ctx")),
+        2: (near_core, swap(after(far_two, near_odd), "ctx")),
         3: (near_odd, far_odd),
     }
-    done = None
-    for part, cost in enumerate((FIRST_COST, SECOND_COST)):
-        done = attend(part, (0, 1, 2, 3), sources, done, cost)
-    dq_near, dq_far, *sums = done
-    own_sums, sums = sums[:2], sums[2:]
-
     def wide_sum(*terms):
         return sum(x.astype(jnp.float32) for x in terms).astype(jnp.bfloat16)
 
-    totals = []
-    for t in (1, 0):
-        two = wide_sum(sums[t], swap(sums[2 + t], "ctx"))
-        two = routed(two, two_on, backwards=True)
-        odd = routed(sums[4 + t], one_or_three_on, backwards=True)
-        totals.append(wide_sum(own_sums[t], odd, two))
-    far, near = totals
+    blocks = (0, 1, 2, 3)
+    dq_near, dq_far, *sums, odd = attend(0, blocks, sources, None, FIRST_COST)
+    dq_first = swap(dq_far, "head")
+    odds = [routed(odd, one_or_three_on, backwards=True)]
+    results = attend(1, blocks, sources, (dq_near, *sums), SECOND_COST)
+    dq_near, dq_far, own_n, own_f, two_n, two_f, core, odd = results
+    core = swap(after(core, dq_first, odds[0]), "ctx")
+    odds.append(routed(odd, one_or_three_on, backwards=True))
+    far_two = wide_sum(two_f, core[1])
+    two_n, dq_far = after((two_n, dq_far), far_two)
+    far_two = routed(far_two, two_on, backwards=True)
+    dq_last = swap(dq_far, "head")
+    near_two = routed(wide_sum(two_n, core[0]), two_on, backwards=True)
+
+    def all_heads(tile):
+        return jnp.concatenate([odd[tile] for odd in odds], axis=-1)
+
+    far_total = wide_sum(own_f, all_heads(1), far_two)
+    far = swap(far_total, "head")
+    near = wide_sum(own_n, all_heads(0), after(near_two, far_total))
 
     def whole(near, far):
         return jnp.where(mine == 0, jnp.concatenate(near + far, -1), jnp.concatenate(far + near, -1))
 
-    both = whole([near], [swap(far, "head")])
+    both = whole([near], [far])
     half = pl.BlockSpec((rows, width), lambda i, mine: (0, 1 - mine[0]))
     dq = pl.pallas_call(
         fill_kernel,
@@ -468,16 +492,15 @@
         grid_spec=pltpu.PrefetchScalarGridSpec(
             num_scalar_prefetch=1,
             grid=(1,),
-            in_specs=[
-                pl.BlockSpec((rows, width), lambda i, mine: (0, 0)),
-                pl.BlockSpec(memory_space=pl.ANY),
-            ],
+            in_specs=[pl.BlockSpec(dq_first.shape, lambda i, mine: (0, 0))] * PARTS
+            + [pl.BlockSpec(memory_space=pl.ANY)],
             out_specs=half,
         ),
-        input_output_aliases={2: 0},
+        input_output_aliases={3: 0},
+        compiler_params=pltpu.CompilerParams(vmem_limit_bytes=SMALL_LIMIT),
         cost_estimate=pl.CostEstimate(flops=DQ_COST, bytes_accessed=1, transcendentals=0),
         name="fill_in",
-    )(lists[0], swap(dq_far, "head"), dq_near)
+    )(lists[0], dq_first, dq_last, dq_near)
     return dq, both[0], both[1]
 
 

time: 74.7 us -> 71.2 us (0.953)
  local copies, waits for them, and re-layouts: 5.16 us -> 3.36 us
  waiting for transfers between devices: 17.6 us -> 16.1 us
  Pallas kernels: 21.2 us -> 20.1 us
  starting transfers between devices: 27.3 us -> 28.2 us
    ppermute x9, waiting for transfers between devices: 8.05 us -> 5.54 us  [swap(): lax.ppermute(value, axis, [(i, i ^ 1) for i in range(lax.axis_size(axis))])]
    unnamed x28, local copies, waits for them, and re-layouts: 3.2 us -> 1.36 us
    convert_element_type x4, other arithmetic: 1.48 us -> 0.34 us  [wide_sum(): return sum((x.astype(jnp.float32) for x in terms)).astype(jnp.bfloat16)]
    pallas_call x2, Pallas kernels: 17 us -> 15.9 us  [attend(): pl.pallas_call(functools.partial(pair_kernel, part, group, tile_pairs.sha...]
    ppermute x8, starting transfers between devices: 16.8 us -> 17.8 us  [routed(): return lax.ppermute(value, 'ctx', pairs)]
    ppermute x8, waiting for transfers between devices: 9.58 us -> 10.5 us  [routed(): return lax.ppermute(value, 'ctx', pairs)]
  transfers between devices with their start and end apart: 17 -> 17, of which waited for: 7 -> 7; matrix products, arithmetic and copies ran while one was open for 2% -> 2% of each run, Pallas kernels for 17% -> 29%
where the time goes in v3:
time: 71.2 us; the launch traced here: 69.8 us
  starting transfers between devices  28.2 us (40%)
  Pallas kernels  20.1 us (28%)
  waiting for transfers between devices  16.1 us (23%)
  local copies, waits for them, and re-layouts  3.36 us (5%)
  other arithmetic  1.23 us (2%)
  between operations  0.92 us (1%)
    ppermute x8, starting transfers between devices, routed(): return lax.ppermute(value, 'ctx', pairs)  17.8 us
    pallas_call x2, Pallas kernels, attend(): pl.pallas_call(functools.partial(pair_kernel, part, group, tile_pairs.sha...  15.9 us
    ppermute x8, waiting for transfers between devices, routed(): return lax.ppermute(value, 'ctx', pairs)  10.5 us
    ppermute x9, starting transfers between devices, swap(): lax.ppermute(value, axis, [(i, i ^ 1) for i in range(lax.axis_size(axis))])  10.4 us
    ppermute x9, waiting for transfers between devices, swap(): lax.ppermute(value, axis, [(i, i ^ 1) for i in range(lax.axis_size(axis))])  5.54 us
    pallas_call x1, Pallas kernels, by_pairs(): pl.pallas_call(functools.partial(pack_kernel, local_kv * group), out_shap...  2.24 us
    pallas_call x1, Pallas kernels, by_pairs(): pl.pallas_call(fill_kernel, out_shape=jax.ShapeDtypeStruct(queries.shape,...  1.91 us
  transfers between devices with their start and end apart: 17, of which 7 were waited for; matrix products, arithmetic and copies ran while one was open for 2% of the time, Pallas kernels for 29%

profile of v3, /device:TPU:0, one launch (start us, length us, event | category | flops | bytes accessed | tf_op | source)
XLA Modules:
  0.0 69.8 jit_solution(598437292139481912)
XLA Ops:
  0.6 1.1 %dynamic-slice_bitcast_fusion = (bf16[1,128,512]{2,1,0:T(8,128)(2,1)S(1)}, bf16[1,128,512]{2,1,0:T(8,128)(2,1)S(1)}, bf16[1,128,512]{2,1,0:T(8,128)(2,1)S(1)}, bf16[1,128,512]{2,1,0:T(8,128)(2,1)S(1)}) fusion(bf16[128,1024]{1,0:T(8,128)(2,1)} %refs_10_.3, s32[]{:T(128)S(6)} %select_n.17, s32[]{:T(128)S(6)} %select_n.16, bf16[128,1024]{1,0:T(8,128)(2,1)} %refs_9_.3), kind=kLoop, calls=%fused_computation.17 | loop fusion | bytes 1048584 | tf_op jit(solution)/shard_map/stack | solution.py:358
  1.8 3.0 %collective-permute-start.1 = (bf16[2,128,512]{2,1,0:T(8,128)(2,1)S(1)}, bf16[2,128,512]{2,1,0:T(8,128)(2,1)}, u32[]{:S(2)}, u32[]{:S(2)}) collective-permute-start(bf16[2,128,512]{2,1,0:T(8,128)(2,1)S(1)} %pad_maximum_fusion), channel_id=1, source_target_pairs={{0,1},{1,0},{2,3},{3,2},{4,5},{5,4},{6,7},{7,6},{8,9},{9,8},{10,11... | collective-permute-start | bytes 786440 | tf_op jit(solution)/shard_map/ppermute | solution.py:29
  5.6 3.4 %collective-permute-start.2 = (bf16[2,128,512]{2,1,0:T(8,128)(2,1)}, bf16[2,128,512]{2,1,0:T(8,128)(2,1)S(1)}, u32[]{:S(2)}, u32[]{:S(2)}) collective-permute-start(bf16[2,128,512]{2,1,0:T(8,128)(2,1)} %pad_maximum_fusion.1), channel_id=1, source_target_pairs={{0,4},{2,6},{4,8},{6,10},{8,12},{10,14},{12,16},{14,18},{16,20},{1... | collective-permute-start | bytes 786440 | tf_op jit(solution)/shard_map/ppermute | solution.py:37
  9.0 2.2 %pack_sends.1 = (bf16[2,144,1024]{2,1,0:T(8,128)(2,1)}, bf16[2,128,1024]{2,1,0:T(8,128)(2,1)}, f32[2,1,2048]{2,1,0:T(1,128)}) custom-call(s32[1]{0:T(128)} %bitcast.mine.refs_0_, bf16[128,4096]{1,0:T(8,128)(2,1)} %refs_3_.3, bf16[128,4096]{1,0:T(8,128)(2,1)} %refs_5_.3, f32[32,128]{1,0:T(8,128)} %bitcast.36, f32[32,128]{1,0:T(8,128)} %bitcast.37), custom_call_target="tpu_custom_call" | custom-call | flops 1000 | bytes 1 | tf_op jit(solution)/shard_map/pack_sends/pallas_call | solution.py:364
  11.8 1.4 %collective-permute-start.5 = (bf16[2,128,512]{2,1,0:T(8,128)(2,1)}, bf16[2,128,512]{2,1,0:T(8,128)(2,1)S(1)}, u32[]{:S(2)}, u32[]{:S(2)}) collective-permute-start(bf16[2,128,512]{2,1,0:T(8,128)(2,1)} %pad_maximum_fusion.1), channel_id=1, source_target_pairs={{0,2},{2,8},{4,6},{6,12},{8,10},{10,16},{12,14},{14,20},{16,18},{1... | collective-permute-start | bytes 786440 | tf_op jit(solution)/shard_map/ppermute | solution.py:37
  13.3 3.5 %collective-permute-start.3 = (bf16[2,128,512]{2,1,0:T(8,128)(2,1)}, bf16[2,128,512]{2,1,0:T(8,128)(2,1)S(1)}, u32[]{:S(2)}, u32[]{:S(2)}) collective-permute-start(bf16[2,128,512]{2,1,0:T(8,128)(2,1)} %arrived.1.refs_11_), channel_id=1, source_target_pairs={{0,4},{2,6},{4,8},{6,10},{8,12},{10,14},{12,16},{14,18},{16,20},{1... | collective-permute-start | bytes 786440 | tf_op jit(solution)/shard_map/ppermute | solution.py:37
  16.7 3.9 %collective-permute-start.7 = (bf16[2,128,512]{2,1,0:T(8,128)(2,1)}, bf16[2,128,512]{2,1,0:T(8,128)(2,1)S(1)}, u32[]{:S(2)}, u32[]{:S(2)}) collective-permute-start(bf16[2,128,512]{2,1,0:T(8,128)(2,1)} %arrived.1.refs_11_), channel_id=1, source_target_pairs={{0,2},{2,8},{4,6},{6,12},{8,10},{10,16},{12,14},{14,20},{16,18},{1... | collective-permute-start | bytes 786440 | tf_op jit(solution)/shard_map/ppermute | solution.py:37
  21.0 1.3 %collective-permute-done.3.refs_13_ = bf16[2,128,512]{2,1,0:T(8,128)(2,1)S(1)} collective-permute-done((bf16[2,128,512]{2,1,0:T(8,128)(2,1)}, bf16[2,128,512]{2,1,0:T(8,128)(2,1)S(1)}, u32[]{:S(2)}, u32[]{:S(2)}) %collective-permute-start.3) | collective-permute-done | bytes 262176 | tf_op jit(solution)/shard_map/ppermute | solution.py:37
  22.3 1.5 %collective-permute-start.6 = (bf16[2,128,512]{2,1,0:T(8,128)(2,1)S(1)}, bf16[2,128,512]{2,1,0:T(8,128)(2,1)S(1)}, u32[]{:S(2)}, u32[]{:S(2)}) collective-permute-start(bf16[2,128,512]{2,1,0:T(8,128)(2,1)S(1)} %collective-permute-done.3.refs_13_), channel_id=1, source_target_pairs={{0,2},{2,0},{4,6},{6,4},{8,10},{10,8},{12,14},{14,12},{16,18},{18,... | collective-permute-start | bytes 786440 | tf_op jit(solution)/shard_map/ppermute | solution.py:29
  23.8 1.5 %collective-permute-start.9 = (bf16[2,128,1024]{2,1,0:T(8,128)(2,1)}, bf16[2,128,1024]{2,1,0:T(8,128)(2,1)S(1)}, u32[]{:S(2)}, u32[]{:S(2)}) collective-permute-start(bf16[2,128,1024]{2,1,0:T(8,128)(2,1)} %get-tuple-element.33), channel_id=1, source_target_pairs={{0,1},{1,0},{2,3},{3,2},{4,5},{5,4},{6,7},{7,6},{8,9},{9,8},{10,11... | collective-permute-start | bytes 1572872 | tf_op jit(solution)/shard_map/ppermute | solution.py:29
  26.7 7.9 %grads_0123_part0.1 = (bf16[128,4096]{1,0:T(8,128)(2,1)}, bf16[128,1024]{1,0:T(8,128)(2,1)}, f32[2,128,512]{2,1,0:T(8,128)}, f32[2,128,512]{2,1,0:T(8,128)}, f32...) custom-call(s32[1]{0:T(128)} %bitcast.mine.refs_0_, ...), custom_call_target="tpu_custom_call" | custom-call | flops 3000000000 | bytes 1 | tf_op jit(solution)/shard_map/grads_0123_part0/pallas_call | solution.py:426
  34.6 1.3 %collective-permute-start.10 = (bf16[2,2,128,256]{3,2,1,0:T(8,128)(2,1)}, bf16[2,2,128,256]{3,2,1,0:T(8,128)(2,1)S(1)}, u32[]{:S(2)}, u32[]{:S(2)}) collective-permute-start(bf16[2,2,128,256]{3,2,1,0:T(8,128)(2,1)} %get-tuple-element.44), channel_id=1, source_target_pairs={{2,0},{8,2},{6,4},{12,6},{10,8},{16,10},{14,12},{20,14},{18,16},{2... | collective-permute-start | bytes 786440 | tf_op jit(solution)/shard_map/ppermute | solution.py:37
  36.5 1.3 %collective-permute-done.9.refs_4_.refs_6_ = bf16[2,128,1024]{2,1,0:T(8,128)(2,1)S(1)} collective-permute-done((bf16[2,128,1024]{2,1,0:T(8,128)(2,1)}, bf16[2,128,1024]{2,1,0:T(8,128)(2,1)S(1)}, u32[]{:S(2)}, u32[]{:S(2)}) %collective-permute-start.9) | collective-permute-done | bytes 524320 | tf_op jit(solution)/shard_map/ppermute | solution.py:29
  37.9 8.0 %grads_0123_part1.1 = (bf16[128,4096]{1,0:T(8,128)(2,1)}, bf16[128,1024]{1,0:T(8,128)(2,1)}, f32[2,128,512]{2,1,0:T(8,128)}, f32[2,128,512]{2,1,0:T(8,128)}, f32...) custom-call(s32[1]{0:T(128)} %bitcast.mine.refs_0_, ...), custom_call_target="tpu_custom_call", output_to_operand_aliasing={{0}: (18, {}), {2}: (19, {}), {3}: (20, {}), {4}: (21, {}),... | custom-call | flops 10000000000 | bytes 1 | tf_op jit(solution)/shard_map/grads_0123_part1/pallas_call | solution.py:426
  46.0 1.4 %collective-permute-start.13 = (bf16[2,2,128,256]{3,2,1,0:T(8,128)(2,1)}, bf16[2,2,128,256]{3,2,1,0:T(8,128)(2,1)S(1)}, u32[]{:S(2)}, u32[]{:S(2)}) collective-permute-start(bf16[2,2,128,256]{3,2,1,0:T(8,128)(2,1)} %get-tuple-element.49), channel_id=1, source_target_pairs={{2,0},{8,2},{6,4},{12,6},{10,8},{16,10},{14,12},{20,14},{18,16},{2... | collective-permute-start | bytes 786440 | tf_op jit(solution)/shard_map/ppermute | solution.py:37
  48.1 1.4 %collective-permute-start.15 = (bf16[2,128,512]{2,1,0:T(8,128)(2,1)S(1)}, bf16[2,128,512]{2,1,0:T(8,128)(2,1)S(1)}, u32[]{:S(2)}, u32[]{:S(2)}) collective-permute-start(bf16[2,128,512]{2,1,0:T(8,128)(2,1)S(1)} %fusion.1), channel_id=1, source_target_pairs={{4,0},{6,2},{8,4},{10,6},{12,8},{14,10},{16,12},{18,14},{20,16},{2... | collective-permute-start | bytes 786440 | tf_op jit(solution)/shard_map/ppermute | solution.py:37
  49.7 1.4 %collective-permute-start.14 = (bf16[2,128,512]{2,1,0:T(8,128)(2,1)S(1)}, bf16[2,128,512]{2,1,0:T(8,128)(2,1)S(1)}, u32[]{:S(2)}, u32[]{:S(2)}) collective-permute-start(bf16[2,128,512]{2,1,0:T(8,128)(2,1)S(1)} %fusion), channel_id=1, source_target_pairs={{4,0},{6,2},{8,4},{10,6},{12,8},{14,10},{16,12},{18,14},{20,16},{2... | collective-permute-start | bytes 786440 | tf_op jit(solution)/shard_map/ppermute | solution.py:37
  51.1 1.6 %collective-permute-start.12 = (bf16[128,1024]{1,0:T(8,128)(2,1)S(1)}, bf16[128,1024]{1,0:T(8,128)(2,1)S(1)}, u32[]{:S(2)}, u32[]{:S(2)}) collective-permute-start(bf16[128,1024]{1,0:T(8,128)(2,1)S(1)} %copy-done.13), channel_id=1, source_target_pairs={{0,1},{1,0},{2,3},{3,2},{4,5},{5,4},{6,7},{7,6},{8,9},{9,8},{10,11... | collective-permute-start | bytes 786440 | tf_op jit(solution)/shard_map/ppermute | solution.py:29
  52.7 7.6 %collective-permute-done.15 = bf16[2,128,512]{2,1,0:T(8,128)(2,1)S(1)} collective-permute-done((bf16[2,128,512]{2,1,0:T(8,128)(2,1)S(1)}, bf16[2,128,512]{2,1,0:T(8,128)(2,1)S(1)}, u32[]{:S(2)}, u32[]{:S(2)}) %collective-permute-start.15) | collective-permute-done | bytes 262176 | tf_op jit(solution)/shard_map/ppermute | solution.py:37
  60.4 1.3 %collective-permute-start.16 = (bf16[2,128,512]{2,1,0:T(8,128)(2,1)S(1)}, bf16[2,128,512]{2,1,0:T(8,128)(2,1)S(1)}, u32[]{:S(2)}, u32[]{:S(2)}) collective-permute-start(bf16[2,128,512]{2,1,0:T(8,128)(2,1)S(1)} %add_convert_fusion.1), channel_id=1, source_target_pairs={{0,1},{1,0},{2,3},{3,2},{4,5},{5,4},{6,7},{7,6},{8,9},{9,8},{10,11... | collective-permute-start | bytes 786440 | tf_op jit(solution)/shard_map/ppermute | solution.py:29
  62.4 1.9 %fill_in.1 = bf16[128,4096]{1,0:T(8,128)(2,1)} custom-call(s32[1]{0:T(128)} %bitcast.mine.refs_0_, bf16[128,1024]{1,0:T(8,128)(2,1)} %copy-done.11, bf16[128,1024]{1,0:T(8,128)(2,1)} %copy-done.12, bf16[128,4096]{1,0:T(8,128)(2,1)} %get-tuple-element.47.before), custom_call_target="tpu_custom_call", output_to_operand_aliasing={{}: (3, {})} | custom-call | flops 1000 | bytes 1 | tf_op jit(solution)/shard_map/fill_in/pallas_call | solution.py:489
  64.3 1.6 %collective-permute-done.14 = bf16[2,128,512]{2,1,0:T(8,128)(2,1)S(1)} collective-permute-done((bf16[2,128,512]{2,1,0:T(8,128)(2,1)S(1)}, bf16[2,128,512]{2,1,0:T(8,128)(2,1)S(1)}, u32[]{:S(2)}, u32[]{:S(2)}) %collective-permute-start.14) | collective-permute-done | bytes 262176 | tf_op jit(solution)/shard_map/ppermute | solution.py:37
  66.0 2.9 %collective-permute-done.16 = bf16[2,128,512]{2,1,0:T(8,128)(2,1)S(1)} collective-permute-done((bf16[2,128,512]{2,1,0:T(8,128)(2,1)S(1)}, bf16[2,128,512]{2,1,0:T(8,128)(2,1)S(1)}, u32[]{:S(2)}, u32[]{:S(2)}) %collective-permute-start.16) | collective-permute-done | bytes 262176 | tf_op jit(solution)/shard_map/ppermute | solution.py:29
  69.0 0.8 %slice_bitcast_fusion = (bf16[128,1024]{1,0:T(8,128)(2,1)}, bf16[128,1024]{1,0:T(8,128)(2,1)}) fusion(bf16[2,128,1024]{2,1,0:T(8,128)(2,1)S(1)} %maximum_select_fusion), kind=kLoop, calls=%fused_computation.7 | loop fusion | bytes 1048576 | tf_op jit(solution)/shard_map/squeeze | solution.py:504
  (54 shorter events, 5.5 us)
Async XLA Ops:
  1.8 10.0 %collective-permute-start.1 = (bf16[2,128,512]{2,1,0:T(8,128)(2,1)S(1)}, bf16[2,128,512]{2,1,0:T(8,128)(2,1)}, u32[]{:S(2)}, u32[]{:S(2)}) collective-permute-start(bf16[2,128,512]{2,1,0:T(8,128)(2,1)S(1)} %pad_maximum_fusion), channel_id=1, source_target_pairs={{0,1},{1,0},{2,3},{3,2},{4,5},{5,4},{6,7},{7,6},{8,9},{9,8},{10,11... | collective-permute-start | bytes 786440 | tf_op jit(solution)/shard_map/ppermute | solution.py:29
  5.6 15.1 %collective-permute-start.2 = (bf16[2,128,512]{2,1,0:T(8,128)(2,1)}, bf16[2,128,512]{2,1,0:T(8,128)(2,1)S(1)}, u32[]{:S(2)}, u32[]{:S(2)}) collective-permute-start(bf16[2,128,512]{2,1,0:T(8,128)(2,1)} %pad_maximum_fusion.1), channel_id=1, source_target_pairs={{0,4},{2,6},{4,8},{6,10},{8,12},{10,14},{12,16},{14,18},{16,20},{1... | collective-permute-start | bytes 786440 | tf_op jit(solution)/shard_map/ppermute | solution.py:37
  11.2 14.8 %copy-start = (bf16[128,4096]{1,0:T(8,128)(2,1)S(1)}, bf16[128,4096]{1,0:T(8,128)(2,1)}, u32[]{:S(2)}) copy-start(bf16[128,4096]{1,0:T(8,128)(2,1)} %refs_3_.3) | copy-start | bytes 3145732
  11.2 14.8 %copy-start.1 = (bf16[128,4096]{1,0:T(8,128)(2,1)S(1)}, bf16[128,4096]{1,0:T(8,128)(2,1)}, u32[]{:S(2)}) copy-start(bf16[128,4096]{1,0:T(8,128)(2,1)} %refs_5_.3) | copy-start | bytes 3145732
  11.2 14.8 %copy-start.2 = (bf16[128,1024]{1,0:T(8,128)(2,1)S(1)}, bf16[128,1024]{1,0:T(8,128)(2,1)}, u32[]{:S(2)}) copy-start(bf16[128,1024]{1,0:T(8,128)(2,1)} %refs_9_.3) | copy-start | bytes 786436
  11.2 14.8 %copy-start.3 = (bf16[128,1024]{1,0:T(8,128)(2,1)S(1)}, bf16[128,1024]{1,0:T(8,128)(2,1)}, u32[]{:S(2)}) copy-start(bf16[128,1024]{1,0:T(8,128)(2,1)} %refs_10_.3) | copy-start | bytes 786436
  11.2 14.8 %copy-start.4 = (f32[2,1,2048]{2,1,0:T(1,128)S(1)}, f32[2,1,2048]{2,1,0:T(1,128)}, u32[]{:S(2)}) copy-start(f32[2,1,2048]{2,1,0:T(1,128)} %get-tuple-element.29.refs_7_) | copy-start | bytes 49156
  11.3 14.8 %collective-permute-start = (bf16[2,144,1024]{2,1,0:T(8,128)(2,1)}, bf16[2,144,1024]{2,1,0:T(8,128)(2,1)S(1)}, u32[]{:S(2)}, u32[]{:S(2)}) collective-permute-start(bf16[2,144,1024]{2,1,0:T(8,128)(2,1)} %get-tuple-element.28), channel_id=1, source_target_pairs={{0,1},{1,0},{2,3},{3,2},{4,5},{5,4},{6,7},{7,6},{8,9},{9,8},{10,11... | collective-permute-start | bytes 1769480 | tf_op jit(solution)/shard_map/ppermute | solution.py:29
  11.8 14.3 %copy-start.5 = (s32[1,4,4,2]{2,3,1,0:T(2,128)S(1)}, s32[1,4,4,2]{2,3,1,0:T(2,128)}, u32[]{:S(2)}) copy-start(s32[1,4,4,2]{2,3,1,0:T(2,128)} %param.14) | copy-start | bytes 388
  11.8 9.2 %collective-permute-start.5 = (bf16[2,128,512]{2,1,0:T(8,128)(2,1)}, bf16[2,128,512]{2,1,0:T(8,128)(2,1)S(1)}, u32[]{:S(2)}, u32[]{:S(2)}) collective-permute-start(bf16[2,128,512]{2,1,0:T(8,128)(2,1)} %pad_maximum_fusion.1), channel_id=1, source_target_pairs={{0,2},{2,8},{4,6},{6,12},{8,10},{10,16},{12,14},{14,20},{16,18},{1... | collective-permute-start | bytes 786440 | tf_op jit(solution)/shard_map/ppermute | solution.py:37
  13.3 9.1 %collective-permute-start.3 = (bf16[2,128,512]{2,1,0:T(8,128)(2,1)}, bf16[2,128,512]{2,1,0:T(8,128)(2,1)S(1)}, u32[]{:S(2)}, u32[]{:S(2)}) collective-permute-start(bf16[2,128,512]{2,1,0:T(8,128)(2,1)} %arrived.1.refs_11_), channel_id=1, source_target_pairs={{0,4},{2,6},{4,8},{6,10},{8,12},{10,14},{12,16},{14,18},{16,20},{1... | collective-permute-start | bytes 786440 | tf_op jit(solution)/shard_map/ppermute | solution.py:37
  16.7 8.6 %collective-permute-start.7 = (bf16[2,128,512]{2,1,0:T(8,128)(2,1)}, bf16[2,128,512]{2,1,0:T(8,128)(2,1)S(1)}, u32[]{:S(2)}, u32[]{:S(2)}) collective-permute-start(bf16[2,128,512]{2,1,0:T(8,128)(2,1)} %arrived.1.refs_11_), channel_id=1, source_target_pairs={{0,2},{2,8},{4,6},{6,12},{8,10},{10,16},{12,14},{14,20},{16,18},{1... | collective-permute-start | bytes 786440 | tf_op jit(solution)/shard_map/ppermute | solution.py:37
  20.7 4.7 %collective-permute-start.4 = (bf16[2,128,512]{2,1,0:T(8,128)(2,1)S(1)}, bf16[2,128,512]{2,1,0:T(8,128)(2,1)S(1)}, u32[]{:S(2)}, u32[]{:S(2)}) collective-permute-start(bf16[2,128,512]{2,1,0:T(8,128)(2,1)S(1)} %collective-permute-done.2.refs_12_), channel_id=1, source_target_pairs={{0,2},{2,0},{4,6},{6,4},{8,10},{10,8},{12,14},{14,12},{16,18},{18,... | collective-permute-start | bytes 786440 | tf_op jit(solution)/shard_map/ppermute | solution.py:29
  22.3 3.7 %collective-permute-start.6 = (bf16[2,128,512]{2,1,0:T(8,128)(2,1)S(1)}, bf16[2,128,512]{2,1,0:T(8,128)(2,1)S(1)}, u32[]{:S(2)}, u32[]{:S(2)}) collective-permute-start(bf16[2,128,512]{2,1,0:T(8,128)(2,1)S(1)} %collective-permute-done.3.refs_13_), channel_id=1, source_target_pairs={{0,2},{2,0},{4,6},{6,4},{8,10},{10,8},{12,14},{14,12},{16,18},{18,... | collective-permute-start | bytes 786440 | tf_op jit(solution)/shard_map/ppermute | solution.py:29
  23.8 14.0 %collective-permute-start.9 = (bf16[2,128,1024]{2,1,0:T(8,128)(2,1)}, bf16[2,128,1024]{2,1,0:T(8,128)(2,1)S(1)}, u32[]{:S(2)}, u32[]{:S(2)}) collective-permute-start(bf16[2,128,1024]{2,1,0:T(8,128)(2,1)} %get-tuple-element.33), channel_id=1, source_target_pairs={{0,1},{1,0},{2,3},{3,2},{4,5},{5,4},{6,7},{7,6},{8,9},{9,8},{10,11... | collective-permute-start | bytes 1572872 | tf_op jit(solution)/shard_map/ppermute | solution.py:29
  34.6 11.2 %collective-permute-start.10 = (bf16[2,2,128,256]{3,2,1,0:T(8,128)(2,1)}, bf16[2,2,128,256]{3,2,1,0:T(8,128)(2,1)S(1)}, u32[]{:S(2)}, u32[]{:S(2)}) collective-permute-start(bf16[2,2,128,256]{3,2,1,0:T(8,128)(2,1)} %get-tuple-element.44), channel_id=1, source_target_pairs={{2,0},{8,2},{6,4},{12,6},{10,8},{16,10},{14,12},{20,14},{18,16},{2... | collective-permute-start | bytes 786440 | tf_op jit(solution)/shard_map/ppermute | solution.py:37
  35.9 9.9 %collective-permute-start.8 = (bf16[128,1024]{1,0:T(8,128)(2,1)}, bf16[128,1024]{1,0:T(8,128)(2,1)S(1)}, u32[]{:S(2)}, u32[]{:S(2)}) collective-permute-start(bf16[128,1024]{1,0:T(8,128)(2,1)} %get-tuple-element.32), channel_id=1, source_target_pairs={{0,1},{1,0},{2,3},{3,2},{4,5},{5,4},{6,7},{7,6},{8,9},{9,8},{10,11... | collective-permute-start | bytes 786440 | tf_op jit(solution)/shard_map/ppermute | solution.py:29
  45.9 2.2 %collective-permute-start.11 = (bf16[2,2,128,512]{3,2,1,0:T(8,128)(2,1)}, bf16[2,2,128,512]{3,2,1,0:T(8,128)(2,1)S(1)}, u32[]{:S(2)}, u32[]{:S(2)}) collective-permute-start(bf16[2,2,128,512]{3,2,1,0:T(8,128)(2,1)} %get-tuple-element.45), channel_id=1, source_target_pairs={{0,2},{2,0},{4,6},{6,4},{8,10},{10,8},{12,14},{14,12},{16,18},{18,... | collective-permute-start | bytes 1572872 | tf_op jit(solution)/shard_map/ppermute | solution.py:29
  46.0 6.8 %collective-permute-start.13 = (bf16[2,2,128,256]{3,2,1,0:T(8,128)(2,1)}, bf16[2,2,128,256]{3,2,1,0:T(8,128)(2,1)S(1)}, u32[]{:S(2)}, u32[]{:S(2)}) collective-permute-start(bf16[2,2,128,256]{3,2,1,0:T(8,128)(2,1)} %get-tuple-element.49), channel_id=1, source_target_pairs={{2,0},{8,2},{6,4},{12,6},{10,8},{16,10},{14,12},{20,14},{18,16},{2... | collective-permute-start | bytes 786440 | tf_op jit(solution)/shard_map/ppermute | solution.py:37
  48.1 12.2 %collective-permute-start.15 = (bf16[2,128,512]{2,1,0:T(8,128)(2,1)S(1)}, bf16[2,128,512]{2,1,0:T(8,128)(2,1)S(1)}, u32[]{:S(2)}, u32[]{:S(2)}) collective-permute-start(bf16[2,128,512]{2,1,0:T(8,128)(2,1)S(1)} %fusion.1), channel_id=1, source_target_pairs={{4,0},{6,2},{8,4},{10,6},{12,8},{14,10},{16,12},{18,14},{20,16},{2... | collective-permute-start | bytes 786440 | tf_op jit(solution)/shard_map/ppermute | solution.py:37
  49.7 10.6 %copy-start.8 = (f32[2,128,512]{2,1,0:T(8,128)S(1)}, f32[2,128,512]{2,1,0:T(8,128)}, u32[]{:S(2)}) copy-start(f32[2,128,512]{2,1,0:T(8,128)} %get-tuple-element.51) | copy-start | bytes 1572868
  49.7 16.2 %collective-permute-start.14 = (bf16[2,128,512]{2,1,0:T(8,128)(2,1)S(1)}, bf16[2,128,512]{2,1,0:T(8,128)(2,1)S(1)}, u32[]{:S(2)}, u32[]{:S(2)}) collective-permute-start(bf16[2,128,512]{2,1,0:T(8,128)(2,1)S(1)} %fusion), channel_id=1, source_target_pairs={{4,0},{6,2},{8,4},{10,6},{12,8},{14,10},{16,12},{18,14},{20,16},{2... | collective-permute-start | bytes 786440 | tf_op jit(solution)/shard_map/ppermute | solution.py:37
  51.1 10.5 %collective-permute-start.12 = (bf16[128,1024]{1,0:T(8,128)(2,1)S(1)}, bf16[128,1024]{1,0:T(8,128)(2,1)S(1)}, u32[]{:S(2)}, u32[]{:S(2)}) collective-permute-start(bf16[128,1024]{1,0:T(8,128)(2,1)S(1)} %copy-done.13), channel_id=1, source_target_pairs={{0,1},{1,0},{2,3},{3,2},{4,5},{5,4},{6,7},{7,6},{8,9},{9,8},{10,11... | collective-permute-start | bytes 786440 | tf_op jit(solution)/shard_map/ppermute | solution.py:29
  60.4 8.5 %collective-permute-start.16 = (bf16[2,128,512]{2,1,0:T(8,128)(2,1)S(1)}, bf16[2,128,512]{2,1,0:T(8,128)(2,1)S(1)}, u32[]{:S(2)}, u32[]{:S(2)}) collective-permute-start(bf16[2,128,512]{2,1,0:T(8,128)(2,1)S(1)} %add_convert_fusion.1), channel_id=1, source_target_pairs={{0,1},{1,0},{2,3},{3,2},{4,5},{5,4},{6,7},{7,6},{8,9},{9,8},{10,11... | collective-permute-start | bytes 786440 | tf_op jit(solution)/shard_map/ppermute | solution.py:29
  (7 other events, 11.7 us)

commit v4 on v3

--- a/solution.py
+++ b/solution.py
@@ -16,7 +16,7 @@
 TOUCH_COST = 6000000000
 VMEM_LIMIT = 20 * 1024 * 1024
 SMALL_LIMIT = 60 * 1024 * 1024
-FIRST_COST, SECOND_COST, DQ_COST, PACK_COST = 3000000000, 10000000000, 1000, 1000
+FIRST_COST, SECOND_COST, DQ_COST, PACK_COST = 1000, 10000000000, 1000, 1000
 NT = (((1,), (1,)), ((), ()))
 NN = (((1,), (0,)), ((), ()))
 
@@ -144,7 +144,7 @@
     outs = {}
     for b in blocks:
         first = refs.pop(0)
-        outs[b] = (first.at[0], first.at[1]) if b >= 2 else (first, refs.pop(0))
+        outs[b] = (first.at[0], first.at[1]) if b == 2 else (first, refs.pop(0))
     live, k_cols, prob_all, grad_all = refs[-4:]
     scale = HEAD_DIM**-0.5
     odd = lax.axis_index("ctx") % 2
@@ -390,8 +390,6 @@
         k_own = pl.BlockSpec((rows, HEAD_DIM), at_mine)
         far = lambda i: pl.BlockSpec((None, rows, wide), lambda h, *_: (i, 0, h))
         kv_spec = pl.BlockSpec((2, rows, HEAD_DIM), lambda h, *_: (0, 0, first + h))
-        dq_spec = pl.BlockSpec((rows, wide), lambda h, *_: (0, h))
-        carry_spec = pl.BlockSpec((None, HEAD_DIM, 2 * group * TILE), lambda h, *_: (h, 0, 0))
         args = [queries, qg_far[part], out_grad, qg_far[part], small, qg_far[0]]
         specs = [
             q_own,
@@ -407,15 +405,15 @@
         dq_shapes = [queries.shape, (rows, kvs * wide)]
         outs = [pltpu.HBM(s, jnp.bfloat16) for s in dq_shapes]
         out_specs = [q_own, pl.BlockSpec((rows, wide), lambda h, *_: (0, h))]
-        both = lambda width, at: (
-            pltpu.HBM((2, 2, rows, width), jnp.bfloat16),
-            pl.BlockSpec((2, 2, rows, HEAD_DIM), lambda h, *_: (0, 0, 0, at + h)),
-        )
-        pairs = [(pltpu.HBM((2, rows, kv_width), jnp.float32), kv_spec)] * 4
-        pairs += [both(kv_width, first), both(kvs * HEAD_DIM, 0)]
-        for shape, spec in pairs:
-            outs.append(shape)
-            out_specs.append(spec)
+        kinds = (jnp.float32, jnp.float32, jnp.bfloat16, jnp.bfloat16)
+        both_spec = pl.BlockSpec((2, 2, rows, HEAD_DIM), lambda h, *_: (0, 0, 0, first + h))
+        for b in blocks:
+            if b == 2:
+                outs.append(pltpu.HBM((2, 2, rows, kv_width), kinds[b]))
+                out_specs.append(both_spec)
+            else:
+                outs += [pltpu.HBM((2, rows, kv_width), kinds[b])] * 2
+                out_specs += [kv_spec] * 2
         alias, n_args = {}, len(args)
         if before is not None:
             for i, array in enumerate(before):
@@ -461,25 +459,21 @@
         return sum(x.astype(jnp.float32) for x in terms).astype(jnp.bfloat16)
 
     blocks = (0, 1, 2, 3)
-    dq_near, dq_far, *sums, odd = attend(0, blocks, sources, None, FIRST_COST)
-    dq_first = swap(dq_far, "head")
-    odds = [routed(odd, one_or_three_on, backwards=True)]
-    results = attend(1, blocks, sources, (dq_near, *sums), SECOND_COST)
-    dq_near, dq_far, own_n, own_f, two_n, two_f, core, odd = results
-    core = swap(after(core, dq_first, odds[0]), "ctx")
-    odds.append(routed(odd, one_or_three_on, backwards=True))
+    dq_near, dq_far, *sums = attend(0, blocks, sources, None, FIRST_COST)
+    dq_before = dq_far
+    dq_near, dq_far, *sums = attend(1, blocks, sources, (dq_near, *sums), SECOND_COST)
+    own_n, own_f, two_n, two_f, core, odd_n, odd_f = sums
+    core = swap(core, "ctx")
+    dq_first = swap(after(dq_before, dq_far), "head")
+    far_odd = routed(odd_f, one_or_three_on, backwards=True)
     far_two = wide_sum(two_f, core[1])
-    two_n, dq_far = after((two_n, dq_far), far_two)
+    odd_n, two_n, dq_far = after((odd_n, two_n, dq_far), far_two)
     far_two = routed(far_two, two_on, backwards=True)
     dq_last = swap(dq_far, "head")
-    near_two = routed(wide_sum(two_n, core[0]), two_on, backwards=True)
-
-    def all_heads(tile):
-        return jnp.concatenate([odd[tile] for odd in odds], axis=-1)
-
-    far_total = wide_sum(own_f, all_heads(1), far_two)
-    far = swap(far_total, "head")
-    near = wide_sum(own_n, all_heads(0), after(near_two, far_total))
+    near_odd = routed(odd_n, one_or_three_on, backwards=True)
+    near_two = routed(wide_sum(after(two_n, dq_first), core[0]), two_on, backwards=True)
+    far = swap(wide_sum(own_f, far_odd, far_two), "head")
+    near = wide_sum(own_n, near_odd, near_two)
 
     def whole(near, far):
         return jnp.where(mine == 0, jnp.concatenate(near + far, -1), jnp.concatenate(far + near, -1))

time: 71.2 us -> 71.1 us (level)
  waiting for transfers between devices: 16.1 us -> 13.9 us
  other arithmetic: 1.23 us -> 2.37 us
  starting transfers between devices: 28.2 us -> 29 us
    ppermute x8, waiting for transfers between devices: 10.5 us -> 5.87 us  [routed(): return lax.ppermute(value, 'ctx', pairs)]
    ppermute x9, waiting for transfers between devices: 5.54 us -> 8 us  [swap(): lax.ppermute(value, axis, [(i, i ^ 1) for i in range(lax.axis_size(axis))])]
    convert_element_type x4, other arithmetic: 0.34 us -> 1.48 us  [wide_sum(): return sum((x.astype(jnp.float32) for x in terms)).astype(jnp.bfloat16)]
    unnamed x28 -> x30, local copies, waits for them, and re-layouts: 1.36 us -> 1.99 us
  transfers between devices with their start and end apart: 17 -> 17, of which waited for: 7 -> 8; matrix products, arithmetic and copies ran while one was open for 2% -> 3% of each run, Pallas kernels for 29% -> 17%
where the time goes in v4:
time: 71.1 us; the launch traced here: 70.1 us
  starting transfers between devices  29 us (41%)
  Pallas kernels  20.1 us (28%)
  waiting for transfers between devices  13.9 us (20%)
  local copies, waits for them, and re-layouts  3.95 us (6%)
  other arithmetic  2.37 us (3%)
  between operations  0.87 us (1%)
    ppermute x8, starting transfers between devices, routed(): return lax.ppermute(value, 'ctx', pairs)  18.5 us
    pallas_call x2, Pallas kernels, attend(): pl.pallas_call(functools.partial(pair_kernel, part, group, tile_pairs.sha...  15.9 us
    ppermute x9, starting transfers between devices, swap(): lax.ppermute(value, axis, [(i, i ^ 1) for i in range(lax.axis_size(axis))])  10.5 us
    ppermute x9, waiting for transfers between devices, swap(): lax.ppermute(value, axis, [(i, i ^ 1) for i in range(lax.axis_size(axis))])  8 us
    ppermute x8, waiting for transfers between devices, routed(): return lax.ppermute(value, 'ctx', pairs)  5.87 us
    pallas_call x1, Pallas kernels, by_pairs(): pl.pallas_call(functools.partial(pack_kernel, local_kv * group), out_shap...  2.24 us
    unnamed x30, local copies, waits for them, and re-layouts  1.99 us
    pallas_call x1, Pallas kernels, by_pairs(): pl.pallas_call(fill_kernel, out_shape=jax.ShapeDtypeStruct(queries.shape,...  1.91 us
  transfers between devices with their start and end apart: 17, of which 8 were waited for; matrix products, arithmetic and copies ran while one was open for 3% of the time, Pallas kernels for 17%

profile of v4, /device:TPU:0, one launch (start us, length us, event | category | flops | bytes accessed | tf_op | source)
XLA Modules:
  0.0 70.1 jit_solution(8179084649065606276)
XLA Ops:
  0.6 1.1 %dynamic-slice_bitcast_fusion = (bf16[1,128,512]{2,1,0:T(8,128)(2,1)S(1)}, bf16[1,128,512]{2,1,0:T(8,128)(2,1)S(1)}, bf16[1,128,512]{2,1,0:T(8,128)(2,1)S(1)}, bf16[1,128,512]{2,1,0:T(8,128)(2,1)S(1)}) fusion(bf16[128,1024]{1,0:T(8,128)(2,1)} %refs_10_.3, s32[]{:T(128)S(6)} %select_n.17, s32[]{:T(128)S(6)} %select_n.16, bf16[128,1024]{1,0:T(8,128)(2,1)} %refs_9_.3), kind=kLoop, calls=%fused_computation.13 | loop fusion | bytes 1048584 | tf_op jit(solution)/shard_map/stack | solution.py:358
  1.8 3.0 %collective-permute-start.1 = (bf16[2,128,512]{2,1,0:T(8,128)(2,1)S(1)}, bf16[2,128,512]{2,1,0:T(8,128)(2,1)}, u32[]{:S(2)}, u32[]{:S(2)}) collective-permute-start(bf16[2,128,512]{2,1,0:T(8,128)(2,1)S(1)} %pad_maximum_fusion), channel_id=1, source_target_pairs={{0,1},{1,0},{2,3},{3,2},{4,5},{5,4},{6,7},{7,6},{8,9},{9,8},{10,11... | collective-permute-start | bytes 786440 | tf_op jit(solution)/shard_map/ppermute | solution.py:29
  4.8 2.2 %pack_sends.1 = (bf16[2,144,1024]{2,1,0:T(8,128)(2,1)}, bf16[2,128,1024]{2,1,0:T(8,128)(2,1)}, f32[2,1,2048]{2,1,0:T(1,128)}) custom-call(s32[1]{0:T(128)} %bitcast.mine.refs_0_, bf16[128,4096]{1,0:T(8,128)(2,1)} %refs_3_.3, bf16[128,4096]{1,0:T(8,128)(2,1)} %refs_5_.3, f32[32,128]{1,0:T(8,128)} %bitcast.28, f32[32,128]{1,0:T(8,128)} %bitcast.29), custom_call_target="tpu_custom_call" | custom-call | flops 1000 | bytes 1 | tf_op jit(solution)/shard_map/pack_sends/pallas_call | solution.py:364
  7.8 4.0 %collective-permute-start.2 = (bf16[2,128,512]{2,1,0:T(8,128)(2,1)}, bf16[2,128,512]{2,1,0:T(8,128)(2,1)S(1)}, u32[]{:S(2)}, u32[]{:S(2)}) collective-permute-start(bf16[2,128,512]{2,1,0:T(8,128)(2,1)} %pad_maximum_fusion.1), channel_id=1, source_target_pairs={{0,4},{2,6},{4,8},{6,10},{8,12},{10,14},{12,16},{14,18},{16,20},{1... | collective-permute-start | bytes 786440 | tf_op jit(solution)/shard_map/ppermute | solution.py:37
  12.1 4.1 %collective-permute-start.3 = (bf16[2,128,512]{2,1,0:T(8,128)(2,1)}, bf16[2,128,512]{2,1,0:T(8,128)(2,1)S(1)}, u32[]{:S(2)}, u32[]{:S(2)}) collective-permute-start(bf16[2,128,512]{2,1,0:T(8,128)(2,1)} %arrived.1.refs_11_), channel_id=1, source_target_pairs={{0,4},{2,6},{4,8},{6,10},{8,12},{10,14},{12,16},{14,18},{16,20},{1... | collective-permute-start | bytes 786440 | tf_op jit(solution)/shard_map/ppermute | solution.py:37
  16.2 1.3 %collective-permute-start.5 = (bf16[2,128,512]{2,1,0:T(8,128)(2,1)}, bf16[2,128,512]{2,1,0:T(8,128)(2,1)S(1)}, u32[]{:S(2)}, u32[]{:S(2)}) collective-permute-start(bf16[2,128,512]{2,1,0:T(8,128)(2,1)} %pad_maximum_fusion.1), channel_id=1, source_target_pairs={{0,2},{2,8},{4,6},{6,12},{8,10},{10,16},{12,14},{14,20},{16,18},{1... | collective-permute-start | bytes 786440 | tf_op jit(solution)/shard_map/ppermute | solution.py:37
  17.5 1.6 %collective-permute-start.8 = (bf16[2,128,1024]{2,1,0:T(8,128)(2,1)}, bf16[2,128,1024]{2,1,0:T(8,128)(2,1)S(1)}, u32[]{:S(2)}, u32[]{:S(2)}) collective-permute-start(bf16[2,128,1024]{2,1,0:T(8,128)(2,1)} %get-tuple-element.36), channel_id=1, source_target_pairs={{0,1},{1,0},{2,3},{3,2},{4,5},{5,4},{6,7},{7,6},{8,9},{9,8},{10,11... | collective-permute-start | bytes 1572872 | tf_op jit(solution)/shard_map/ppermute | solution.py:29
  19.1 3.9 %collective-permute-start.7 = (bf16[2,128,512]{2,1,0:T(8,128)(2,1)}, bf16[2,128,512]{2,1,0:T(8,128)(2,1)S(1)}, u32[]{:S(2)}, u32[]{:S(2)}) collective-permute-start(bf16[2,128,512]{2,1,0:T(8,128)(2,1)} %arrived.1.refs_11_), channel_id=1, source_target_pairs={{0,2},{2,8},{4,6},{6,12},{8,10},{10,16},{12,14},{14,20},{16,18},{1... | collective-permute-start | bytes 786440 | tf_op jit(solution)/shard_map/ppermute | solution.py:37
  23.0 1.4 %collective-permute-start.4 = (bf16[2,128,512]{2,1,0:T(8,128)(2,1)S(1)}, bf16[2,128,512]{2,1,0:T(8,128)(2,1)S(1)}, u32[]{:S(2)}, u32[]{:S(2)}) collective-permute-start(bf16[2,128,512]{2,1,0:T(8,128)(2,1)S(1)} %collective-permute-done.2.refs_12_), channel_id=1, source_target_pairs={{0,2},{2,0},{4,6},{6,4},{8,10},{10,8},{12,14},{14,12},{16,18},{18,... | collective-permute-start | bytes 786440 | tf_op jit(solution)/shard_map/ppermute | solution.py:29
  24.5 1.1 %collective-permute-done.4.refs_14_ = bf16[2,128,512]{2,1,0:T(8,128)(2,1)S(1)} collective-permute-done((bf16[2,128,512]{2,1,0:T(8,128)(2,1)S(1)}, bf16[2,128,512]{2,1,0:T(8,128)(2,1)S(1)}, u32[]{:S(2)}, u32[]{:S(2)}) %collective-permute-start.4) | collective-permute-done | bytes 262176 | tf_op jit(solution)/shard_map/ppermute | solution.py:29
  26.6 7.9 %grads_0123_part0.1 = (bf16[128,4096]{1,0:T(8,128)(2,1)}, bf16[128,1024]{1,0:T(8,128)(2,1)}, f32[2,128,512]{2,1,0:T(8,128)}, f32[2,128,512]{2,1,0:T(8,128)}, f32...) custom-call(s32[1]{0:T(128)} %bitcast.mine.refs_0_, ...), custom_call_target="tpu_custom_call" | custom-call | flops 1000 | bytes 1 | tf_op jit(solution)/shard_map/grads_0123_part0/pallas_call | solution.py:424
  35.0 8.0 %grads_0123_part1.1 = (bf16[128,4096]{1,0:T(8,128)(2,1)}, bf16[128,1024]{1,0:T(8,128)(2,1)}, f32[2,128,512]{2,1,0:T(8,128)}, f32[2,128,512]{2,1,0:T(8,128)}, f32...) custom-call(s32[1]{0:T(128)} %bitcast.mine.refs_0_, ...), custom_call_target="tpu_custom_call", output_to_operand_aliasing={{0}: (18, {}), {2}: (19, {}), {3}: (20, {}), {4}: (21, {}),... | custom-call | flops 10000000000 | bytes 1 | tf_op jit(solution)/shard_map/grads_0123_part1/pallas_call | solution.py:424
  43.0 1.7 %collective-permute-start.10 = (bf16[2,2,128,512]{3,2,1,0:T(8,128)(2,1)}, bf16[2,2,128,512]{3,2,1,0:T(8,128)(2,1)S(1)}, u32[]{:S(2)}, u32[]{:S(2)}) collective-permute-start(bf16[2,2,128,512]{3,2,1,0:T(8,128)(2,1)} %get-tuple-element.50), channel_id=1, source_target_pairs={{0,2},{2,0},{4,6},{6,4},{8,10},{10,8},{12,14},{14,12},{16,18},{18,... | collective-permute-start | bytes 1572872 | tf_op jit(solution)/shard_map/ppermute | solution.py:29
  44.7 1.5 %collective-permute-start.9 = (bf16[128,1024]{1,0:T(8,128)(2,1)S(1)}, bf16[128,1024]{1,0:T(8,128)(2,1)S(1)}, u32[]{:S(2)}, u32[]{:S(2)}) collective-permute-start(bf16[128,1024]{1,0:T(8,128)(2,1)S(1)} %copy-done.13), channel_id=1, source_target_pairs={{0,1},{1,0},{2,3},{3,2},{4,5},{5,4},{6,7},{7,6},{8,9},{9,8},{10,11... | collective-permute-start | bytes 786440 | tf_op jit(solution)/shard_map/ppermute | solution.py:29
  46.3 1.3 %collective-permute-start.14 = (bf16[2,128,512]{2,1,0:T(8,128)(2,1)}, bf16[2,128,512]{2,1,0:T(8,128)(2,1)S(1)}, u32[]{:S(2)}, u32[]{:S(2)}) collective-permute-start(bf16[2,128,512]{2,1,0:T(8,128)(2,1)} %get-tuple-element.58), channel_id=1, source_target_pairs={{2,0},{8,2},{6,4},{12,6},{10,8},{16,10},{14,12},{20,14},{18,16},{2... | collective-permute-start | bytes 786440 | tf_op jit(solution)/shard_map/ppermute | solution.py:37
  47.6 1.2 %fusion.1 = bf16[2,128,512]{2,1,0:T(8,128)(2,1)S(1)} fusion(f32[2,128,512]{2,1,0:T(8,128)} %get-tuple-element.49, bf16[2,2,128,512]{3,2,1,0:T(8,128)(2,1)S(1)} %collective-permute-done.10), kind=kLoop, calls=%fused_computation.4 | loop fusion | flops 393216 | bytes 1048576 | tf_op jit(solution)/shard_map/convert_element_type | solution.py:459
  48.8 1.3 %collective-permute-start.15 = (bf16[2,128,512]{2,1,0:T(8,128)(2,1)S(1)}, bf16[2,128,512]{2,1,0:T(8,128)(2,1)S(1)}, u32[]{:S(2)}, u32[]{:S(2)}) collective-permute-start(bf16[2,128,512]{2,1,0:T(8,128)(2,1)S(1)} %fusion.1), channel_id=1, source_target_pairs={{4,0},{6,2},{8,4},{10,6},{12,8},{14,10},{16,12},{18,14},{20,16},{2... | collective-permute-start | bytes 786440 | tf_op jit(solution)/shard_map/ppermute | solution.py:37
  50.7 2.4 %collective-permute-done.9.first = bf16[128,1024]{1,0:T(8,128)(2,1)S(1)} collective-permute-done((bf16[128,1024]{1,0:T(8,128)(2,1)S(1)}, bf16[128,1024]{1,0:T(8,128)(2,1)S(1)}, u32[]{:S(2)}, u32[]{:S(2)}) %collective-permute-start.9) | collective-permute-done | bytes 262176 | tf_op jit(solution)/shard_map/ppermute | solution.py:29
  53.8 1.3 %collective-permute-start.13 = (bf16[2,128,512]{2,1,0:T(8,128)(2,1)S(1)}, bf16[2,128,512]{2,1,0:T(8,128)(2,1)S(1)}, u32[]{:S(2)}, u32[]{:S(2)}) collective-permute-start(bf16[2,128,512]{2,1,0:T(8,128)(2,1)S(1)} %fusion), channel_id=1, source_target_pairs={{4,0},{6,2},{8,4},{10,6},{12,8},{14,10},{16,12},{18,14},{20,16},{2... | collective-permute-start | bytes 786440 | tf_op jit(solution)/shard_map/ppermute | solution.py:37
  55.0 1.3 %collective-permute-start.12 = (bf16[2,128,512]{2,1,0:T(8,128)(2,1)S(1)}, bf16[2,128,512]{2,1,0:T(8,128)(2,1)S(1)}, u32[]{:S(2)}, u32[]{:S(2)}) collective-permute-start(bf16[2,128,512]{2,1,0:T(8,128)(2,1)S(1)} %copy-done.14), channel_id=1, source_target_pairs={{2,0},{8,2},{6,4},{12,6},{10,8},{16,10},{14,12},{20,14},{18,16},{2... | collective-permute-start | bytes 786440 | tf_op jit(solution)/shard_map/ppermute | solution.py:37
  56.4 3.5 %collective-permute-done.15 = bf16[2,128,512]{2,1,0:T(8,128)(2,1)S(1)} collective-permute-done((bf16[2,128,512]{2,1,0:T(8,128)(2,1)S(1)}, bf16[2,128,512]{2,1,0:T(8,128)(2,1)S(1)}, u32[]{:S(2)}, u32[]{:S(2)}) %collective-permute-start.15) | collective-permute-done | bytes 262176 | tf_op jit(solution)/shard_map/ppermute | solution.py:37
  61.3 1.9 %fill_in.1 = bf16[128,4096]{1,0:T(8,128)(2,1)} custom-call(s32[1]{0:T(128)} %bitcast.mine.refs_0_, bf16[128,1024]{1,0:T(8,128)(2,1)} %copy-done.10, bf16[128,1024]{1,0:T(8,128)(2,1)} %copy-done.11, bf16[128,4096]{1,0:T(8,128)(2,1)} %get-tuple-element.52.before), custom_call_target="tpu_custom_call", output_to_operand_aliasing={{}: (3, {})} | custom-call | flops 1000 | bytes 1 | tf_op jit(solution)/shard_map/fill_in/pallas_call | solution.py:483
  63.2 2.3 %collective-permute-done.13 = bf16[2,128,512]{2,1,0:T(8,128)(2,1)S(1)} collective-permute-done((bf16[2,128,512]{2,1,0:T(8,128)(2,1)S(1)}, bf16[2,128,512]{2,1,0:T(8,128)(2,1)S(1)}, u32[]{:S(2)}, u32[]{:S(2)}) %collective-permute-start.13) | collective-permute-done | bytes 262176 | tf_op jit(solution)/shard_map/ppermute | solution.py:37
  65.6 3.5 %collective-permute-done.16 = bf16[2,128,512]{2,1,0:T(8,128)(2,1)S(1)} collective-permute-done((bf16[2,128,512]{2,1,0:T(8,128)(2,1)S(1)}, bf16[2,128,512]{2,1,0:T(8,128)(2,1)S(1)}, u32[]{:S(2)}, u32[]{:S(2)}) %collective-permute-start.16) | collective-permute-done | bytes 262176 | tf_op jit(solution)/shard_map/ppermute | solution.py:29
  (54 shorter events, 6.3 us)
Async XLA Ops:
  1.8 10.3 %collective-permute-start.1 = (bf16[2,128,512]{2,1,0:T(8,128)(2,1)S(1)}, bf16[2,128,512]{2,1,0:T(8,128)(2,1)}, u32[]{:S(2)}, u32[]{:S(2)}) collective-permute-start(bf16[2,128,512]{2,1,0:T(8,128)(2,1)S(1)} %pad_maximum_fusion), channel_id=1, source_target_pairs={{0,1},{1,0},{2,3},{3,2},{4,5},{5,4},{6,7},{7,6},{8,9},{9,8},{10,11... | collective-permute-start | bytes 786440 | tf_op jit(solution)/shard_map/ppermute | solution.py:29
  7.1 18.5 %collective-permute-start = (bf16[2,144,1024]{2,1,0:T(8,128)(2,1)}, bf16[2,144,1024]{2,1,0:T(8,128)(2,1)S(1)}, u32[]{:S(2)}, u32[]{:S(2)}) collective-permute-start(bf16[2,144,1024]{2,1,0:T(8,128)(2,1)} %get-tuple-element.31), channel_id=1, source_target_pairs={{0,1},{1,0},{2,3},{3,2},{4,5},{5,4},{6,7},{7,6},{8,9},{9,8},{10,11... | collective-permute-start | bytes 1769480 | tf_op jit(solution)/shard_map/ppermute | solution.py:29
  7.8 18.1 %copy-start = (bf16[128,4096]{1,0:T(8,128)(2,1)S(1)}, bf16[128,4096]{1,0:T(8,128)(2,1)}, u32[]{:S(2)}) copy-start(bf16[128,4096]{1,0:T(8,128)(2,1)} %refs_3_.3) | copy-start | bytes 3145732
  7.8 18.1 %copy-start.1 = (bf16[128,4096]{1,0:T(8,128)(2,1)S(1)}, bf16[128,4096]{1,0:T(8,128)(2,1)}, u32[]{:S(2)}) copy-start(bf16[128,4096]{1,0:T(8,128)(2,1)} %refs_5_.3) | copy-start | bytes 3145732
  7.8 18.1 %copy-start.2 = (bf16[128,1024]{1,0:T(8,128)(2,1)S(1)}, bf16[128,1024]{1,0:T(8,128)(2,1)}, u32[]{:S(2)}) copy-start(bf16[128,1024]{1,0:T(8,128)(2,1)} %refs_9_.3) | copy-start | bytes 786436
  7.8 18.1 %copy-start.3 = (bf16[128,1024]{1,0:T(8,128)(2,1)S(1)}, bf16[128,1024]{1,0:T(8,128)(2,1)}, u32[]{:S(2)}) copy-start(bf16[128,1024]{1,0:T(8,128)(2,1)} %refs_10_.3) | copy-start | bytes 786436
  7.8 11.2 %collective-permute-start.2 = (bf16[2,128,512]{2,1,0:T(8,128)(2,1)}, bf16[2,128,512]{2,1,0:T(8,128)(2,1)S(1)}, u32[]{:S(2)}, u32[]{:S(2)}) collective-permute-start(bf16[2,128,512]{2,1,0:T(8,128)(2,1)} %pad_maximum_fusion.1), channel_id=1, source_target_pairs={{0,4},{2,6},{4,8},{6,10},{8,12},{10,14},{12,16},{14,18},{16,20},{1... | collective-permute-start | bytes 786440 | tf_op jit(solution)/shard_map/ppermute | solution.py:37
  12.1 13.9 %copy-start.4 = (f32[2,1,2048]{2,1,0:T(1,128)S(1)}, f32[2,1,2048]{2,1,0:T(1,128)}, u32[]{:S(2)}) copy-start(f32[2,1,2048]{2,1,0:T(1,128)} %get-tuple-element.32.refs_7_) | copy-start | bytes 49156
  12.1 13.9 %copy-start.5 = (s32[1,4,4,2]{2,3,1,0:T(2,128)S(1)}, s32[1,4,4,2]{2,3,1,0:T(2,128)}, u32[]{:S(2)}) copy-start(s32[1,4,4,2]{2,3,1,0:T(2,128)} %param.14) | copy-start | bytes 388
  12.1 10.9 %collective-permute-start.3 = (bf16[2,128,512]{2,1,0:T(8,128)(2,1)}, bf16[2,128,512]{2,1,0:T(8,128)(2,1)S(1)}, u32[]{:S(2)}, u32[]{:S(2)}) collective-permute-start(bf16[2,128,512]{2,1,0:T(8,128)(2,1)} %arrived.1.refs_11_), channel_id=1, source_target_pairs={{0,4},{2,6},{4,8},{6,10},{8,12},{10,14},{12,16},{14,18},{16,20},{1... | collective-permute-start | bytes 786440 | tf_op jit(solution)/shard_map/ppermute | solution.py:37
  16.2 8.2 %collective-permute-start.5 = (bf16[2,128,512]{2,1,0:T(8,128)(2,1)}, bf16[2,128,512]{2,1,0:T(8,128)(2,1)S(1)}, u32[]{:S(2)}, u32[]{:S(2)}) collective-permute-start(bf16[2,128,512]{2,1,0:T(8,128)(2,1)} %pad_maximum_fusion.1), channel_id=1, source_target_pairs={{0,2},{2,8},{4,6},{6,12},{8,10},{10,16},{12,14},{14,20},{16,18},{1... | collective-permute-start | bytes 786440 | tf_op jit(solution)/shard_map/ppermute | solution.py:37
  17.5 17.5 %collective-permute-start.8 = (bf16[2,128,1024]{2,1,0:T(8,128)(2,1)}, bf16[2,128,1024]{2,1,0:T(8,128)(2,1)S(1)}, u32[]{:S(2)}, u32[]{:S(2)}) collective-permute-start(bf16[2,128,1024]{2,1,0:T(8,128)(2,1)} %get-tuple-element.36), channel_id=1, source_target_pairs={{0,1},{1,0},{2,3},{3,2},{4,5},{5,4},{6,7},{7,6},{8,9},{9,8},{10,11... | collective-permute-start | bytes 1572872 | tf_op jit(solution)/shard_map/ppermute | solution.py:29
  19.1 6.5 %collective-permute-start.7 = (bf16[2,128,512]{2,1,0:T(8,128)(2,1)}, bf16[2,128,512]{2,1,0:T(8,128)(2,1)S(1)}, u32[]{:S(2)}, u32[]{:S(2)}) collective-permute-start(bf16[2,128,512]{2,1,0:T(8,128)(2,1)} %arrived.1.refs_11_), channel_id=1, source_target_pairs={{0,2},{2,8},{4,6},{6,12},{8,10},{10,16},{12,14},{14,20},{16,18},{1... | collective-permute-start | bytes 786440 | tf_op jit(solution)/shard_map/ppermute | solution.py:37
  23.0 2.5 %collective-permute-start.4 = (bf16[2,128,512]{2,1,0:T(8,128)(2,1)S(1)}, bf16[2,128,512]{2,1,0:T(8,128)(2,1)S(1)}, u32[]{:S(2)}, u32[]{:S(2)}) collective-permute-start(bf16[2,128,512]{2,1,0:T(8,128)(2,1)S(1)} %collective-permute-done.2.refs_12_), channel_id=1, source_target_pairs={{0,2},{2,0},{4,6},{6,4},{8,10},{10,8},{12,14},{14,12},{16,18},{18,... | collective-permute-start | bytes 786440 | tf_op jit(solution)/shard_map/ppermute | solution.py:29
  24.4 1.5 %collective-permute-start.6 = (bf16[2,128,512]{2,1,0:T(8,128)(2,1)S(1)}, bf16[2,128,512]{2,1,0:T(8,128)(2,1)S(1)}, u32[]{:S(2)}, u32[]{:S(2)}) collective-permute-start(bf16[2,128,512]{2,1,0:T(8,128)(2,1)S(1)} %collective-permute-done.3.refs_13_), channel_id=1, source_target_pairs={{0,2},{2,0},{4,6},{6,4},{8,10},{10,8},{12,14},{14,12},{16,18},{18,... | collective-permute-start | bytes 786440 | tf_op jit(solution)/shard_map/ppermute | solution.py:29
  43.0 4.6 %collective-permute-start.10 = (bf16[2,2,128,512]{3,2,1,0:T(8,128)(2,1)}, bf16[2,2,128,512]{3,2,1,0:T(8,128)(2,1)S(1)}, u32[]{:S(2)}, u32[]{:S(2)}) collective-permute-start(bf16[2,2,128,512]{3,2,1,0:T(8,128)(2,1)} %get-tuple-element.50), channel_id=1, source_target_pairs={{0,2},{2,0},{4,6},{6,4},{8,10},{10,8},{12,14},{14,12},{16,18},{18,... | collective-permute-start | bytes 1572872 | tf_op jit(solution)/shard_map/ppermute | solution.py:29
  44.7 8.3 %collective-permute-start.9 = (bf16[128,1024]{1,0:T(8,128)(2,1)S(1)}, bf16[128,1024]{1,0:T(8,128)(2,1)S(1)}, u32[]{:S(2)}, u32[]{:S(2)}) collective-permute-start(bf16[128,1024]{1,0:T(8,128)(2,1)S(1)} %copy-done.13), channel_id=1, source_target_pairs={{0,1},{1,0},{2,3},{3,2},{4,5},{5,4},{6,7},{7,6},{8,9},{9,8},{10,11... | collective-permute-start | bytes 786440 | tf_op jit(solution)/shard_map/ppermute | solution.py:29
  46.3 10.1 %collective-permute-start.14 = (bf16[2,128,512]{2,1,0:T(8,128)(2,1)}, bf16[2,128,512]{2,1,0:T(8,128)(2,1)S(1)}, u32[]{:S(2)}, u32[]{:S(2)}) collective-permute-start(bf16[2,128,512]{2,1,0:T(8,128)(2,1)} %get-tuple-element.58), channel_id=1, source_target_pairs={{2,0},{8,2},{6,4},{12,6},{10,8},{16,10},{14,12},{20,14},{18,16},{2... | collective-permute-start | bytes 786440 | tf_op jit(solution)/shard_map/ppermute | solution.py:37
  48.8 11.1 %collective-permute-start.15 = (bf16[2,128,512]{2,1,0:T(8,128)(2,1)S(1)}, bf16[2,128,512]{2,1,0:T(8,128)(2,1)S(1)}, u32[]{:S(2)}, u32[]{:S(2)}) collective-permute-start(bf16[2,128,512]{2,1,0:T(8,128)(2,1)S(1)} %fusion.1), channel_id=1, source_target_pairs={{4,0},{6,2},{8,4},{10,6},{12,8},{14,10},{16,12},{18,14},{20,16},{2... | collective-permute-start | bytes 786440 | tf_op jit(solution)/shard_map/ppermute | solution.py:37
  50.1 9.8 %copy-start.8 = (f32[2,128,512]{2,1,0:T(8,128)S(1)}, f32[2,128,512]{2,1,0:T(8,128)}, u32[]{:S(2)}) copy-start(f32[2,128,512]{2,1,0:T(8,128)} %get-tuple-element.57) | copy-start | bytes 1572868
  50.1 10.5 %collective-permute-start.11 = (bf16[128,1024]{1,0:T(8,128)(2,1)S(1)}, bf16[128,1024]{1,0:T(8,128)(2,1)S(1)}, u32[]{:S(2)}, u32[]{:S(2)}) collective-permute-start(bf16[128,1024]{1,0:T(8,128)(2,1)S(1)} %copy-done.12), channel_id=1, source_target_pairs={{0,1},{1,0},{2,3},{3,2},{4,5},{5,4},{6,7},{7,6},{8,9},{9,8},{10,11... | collective-permute-start | bytes 786440 | tf_op jit(solution)/shard_map/ppermute | solution.py:29
  53.8 11.8 %collective-permute-start.13 = (bf16[2,128,512]{2,1,0:T(8,128)(2,1)S(1)}, bf16[2,128,512]{2,1,0:T(8,128)(2,1)S(1)}, u32[]{:S(2)}, u32[]{:S(2)}) collective-permute-start(bf16[2,128,512]{2,1,0:T(8,128)(2,1)S(1)} %fusion), channel_id=1, source_target_pairs={{4,0},{6,2},{8,4},{10,6},{12,8},{14,10},{16,12},{18,14},{20,16},{2... | collective-permute-start | bytes 786440 | tf_op jit(solution)/shard_map/ppermute | solution.py:37
  55.0 10.5 %collective-permute-start.12 = (bf16[2,128,512]{2,1,0:T(8,128)(2,1)S(1)}, bf16[2,128,512]{2,1,0:T(8,128)(2,1)S(1)}, u32[]{:S(2)}, u32[]{:S(2)}) collective-permute-start(bf16[2,128,512]{2,1,0:T(8,128)(2,1)S(1)} %copy-done.14), channel_id=1, source_target_pairs={{2,0},{8,2},{6,4},{12,6},{10,8},{16,10},{14,12},{20,14},{18,16},{2... | collective-permute-start | bytes 786440 | tf_op jit(solution)/shard_map/ppermute | solution.py:37
  60.0 9.1 %collective-permute-start.16 = (bf16[2,128,512]{2,1,0:T(8,128)(2,1)S(1)}, bf16[2,128,512]{2,1,0:T(8,128)(2,1)S(1)}, u32[]{:S(2)}, u32[]{:S(2)}) collective-permute-start(bf16[2,128,512]{2,1,0:T(8,128)(2,1)S(1)} %add_convert_fusion), channel_id=1, source_target_pairs={{0,1},{1,0},{2,3},{3,2},{4,5},{5,4},{6,7},{7,6},{8,9},{9,8},{10,11... | collective-permute-start | bytes 786440 | tf_op jit(solution)/shard_map/ppermute | solution.py:29
  (8 other events, 28.9 us)

commit v5 on v4

--- a/solution.py
+++ b/solution.py
@@ -313,10 +313,8 @@
             parts[0][i, tile:, at * tile : (at + 1) * tile] = block
 
 
-def fill_kernel(mine, first, last, before, half):
-    size = first.shape[1]
-    half[:, :size] = first[...]
-    half[:, size:] = last[...]
+def fill_kernel(mine, got, before, half):
+    half[...] = got[...]
 
 
 def after(value, *before):
@@ -402,9 +400,9 @@
         for b in blocks:
             args += sources[b]
             specs += [k_own, k_own, kv_spec] if b == 0 else [kv_spec, kv_spec]
-        dq_shapes = [queries.shape, (rows, kvs * wide)]
+        dq_shapes = [queries.shape, (rows, width)]
         outs = [pltpu.HBM(s, jnp.bfloat16) for s in dq_shapes]
-        out_specs = [q_own, pl.BlockSpec((rows, wide), lambda h, *_: (0, h))]
+        out_specs = [q_own, pl.BlockSpec((rows, wide), lambda h, *_: (0, first + h))]
         kinds = (jnp.float32, jnp.float32, jnp.bfloat16, jnp.bfloat16)
         both_spec = pl.BlockSpec((2, 2, rows, HEAD_DIM), lambda h, *_: (0, 0, 0, first + h))
         for b in blocks:
@@ -417,7 +415,7 @@
         alias, n_args = {}, len(args)
         if before is not None:
             for i, array in enumerate(before):
-                alias[len(lists) + len(args)] = i if i == 0 else i + 1
+                alias[len(lists) + len(args)] = i
                 args.append(array)
         specs += [pl.BlockSpec(memory_space=pl.ANY)] * (len(args) - n_args)
         keys_all = len(blocks) * 2 * TILE
@@ -459,20 +457,18 @@
         return sum(x.astype(jnp.float32) for x in terms).astype(jnp.bfloat16)
 
     blocks = (0, 1, 2, 3)
-    dq_near, dq_far, *sums = attend(0, blocks, sources, None, FIRST_COST)
-    dq_before = dq_far
-    dq_near, dq_far, *sums = attend(1, blocks, sources, (dq_near, *sums), SECOND_COST)
+    first = attend(0, blocks, sources, None, FIRST_COST)
+    dq_near, dq_far, *sums = attend(1, blocks, sources, first, SECOND_COST)
     own_n, own_f, two_n, two_f, core, odd_n, odd_f = sums
     core = swap(core, "ctx")
-    dq_first = swap(after(dq_before, dq_far), "head")
+    dq_far = swap(dq_far, "head")
     far_odd = routed(odd_f, one_or_three_on, backwards=True)
     far_two = wide_sum(two_f, core[1])
-    odd_n, two_n, dq_far = after((odd_n, two_n, dq_far), far_two)
+    odd_n, two_n = after((odd_n, two_n), far_two)
     far_two = routed(far_two, two_on, backwards=True)
-    dq_last = swap(dq_far, "head")
     near_odd = routed(odd_n, one_or_three_on, backwards=True)
-    near_two = routed(wide_sum(after(two_n, dq_first), core[0]), two_on, backwards=True)
-    far = swap(wide_sum(own_f, far_odd, far_two), "head")
+    near_two = routed(wide_sum(two_n, core[0]), two_on, backwards=True)
+    far = swap(wide_sum(after(own_f, dq_far), far_odd, far_two), "head")
     near = wide_sum(own_n, near_odd, near_two)
 
     def whole(near, far):
@@ -486,15 +482,15 @@
         grid_spec=pltpu.PrefetchScalarGridSpec(
             num_scalar_prefetch=1,
             grid=(1,),
-            in_specs=[pl.BlockSpec(dq_first.shape, lambda i, mine: (0, 0))] * PARTS
+            in_specs=[pl.BlockSpec((rows, width), lambda i, mine: (0, 0))]
             + [pl.BlockSpec(memory_space=pl.ANY)],
             out_specs=half,
         ),
-        input_output_aliases={3: 0},
+        input_output_aliases={2: 0},
         compiler_params=pltpu.CompilerParams(vmem_limit_bytes=SMALL_LIMIT),
         cost_estimate=pl.CostEstimate(flops=DQ_COST, bytes_accessed=1, transcendentals=0),
         name="fill_in",
-    )(lists[0], dq_first, dq_last, dq_near)
+    )(lists[0], dq_far, dq_near)
     return dq, both[0], both[1]
 
 

time: 71.1 us -> 70.2 us (0.987)
  starting transfers between devices: 29 us -> 25.4 us
  waiting for transfers between devices: 13.9 us -> 17.5 us
    ppermute x9 -> x8, waiting for transfers between devices: 8 us -> 15.3 us  [swap(): lax.ppermute(value, axis, [(i, i ^ 1) for i in range(lax.axis_size(axis))])]
    ppermute x8, waiting for transfers between devices: 5.87 us -> 2.18 us  [routed(): return lax.ppermute(value, 'ctx', pairs)]
    ppermute x9 -> x8, starting transfers between devices: 10.5 us -> 8.18 us  [swap(): lax.ppermute(value, axis, [(i, i ^ 1) for i in range(lax.axis_size(axis))])]
    ppermute x8, starting transfers between devices: 18.5 us -> 17.2 us  [routed(): return lax.ppermute(value, 'ctx', pairs)]
    unnamed x30 -> x24, local copies, waits for them, and re-layouts: 1.99 us -> 1.32 us
  transfers between devices with their start and end apart: 17 -> 16, of which waited for: 8 -> 6; matrix products, arithmetic and copies ran while one was open for 3% -> 3% of each run, Pallas kernels for 17% -> 17%
where the time goes in v5:
time: 70.2 us; the launch traced here: 69.5 us
  starting transfers between devices  25.4 us (36%)
  Pallas kernels  20 us (28%)
  waiting for transfers between devices  17.5 us (25%)
  local copies, waits for them, and re-layouts  3.28 us (5%)
  other arithmetic  2.36 us (3%)
  between operations  0.88 us (1%)
    ppermute x8, starting transfers between devices, routed(): return lax.ppermute(value, 'ctx', pairs)  17.2 us
    pallas_call x2, Pallas kernels, attend(): pl.pallas_call(functools.partial(pair_kernel, part, group, tile_pairs.sha...  15.9 us
    ppermute x8, waiting for transfers between devices, swap(): lax.ppermute(value, axis, [(i, i ^ 1) for i in range(lax.axis_size(axis))])  15.3 us
    ppermute x8, starting transfers between devices, swap(): lax.ppermute(value, axis, [(i, i ^ 1) for i in range(lax.axis_size(axis))])  8.18 us
    pallas_call x1, Pallas kernels, by_pairs(): pl.pallas_call(functools.partial(pack_kernel, local_kv * group), out_shap...  2.24 us
    ppermute x8, waiting for transfers between devices, routed(): return lax.ppermute(value, 'ctx', pairs)  2.18 us
    pallas_call x1, Pallas kernels, by_pairs(): pl.pallas_call(fill_kernel, out_shape=jax.ShapeDtypeStruct(queries.shape,...  1.93 us
    convert_element_type x4, other arithmetic, wide_sum(): return sum((x.astype(jnp.float32) for x in terms)).astype(jnp.bfloat16)  1.47 us
  transfers between devices with their start and end apart: 16, of which 6 were waited for; matrix products, arithmetic and copies ran while one was open for 3% of the time, Pallas kernels for 17%

profile of v5, /device:TPU:0, one launch (start us, length us, event | category | flops | bytes accessed | tf_op | source)
XLA Modules:
  0.0 69.5 jit_solution(11554223449473812704)
XLA Ops:
  0.6 1.1 %dynamic-slice_bitcast_fusion = (bf16[1,128,512]{2,1,0:T(8,128)(2,1)S(1)}, bf16[1,128,512]{2,1,0:T(8,128)(2,1)S(1)}, bf16[1,128,512]{2,1,0:T(8,128)(2,1)S(1)}, bf16[1,128,512]{2,1,0:T(8,128)(2,1)S(1)}) fusion(bf16[128,1024]{1,0:T(8,128)(2,1)} %refs_10_.3, s32[]{:T(128)S(6)} %select_n.17, s32[]{:T(128)S(6)} %select_n.16, bf16[128,1024]{1,0:T(8,128)(2,1)} %refs_9_.3), kind=kLoop, calls=%fused_computation.13 | loop fusion | bytes 1048584 | tf_op jit(solution)/shard_map/stack | solution.py:356
  1.8 3.0 %collective-permute-start.2 = (bf16[2,128,512]{2,1,0:T(8,128)(2,1)S(1)}, bf16[2,128,512]{2,1,0:T(8,128)(2,1)}, u32[]{:S(2)}, u32[]{:S(2)}) collective-permute-start(bf16[2,128,512]{2,1,0:T(8,128)(2,1)S(1)} %pad_maximum_fusion), channel_id=1, source_target_pairs={{0,1},{1,0},{2,3},{3,2},{4,5},{5,4},{6,7},{7,6},{8,9},{9,8},{10,11... | collective-permute-start | bytes 786440 | tf_op jit(solution)/shard_map/ppermute | solution.py:29
  4.8 0.7 %pad_maximum_fusion.1 = bf16[2,128,512]{2,1,0:T(8,128)(2,1)} fusion(bf16[1,128,512]{2,1,0:T(8,128)(2,1)S(1)} %get-tuple-element.59, bf16[1,128,512]{2,1,0:T(8,128)(2,1)S(1)} %get-tuple-element.62), kind=kLoop, calls=%fused_computation.12 | loop fusion | flops 131072 | bytes 524288 | tf_op jit(solution)/shard_map/stack | solution.py:356
  5.6 3.4 %collective-permute-start.3 = (bf16[2,128,512]{2,1,0:T(8,128)(2,1)}, bf16[2,128,512]{2,1,0:T(8,128)(2,1)S(1)}, u32[]{:S(2)}, u32[]{:S(2)}) collective-permute-start(bf16[2,128,512]{2,1,0:T(8,128)(2,1)} %pad_maximum_fusion.1), channel_id=1, source_target_pairs={{0,4},{2,6},{4,8},{6,10},{8,12},{10,14},{12,16},{14,18},{16,20},{1... | collective-permute-start | bytes 786440 | tf_op jit(solution)/shard_map/ppermute | solution.py:37
  9.0 2.2 %pack_sends.1 = (bf16[2,144,1024]{2,1,0:T(8,128)(2,1)}, bf16[2,128,1024]{2,1,0:T(8,128)(2,1)}, f32[2,1,2048]{2,1,0:T(1,128)}) custom-call(s32[1]{0:T(128)} %bitcast.mine.refs_0_, bf16[128,4096]{1,0:T(8,128)(2,1)} %refs_3_.3, bf16[128,4096]{1,0:T(8,128)(2,1)} %refs_5_.3, f32[32,128]{1,0:T(8,128)} %bitcast.28, f32[32,128]{1,0:T(8,128)} %bitcast.29), custom_call_target="tpu_custom_call" | custom-call | flops 1000 | bytes 1 | tf_op jit(solution)/shard_map/pack_sends/pallas_call | solution.py:362
  11.8 1.4 %collective-permute-start.6 = (bf16[2,128,512]{2,1,0:T(8,128)(2,1)}, bf16[2,128,512]{2,1,0:T(8,128)(2,1)S(1)}, u32[]{:S(2)}, u32[]{:S(2)}) collective-permute-start(bf16[2,128,512]{2,1,0:T(8,128)(2,1)} %pad_maximum_fusion.1), channel_id=1, source_target_pairs={{0,2},{2,8},{4,6},{6,12},{8,10},{10,16},{12,14},{14,20},{16,18},{1... | collective-permute-start | bytes 786440 | tf_op jit(solution)/shard_map/ppermute | solution.py:37
  13.3 3.5 %collective-permute-start.4 = (bf16[2,128,512]{2,1,0:T(8,128)(2,1)}, bf16[2,128,512]{2,1,0:T(8,128)(2,1)S(1)}, u32[]{:S(2)}, u32[]{:S(2)}) collective-permute-start(bf16[2,128,512]{2,1,0:T(8,128)(2,1)} %arrived.1.refs_11_), channel_id=1, source_target_pairs={{0,4},{2,6},{4,8},{6,10},{8,12},{10,14},{12,16},{14,18},{16,20},{1... | collective-permute-start | bytes 786440 | tf_op jit(solution)/shard_map/ppermute | solution.py:37
  16.7 1.6 %collective-permute-start = (bf16[2,128,1024]{2,1,0:T(8,128)(2,1)}, bf16[2,128,1024]{2,1,0:T(8,128)(2,1)S(1)}, u32[]{:S(2)}, u32[]{:S(2)}) collective-permute-start(bf16[2,128,1024]{2,1,0:T(8,128)(2,1)} %get-tuple-element.29), channel_id=1, source_target_pairs={{0,1},{1,0},{2,3},{3,2},{4,5},{5,4},{6,7},{7,6},{8,9},{9,8},{10,11... | collective-permute-start | bytes 1572872 | tf_op jit(solution)/shard_map/ppermute | solution.py:29
  18.3 3.6 %collective-permute-start.8 = (bf16[2,128,512]{2,1,0:T(8,128)(2,1)}, bf16[2,128,512]{2,1,0:T(8,128)(2,1)S(1)}, u32[]{:S(2)}, u32[]{:S(2)}) collective-permute-start(bf16[2,128,512]{2,1,0:T(8,128)(2,1)} %arrived.1.refs_11_), channel_id=1, source_target_pairs={{0,2},{2,8},{4,6},{6,12},{8,10},{10,16},{12,14},{14,20},{16,18},{1... | collective-permute-start | bytes 786440 | tf_op jit(solution)/shard_map/ppermute | solution.py:37
  22.6 1.2 %collective-permute-start.7 = (bf16[2,128,512]{2,1,0:T(8,128)(2,1)S(1)}, bf16[2,128,512]{2,1,0:T(8,128)(2,1)S(1)}, u32[]{:S(2)}, u32[]{:S(2)}) collective-permute-start(bf16[2,128,512]{2,1,0:T(8,128)(2,1)S(1)} %collective-permute-done.4.refs_13_), channel_id=1, source_target_pairs={{0,2},{2,0},{4,6},{6,4},{8,10},{10,8},{12,14},{14,12},{16,18},{18,... | collective-permute-start | bytes 786440 | tf_op jit(solution)/shard_map/ppermute | solution.py:29
  23.8 3.9 %collective-permute-done.1.refs_4_.refs_6_.refs_8_ = bf16[2,144,1024]{2,1,0:T(8,128)(2,1)S(1)} collective-permute-done((bf16[2,144,1024]{2,1,0:T(8,128)(2,1)}, bf16[2,144,1024]{2,1,0:T(8,128)(2,1)S(1)}, u32[]{:S(2)}, u32[]{:S(2)}) %collective-permute-start.1) | collective-permute-done | bytes 589856 | tf_op jit(solution)/shard_map/ppermute | solution.py:29
  28.4 7.9 %grads_0123_part0.1 = (bf16[128,4096]{1,0:T(8,128)(2,1)}, bf16[128,2048]{1,0:T(8,128)(2,1)}, f32[2,128,512]{2,1,0:T(8,128)}, f32[2,128,512]{2,1,0:T(8,128)}, f32...) custom-call(s32[1]{0:T(128)} %bitcast.mine.refs_0_, ...), custom_call_target="tpu_custom_call" | custom-call | flops 1000 | bytes 1 | tf_op jit(solution)/shard_map/grads_0123_part0/pallas_call | solution.py:422
  36.4 0.9 %collective-permute-done.refs_4_.refs_6_ = bf16[2,128,1024]{2,1,0:T(8,128)(2,1)S(1)} collective-permute-done((bf16[2,128,1024]{2,1,0:T(8,128)(2,1)}, bf16[2,128,1024]{2,1,0:T(8,128)(2,1)S(1)}, u32[]{:S(2)}, u32[]{:S(2)}) %collective-permute-start) | collective-permute-done | bytes 524320 | tf_op jit(solution)/shard_map/ppermute | solution.py:29
  37.3 7.9 %grads_0123_part1.1 = (bf16[128,4096]{1,0:T(8,128)(2,1)}, bf16[128,2048]{1,0:T(8,128)(2,1)}, f32[2,128,512]{2,1,0:T(8,128)}, f32[2,128,512]{2,1,0:T(8,128)}, f32...) custom-call(s32[1]{0:T(128)} %bitcast.mine.refs_0_, ...), custom_call_target="tpu_custom_call", output_to_operand_aliasing={{0}: (18, {}), {1}: (19, {}), {2}: (20, {}), {3}: (21, {}),... | custom-call | flops 10000000000 | bytes 1 | tf_op jit(solution)/shard_map/grads_0123_part1/pallas_call | solution.py:422
  45.9 1.3 %collective-permute-start.13 = (bf16[2,128,512]{2,1,0:T(8,128)(2,1)}, bf16[2,128,512]{2,1,0:T(8,128)(2,1)S(1)}, u32[]{:S(2)}, u32[]{:S(2)}) collective-permute-start(bf16[2,128,512]{2,1,0:T(8,128)(2,1)} %get-tuple-element.54), channel_id=1, source_target_pairs={{2,0},{8,2},{6,4},{12,6},{10,8},{16,10},{14,12},{20,14},{18,16},{2... | collective-permute-start | bytes 786440 | tf_op jit(solution)/shard_map/ppermute | solution.py:37
  47.4 1.2 %fusion.1 = bf16[2,128,512]{2,1,0:T(8,128)(2,1)S(1)} fusion(f32[2,128,512]{2,1,0:T(8,128)} %get-tuple-element.48, bf16[2,2,128,512]{3,2,1,0:T(8,128)(2,1)S(1)} %collective-permute-done.10), kind=kLoop, calls=%fused_computation.4 | loop fusion | flops 393216 | bytes 1048576 | tf_op jit(solution)/shard_map/convert_element_type | solution.py:457
  48.6 1.3 %collective-permute-start.14 = (bf16[2,128,512]{2,1,0:T(8,128)(2,1)S(1)}, bf16[2,128,512]{2,1,0:T(8,128)(2,1)S(1)}, u32[]{:S(2)}, u32[]{:S(2)}) collective-permute-start(bf16[2,128,512]{2,1,0:T(8,128)(2,1)S(1)} %fusion.1), channel_id=1, source_target_pairs={{4,0},{6,2},{8,4},{10,6},{12,8},{14,10},{16,12},{18,14},{20,16},{2... | collective-permute-start | bytes 786440 | tf_op jit(solution)/shard_map/ppermute | solution.py:37
  50.0 1.4 %collective-permute-start.12 = (bf16[2,128,512]{2,1,0:T(8,128)(2,1)S(1)}, bf16[2,128,512]{2,1,0:T(8,128)(2,1)S(1)}, u32[]{:S(2)}, u32[]{:S(2)}) collective-permute-start(bf16[2,128,512]{2,1,0:T(8,128)(2,1)S(1)} %fusion), channel_id=1, source_target_pairs={{4,0},{6,2},{8,4},{10,6},{12,8},{14,10},{16,12},{18,14},{20,16},{2... | collective-permute-start | bytes 786440 | tf_op jit(solution)/shard_map/ppermute | solution.py:37
  51.4 1.3 %collective-permute-start.11 = (bf16[2,128,512]{2,1,0:T(8,128)(2,1)S(1)}, bf16[2,128,512]{2,1,0:T(8,128)(2,1)S(1)}, u32[]{:S(2)}, u32[]{:S(2)}) collective-permute-start(bf16[2,128,512]{2,1,0:T(8,128)(2,1)S(1)} %copy-done.11), channel_id=1, source_target_pairs={{2,0},{8,2},{6,4},{12,6},{10,8},{16,10},{14,12},{20,14},{18,16},{2... | collective-permute-start | bytes 786440 | tf_op jit(solution)/shard_map/ppermute | solution.py:37
  52.7 7.1 %collective-permute-done.9.got = bf16[128,2048]{1,0:T(8,128)(2,1)S(1)} collective-permute-done((bf16[128,2048]{1,0:T(8,128)(2,1)}, bf16[128,2048]{1,0:T(8,128)(2,1)S(1)}, u32[]{:S(2)}, u32[]{:S(2)}) %collective-permute-start.9) | collective-permute-done | bytes 524320 | tf_op jit(solution)/shard_map/ppermute | solution.py:29
  61.1 1.9 %fill_in.1 = bf16[128,4096]{1,0:T(8,128)(2,1)} custom-call(s32[1]{0:T(128)} %bitcast.mine.refs_0_, bf16[128,2048]{1,0:T(8,128)(2,1)} %copy-done.10, bf16[128,4096]{1,0:T(8,128)(2,1)} %get-tuple-element.44.before), custom_call_target="tpu_custom_call", output_to_operand_aliasing={{}: (2, {})} | custom-call | flops 1000 | bytes 1 | tf_op jit(solution)/shard_map/fill_in/pallas_call | solution.py:479
  63.1 2.2 %collective-permute-done.12 = bf16[2,128,512]{2,1,0:T(8,128)(2,1)S(1)} collective-permute-done((bf16[2,128,512]{2,1,0:T(8,128)(2,1)S(1)}, bf16[2,128,512]{2,1,0:T(8,128)(2,1)S(1)}, u32[]{:S(2)}, u32[]{:S(2)}) %collective-permute-start.12) | collective-permute-done | bytes 262176 | tf_op jit(solution)/shard_map/ppermute | solution.py:37
  65.4 3.2 %collective-permute-done.15 = bf16[2,128,512]{2,1,0:T(8,128)(2,1)S(1)} collective-permute-done((bf16[2,128,512]{2,1,0:T(8,128)(2,1)S(1)}, bf16[2,128,512]{2,1,0:T(8,128)(2,1)S(1)}, u32[]{:S(2)}, u32[]{:S(2)}) %collective-permute-start.15) | collective-permute-done | bytes 262176 | tf_op jit(solution)/shard_map/ppermute | solution.py:29
  68.7 0.8 %slice_bitcast_fusion = (bf16[128,1024]{1,0:T(8,128)(2,1)}, bf16[128,1024]{1,0:T(8,128)(2,1)}) fusion(bf16[2,128,1024]{2,1,0:T(8,128)(2,1)S(1)} %maximum_select_fusion), kind=kLoop, calls=%fused_computation.7 | loop fusion | bytes 1048576 | tf_op jit(solution)/shard_map/squeeze | solution.py:494
  (46 shorter events, 4.4 us)
Async XLA Ops:
  1.8 10.0 %collective-permute-start.2 = (bf16[2,128,512]{2,1,0:T(8,128)(2,1)S(1)}, bf16[2,128,512]{2,1,0:T(8,128)(2,1)}, u32[]{:S(2)}, u32[]{:S(2)}) collective-permute-start(bf16[2,128,512]{2,1,0:T(8,128)(2,1)S(1)} %pad_maximum_fusion), channel_id=1, source_target_pairs={{0,1},{1,0},{2,3},{3,2},{4,5},{5,4},{6,7},{7,6},{8,9},{9,8},{10,11... | collective-permute-start | bytes 786440 | tf_op jit(solution)/shard_map/ppermute | solution.py:29
  5.6 12.8 %collective-permute-start.3 = (bf16[2,128,512]{2,1,0:T(8,128)(2,1)}, bf16[2,128,512]{2,1,0:T(8,128)(2,1)S(1)}, u32[]{:S(2)}, u32[]{:S(2)}) collective-permute-start(bf16[2,128,512]{2,1,0:T(8,128)(2,1)} %pad_maximum_fusion.1), channel_id=1, source_target_pairs={{0,4},{2,6},{4,8},{6,10},{8,12},{10,14},{12,16},{14,18},{16,20},{1... | collective-permute-start | bytes 786440 | tf_op jit(solution)/shard_map/ppermute | solution.py:37
  11.2 16.6 %copy-start = (bf16[128,4096]{1,0:T(8,128)(2,1)S(1)}, bf16[128,4096]{1,0:T(8,128)(2,1)}, u32[]{:S(2)}) copy-start(bf16[128,4096]{1,0:T(8,128)(2,1)} %refs_3_.3) | copy-start | bytes 3145732
  11.2 16.6 %copy-start.1 = (bf16[128,4096]{1,0:T(8,128)(2,1)S(1)}, bf16[128,4096]{1,0:T(8,128)(2,1)}, u32[]{:S(2)}) copy-start(bf16[128,4096]{1,0:T(8,128)(2,1)} %refs_5_.3) | copy-start | bytes 3145732
  11.2 16.6 %copy-start.2 = (bf16[128,1024]{1,0:T(8,128)(2,1)S(1)}, bf16[128,1024]{1,0:T(8,128)(2,1)}, u32[]{:S(2)}) copy-start(bf16[128,1024]{1,0:T(8,128)(2,1)} %refs_9_.3) | copy-start | bytes 786436
  11.2 16.6 %copy-start.3 = (bf16[128,1024]{1,0:T(8,128)(2,1)S(1)}, bf16[128,1024]{1,0:T(8,128)(2,1)}, u32[]{:S(2)}) copy-start(bf16[128,1024]{1,0:T(8,128)(2,1)} %refs_10_.3) | copy-start | bytes 786436
  11.2 16.5 %collective-permute-start.1 = (bf16[2,144,1024]{2,1,0:T(8,128)(2,1)}, bf16[2,144,1024]{2,1,0:T(8,128)(2,1)S(1)}, u32[]{:S(2)}, u32[]{:S(2)}) collective-permute-start(bf16[2,144,1024]{2,1,0:T(8,128)(2,1)} %get-tuple-element.31), channel_id=1, source_target_pairs={{0,1},{1,0},{2,3},{3,2},{4,5},{5,4},{6,7},{7,6},{8,9},{9,8},{10,11... | collective-permute-start | bytes 1769480 | tf_op jit(solution)/shard_map/ppermute | solution.py:29
  11.8 16.0 %copy-start.4 = (f32[2,1,2048]{2,1,0:T(1,128)S(1)}, f32[2,1,2048]{2,1,0:T(1,128)}, u32[]{:S(2)}) copy-start(f32[2,1,2048]{2,1,0:T(1,128)} %get-tuple-element.30.refs_7_) | copy-start | bytes 49156
  11.8 16.0 %copy-start.5 = (s32[1,4,4,2]{2,3,1,0:T(2,128)S(1)}, s32[1,4,4,2]{2,3,1,0:T(2,128)}, u32[]{:S(2)}) copy-start(s32[1,4,4,2]{2,3,1,0:T(2,128)} %param.14) | copy-start | bytes 388
  11.8 10.2 %collective-permute-start.6 = (bf16[2,128,512]{2,1,0:T(8,128)(2,1)}, bf16[2,128,512]{2,1,0:T(8,128)(2,1)S(1)}, u32[]{:S(2)}, u32[]{:S(2)}) collective-permute-start(bf16[2,128,512]{2,1,0:T(8,128)(2,1)} %pad_maximum_fusion.1), channel_id=1, source_target_pairs={{0,2},{2,8},{4,6},{6,12},{8,10},{10,16},{12,14},{14,20},{16,18},{1... | collective-permute-start | bytes 786440 | tf_op jit(solution)/shard_map/ppermute | solution.py:37
  13.3 9.3 %collective-permute-start.4 = (bf16[2,128,512]{2,1,0:T(8,128)(2,1)}, bf16[2,128,512]{2,1,0:T(8,128)(2,1)S(1)}, u32[]{:S(2)}, u32[]{:S(2)}) collective-permute-start(bf16[2,128,512]{2,1,0:T(8,128)(2,1)} %arrived.1.refs_11_), channel_id=1, source_target_pairs={{0,4},{2,6},{4,8},{6,10},{8,12},{10,14},{12,16},{14,18},{16,20},{1... | collective-permute-start | bytes 786440 | tf_op jit(solution)/shard_map/ppermute | solution.py:37
  16.7 20.5 %collective-permute-start = (bf16[2,128,1024]{2,1,0:T(8,128)(2,1)}, bf16[2,128,1024]{2,1,0:T(8,128)(2,1)S(1)}, u32[]{:S(2)}, u32[]{:S(2)}) collective-permute-start(bf16[2,128,1024]{2,1,0:T(8,128)(2,1)} %get-tuple-element.29), channel_id=1, source_target_pairs={{0,1},{1,0},{2,3},{3,2},{4,5},{5,4},{6,7},{7,6},{8,9},{9,8},{10,11... | collective-permute-start | bytes 1572872 | tf_op jit(solution)/shard_map/ppermute | solution.py:29
  18.3 5.5 %collective-permute-start.8 = (bf16[2,128,512]{2,1,0:T(8,128)(2,1)}, bf16[2,128,512]{2,1,0:T(8,128)(2,1)S(1)}, u32[]{:S(2)}, u32[]{:S(2)}) collective-permute-start(bf16[2,128,512]{2,1,0:T(8,128)(2,1)} %arrived.1.refs_11_), channel_id=1, source_target_pairs={{0,2},{2,8},{4,6},{6,12},{8,10},{10,16},{12,14},{14,20},{16,18},{1... | collective-permute-start | bytes 786440 | tf_op jit(solution)/shard_map/ppermute | solution.py:37
  22.0 1.9 %collective-permute-start.5 = (bf16[2,128,512]{2,1,0:T(8,128)(2,1)S(1)}, bf16[2,128,512]{2,1,0:T(8,128)(2,1)S(1)}, u32[]{:S(2)}, u32[]{:S(2)}) collective-permute-start(bf16[2,128,512]{2,1,0:T(8,128)(2,1)S(1)} %collective-permute-done.3.refs_12_), channel_id=1, source_target_pairs={{0,2},{2,0},{4,6},{6,4},{8,10},{10,8},{12,14},{14,12},{16,18},{18,... | collective-permute-start | bytes 786440 | tf_op jit(solution)/shard_map/ppermute | solution.py:29
  22.6 5.2 %collective-permute-start.7 = (bf16[2,128,512]{2,1,0:T(8,128)(2,1)S(1)}, bf16[2,128,512]{2,1,0:T(8,128)(2,1)S(1)}, u32[]{:S(2)}, u32[]{:S(2)}) collective-permute-start(bf16[2,128,512]{2,1,0:T(8,128)(2,1)S(1)} %collective-permute-done.4.refs_13_), channel_id=1, source_target_pairs={{0,2},{2,0},{4,6},{6,4},{8,10},{10,8},{12,14},{14,12},{16,18},{18,... | collective-permute-start | bytes 786440 | tf_op jit(solution)/shard_map/ppermute | solution.py:29
  45.2 2.2 %collective-permute-start.10 = (bf16[2,2,128,512]{3,2,1,0:T(8,128)(2,1)}, bf16[2,2,128,512]{3,2,1,0:T(8,128)(2,1)S(1)}, u32[]{:S(2)}, u32[]{:S(2)}) collective-permute-start(bf16[2,2,128,512]{3,2,1,0:T(8,128)(2,1)} %get-tuple-element.49), channel_id=1, source_target_pairs={{0,2},{2,0},{4,6},{6,4},{8,10},{10,8},{12,14},{14,12},{16,18},{18,... | collective-permute-start | bytes 1572872 | tf_op jit(solution)/shard_map/ppermute | solution.py:29
  45.3 14.6 %collective-permute-start.9 = (bf16[128,2048]{1,0:T(8,128)(2,1)}, bf16[128,2048]{1,0:T(8,128)(2,1)S(1)}, u32[]{:S(2)}, u32[]{:S(2)}) collective-permute-start(bf16[128,2048]{1,0:T(8,128)(2,1)} %get-tuple-element.43), channel_id=1, source_target_pairs={{0,1},{1,0},{2,3},{3,2},{4,5},{5,4},{6,7},{7,6},{8,9},{9,8},{10,11... | collective-permute-start | bytes 1572872 | tf_op jit(solution)/shard_map/ppermute | solution.py:29
  45.9 14.0 %collective-permute-start.13 = (bf16[2,128,512]{2,1,0:T(8,128)(2,1)}, bf16[2,128,512]{2,1,0:T(8,128)(2,1)S(1)}, u32[]{:S(2)}, u32[]{:S(2)}) collective-permute-start(bf16[2,128,512]{2,1,0:T(8,128)(2,1)} %get-tuple-element.54), channel_id=1, source_target_pairs={{2,0},{8,2},{6,4},{12,6},{10,8},{16,10},{14,12},{20,14},{18,16},{2... | collective-permute-start | bytes 786440 | tf_op jit(solution)/shard_map/ppermute | solution.py:37
  48.6 11.3 %collective-permute-start.14 = (bf16[2,128,512]{2,1,0:T(8,128)(2,1)S(1)}, bf16[2,128,512]{2,1,0:T(8,128)(2,1)S(1)}, u32[]{:S(2)}, u32[]{:S(2)}) collective-permute-start(bf16[2,128,512]{2,1,0:T(8,128)(2,1)S(1)} %fusion.1), channel_id=1, source_target_pairs={{4,0},{6,2},{8,4},{10,6},{12,8},{14,10},{16,12},{18,14},{20,16},{2... | collective-permute-start | bytes 786440 | tf_op jit(solution)/shard_map/ppermute | solution.py:37
  49.9 10.0 %copy-start.8 = (f32[2,128,512]{2,1,0:T(8,128)S(1)}, f32[2,128,512]{2,1,0:T(8,128)}, u32[]{:S(2)}) copy-start(f32[2,128,512]{2,1,0:T(8,128)} %get-tuple-element.53) | copy-start | bytes 1572868
  50.0 15.3 %collective-permute-start.12 = (bf16[2,128,512]{2,1,0:T(8,128)(2,1)S(1)}, bf16[2,128,512]{2,1,0:T(8,128)(2,1)S(1)}, u32[]{:S(2)}, u32[]{:S(2)}) collective-permute-start(bf16[2,128,512]{2,1,0:T(8,128)(2,1)S(1)} %fusion), channel_id=1, source_target_pairs={{4,0},{6,2},{8,4},{10,6},{12,8},{14,10},{16,12},{18,14},{20,16},{2... | collective-permute-start | bytes 786440 | tf_op jit(solution)/shard_map/ppermute | solution.py:37
  51.4 13.8 %collective-permute-start.11 = (bf16[2,128,512]{2,1,0:T(8,128)(2,1)S(1)}, bf16[2,128,512]{2,1,0:T(8,128)(2,1)S(1)}, u32[]{:S(2)}, u32[]{:S(2)}) collective-permute-start(bf16[2,128,512]{2,1,0:T(8,128)(2,1)S(1)} %copy-done.11), channel_id=1, source_target_pairs={{2,0},{8,2},{6,4},{12,6},{10,8},{16,10},{14,12},{20,14},{18,16},{2... | collective-permute-start | bytes 786440 | tf_op jit(solution)/shard_map/ppermute | solution.py:37
  60.6 7.9 %collective-permute-start.15 = (bf16[2,128,512]{2,1,0:T(8,128)(2,1)S(1)}, bf16[2,128,512]{2,1,0:T(8,128)(2,1)S(1)}, u32[]{:S(2)}, u32[]{:S(2)}) collective-permute-start(bf16[2,128,512]{2,1,0:T(8,128)(2,1)S(1)} %add_convert_fusion), channel_id=1, source_target_pairs={{0,1},{1,0},{2,3},{3,2},{4,5},{5,4},{6,7},{7,6},{8,9},{9,8},{10,11... | collective-permute-start | bytes 786440 | tf_op jit(solution)/shard_map/ppermute | solution.py:29
  61.1 4.1 %copy-start.7 = (f32[2,128,512]{2,1,0:T(8,128)S(1)}, f32[2,128,512]{2,1,0:T(8,128)}, u32[]{:S(2)}) copy-start(f32[2,128,512]{2,1,0:T(8,128)} %get-tuple-element.45) | copy-start | bytes 1572868
  (4 other events, 5.5 us)

commit v6 on v5

--- a/solution.py
+++ b/solution.py
@@ -450,7 +450,7 @@
     sources = {
         0: (keys, values, kv_far),
         1: (near_two, far_two),
-        2: (near_core, swap(after(far_two, near_odd), "ctx")),
+        2: (near_core, swap(far_two, "ctx")),
         3: (near_odd, far_odd),
     }
     def wide_sum(*terms):

time: 70.2 us -> 70.2 us (level)
  no operation moved by 1% of the time
where the time goes in v6:
time: 70.2 us; the launch traced here: 69.5 us
  starting transfers between devices  25.4 us (36%)
  Pallas kernels  20.1 us (29%)
  waiting for transfers between devices  17.5 us (25%)
  local copies, waits for them, and re-layouts  3.28 us (5%)
  other arithmetic  2.36 us (3%)
  between operations  0.88 us (1%)
    ppermute x8, starting transfers between devices, routed(): return lax.ppermute(value, 'ctx', pairs)  17.2 us
    pallas_call x2, Pallas kernels, attend(): pl.pallas_call(functools.partial(pair_kernel, part, group, tile_pairs.sha...  15.9 us
    ppermute x8, waiting for transfers between devices, swap(): lax.ppermute(value, axis, [(i, i ^ 1) for i in range(lax.axis_size(axis))])  15.3 us
    ppermute x8, starting transfers between devices, swap(): lax.ppermute(value, axis, [(i, i ^ 1) for i in range(lax.axis_size(axis))])  8.18 us
    pallas_call x1, Pallas kernels, by_pairs(): pl.pallas_call(functools.partial(pack_kernel, local_kv * group), out_shap...  2.24 us
    ppermute x8, waiting for transfers between devices, routed(): return lax.ppermute(value, 'ctx', pairs)  2.16 us
    pallas_call x1, Pallas kernels, by_pairs(): pl.pallas_call(fill_kernel, out_shape=jax.ShapeDtypeStruct(queries.shape,...  1.93 us
    convert_element_type x4, other arithmetic, wide_sum(): return sum((x.astype(jnp.float32) for x in terms)).astype(jnp.bfloat16)  1.47 us
  transfers between devices with their start and end apart: 16, of which 6 were waited for; matrix products, arithmetic and copies ran while one was open for 3% of the time, Pallas kernels for 17%

profile of v6, /device:TPU:0, one launch (start us, length us, event | category | flops | bytes accessed | tf_op | source)
XLA Modules:
  0.0 69.5 jit_solution(11554223449473812704)
XLA Ops:
  0.6 1.1 %dynamic-slice_bitcast_fusion = (bf16[1,128,512]{2,1,0:T(8,128)(2,1)S(1)}, bf16[1,128,512]{2,1,0:T(8,128)(2,1)S(1)}, bf16[1,128,512]{2,1,0:T(8,128)(2,1)S(1)}, bf16[1,128,512]{2,1,0:T(8,128)(2,1)S(1)}) fusion(bf16[128,1024]{1,0:T(8,128)(2,1)} %refs_10_.3, s32[]{:T(128)S(6)} %select_n.17, s32[]{:T(128)S(6)} %select_n.16, bf16[128,1024]{1,0:T(8,128)(2,1)} %refs_9_.3), kind=kLoop, calls=%fused_computation.13 | loop fusion | bytes 1048584 | tf_op jit(solution)/shard_map/stack | solution.py:356
  1.8 3.0 %collective-permute-start.2 = (bf16[2,128,512]{2,1,0:T(8,128)(2,1)S(1)}, bf16[2,128,512]{2,1,0:T(8,128)(2,1)}, u32[]{:S(2)}, u32[]{:S(2)}) collective-permute-start(bf16[2,128,512]{2,1,0:T(8,128)(2,1)S(1)} %pad_maximum_fusion), channel_id=1, source_target_pairs={{0,1},{1,0},{2,3},{3,2},{4,5},{5,4},{6,7},{7,6},{8,9},{9,8},{10,11... | collective-permute-start | bytes 786440 | tf_op jit(solution)/shard_map/ppermute | solution.py:29
  4.8 0.7 %pad_maximum_fusion.1 = bf16[2,128,512]{2,1,0:T(8,128)(2,1)} fusion(bf16[1,128,512]{2,1,0:T(8,128)(2,1)S(1)} %get-tuple-element.57, bf16[1,128,512]{2,1,0:T(8,128)(2,1)S(1)} %get-tuple-element.60), kind=kLoop, calls=%fused_computation.12 | loop fusion | flops 131072 | bytes 524288 | tf_op jit(solution)/shard_map/stack | solution.py:356
  5.6 3.4 %collective-permute-start.3 = (bf16[2,128,512]{2,1,0:T(8,128)(2,1)}, bf16[2,128,512]{2,1,0:T(8,128)(2,1)S(1)}, u32[]{:S(2)}, u32[]{:S(2)}) collective-permute-start(bf16[2,128,512]{2,1,0:T(8,128)(2,1)} %pad_maximum_fusion.1), channel_id=1, source_target_pairs={{0,4},{2,6},{4,8},{6,10},{8,12},{10,14},{12,16},{14,18},{16,20},{1... | collective-permute-start | bytes 786440 | tf_op jit(solution)/shard_map/ppermute | solution.py:37
  9.0 2.2 %pack_sends.1 = (bf16[2,144,1024]{2,1,0:T(8,128)(2,1)}, bf16[2,128,1024]{2,1,0:T(8,128)(2,1)}, f32[2,1,2048]{2,1,0:T(1,128)}) custom-call(s32[1]{0:T(128)} %bitcast.mine.refs_0_, bf16[128,4096]{1,0:T(8,128)(2,1)} %refs_3_.3, bf16[128,4096]{1,0:T(8,128)(2,1)} %refs_5_.3, f32[32,128]{1,0:T(8,128)} %bitcast.28, f32[32,128]{1,0:T(8,128)} %bitcast.29), custom_call_target="tpu_custom_call" | custom-call | flops 1000 | bytes 1 | tf_op jit(solution)/shard_map/pack_sends/pallas_call | solution.py:362
  11.8 1.4 %collective-permute-start.7 = (bf16[2,128,512]{2,1,0:T(8,128)(2,1)}, bf16[2,128,512]{2,1,0:T(8,128)(2,1)S(1)}, u32[]{:S(2)}, u32[]{:S(2)}) collective-permute-start(bf16[2,128,512]{2,1,0:T(8,128)(2,1)} %pad_maximum_fusion.1), channel_id=1, source_target_pairs={{0,2},{2,8},{4,6},{6,12},{8,10},{10,16},{12,14},{14,20},{16,18},{1... | collective-permute-start | bytes 786440 | tf_op jit(solution)/shard_map/ppermute | solution.py:37
  13.3 3.5 %collective-permute-start.4 = (bf16[2,128,512]{2,1,0:T(8,128)(2,1)}, bf16[2,128,512]{2,1,0:T(8,128)(2,1)S(1)}, u32[]{:S(2)}, u32[]{:S(2)}) collective-permute-start(bf16[2,128,512]{2,1,0:T(8,128)(2,1)} %arrived.1.refs_11_), channel_id=1, source_target_pairs={{0,4},{2,6},{4,8},{6,10},{8,12},{10,14},{12,16},{14,18},{16,20},{1... | collective-permute-start | bytes 786440 | tf_op jit(solution)/shard_map/ppermute | solution.py:37
  16.7 1.6 %collective-permute-start = (bf16[2,128,1024]{2,1,0:T(8,128)(2,1)}, bf16[2,128,1024]{2,1,0:T(8,128)(2,1)S(1)}, u32[]{:S(2)}, u32[]{:S(2)}) collective-permute-start(bf16[2,128,1024]{2,1,0:T(8,128)(2,1)} %get-tuple-element.28), channel_id=1, source_target_pairs={{0,1},{1,0},{2,3},{3,2},{4,5},{5,4},{6,7},{7,6},{8,9},{9,8},{10,11... | collective-permute-start | bytes 1572872 | tf_op jit(solution)/shard_map/ppermute | solution.py:29
  18.3 3.6 %collective-permute-start.8 = (bf16[2,128,512]{2,1,0:T(8,128)(2,1)}, bf16[2,128,512]{2,1,0:T(8,128)(2,1)S(1)}, u32[]{:S(2)}, u32[]{:S(2)}) collective-permute-start(bf16[2,128,512]{2,1,0:T(8,128)(2,1)} %arrived.1.refs_11_), channel_id=1, source_target_pairs={{0,2},{2,8},{4,6},{6,12},{8,10},{10,16},{12,14},{14,20},{16,18},{1... | collective-permute-start | bytes 786440 | tf_op jit(solution)/shard_map/ppermute | solution.py:37
  22.6 1.2 %collective-permute-start.6 = (bf16[2,128,512]{2,1,0:T(8,128)(2,1)S(1)}, bf16[2,128,512]{2,1,0:T(8,128)(2,1)S(1)}, u32[]{:S(2)}, u32[]{:S(2)}) collective-permute-start(bf16[2,128,512]{2,1,0:T(8,128)(2,1)S(1)} %collective-permute-done.4.refs_13_), channel_id=1, source_target_pairs={{0,2},{2,0},{4,6},{6,4},{8,10},{10,8},{12,14},{14,12},{16,18},{18,... | collective-permute-start | bytes 786440 | tf_op jit(solution)/shard_map/ppermute | solution.py:29
  23.8 3.9 %collective-permute-done.1.refs_4_.refs_6_.refs_8_ = bf16[2,144,1024]{2,1,0:T(8,128)(2,1)S(1)} collective-permute-done((bf16[2,144,1024]{2,1,0:T(8,128)(2,1)}, bf16[2,144,1024]{2,1,0:T(8,128)(2,1)S(1)}, u32[]{:S(2)}, u32[]{:S(2)}) %collective-permute-start.1) | collective-permute-done | bytes 589856 | tf_op jit(solution)/shard_map/ppermute | solution.py:29
  28.4 8.0 %grads_0123_part0.1 = (bf16[128,4096]{1,0:T(8,128)(2,1)}, bf16[128,2048]{1,0:T(8,128)(2,1)}, f32[2,128,512]{2,1,0:T(8,128)}, f32[2,128,512]{2,1,0:T(8,128)}, f32...) custom-call(s32[1]{0:T(128)} %bitcast.mine.refs_0_, ...), custom_call_target="tpu_custom_call" | custom-call | flops 1000 | bytes 1 | tf_op jit(solution)/shard_map/grads_0123_part0/pallas_call | solution.py:422
  36.4 0.9 %collective-permute-done.refs_4_.refs_6_ = bf16[2,128,1024]{2,1,0:T(8,128)(2,1)S(1)} collective-permute-done((bf16[2,128,1024]{2,1,0:T(8,128)(2,1)}, bf16[2,128,1024]{2,1,0:T(8,128)(2,1)S(1)}, u32[]{:S(2)}, u32[]{:S(2)}) %collective-permute-start) | collective-permute-done | bytes 524320 | tf_op jit(solution)/shard_map/ppermute | solution.py:29
  37.3 8.0 %grads_0123_part1.1 = (bf16[128,4096]{1,0:T(8,128)(2,1)}, bf16[128,2048]{1,0:T(8,128)(2,1)}, f32[2,128,512]{2,1,0:T(8,128)}, f32[2,128,512]{2,1,0:T(8,128)}, f32...) custom-call(s32[1]{0:T(128)} %bitcast.mine.refs_0_, ...), custom_call_target="tpu_custom_call", output_to_operand_aliasing={{0}: (18, {}), {1}: (19, {}), {2}: (20, {}), {3}: (21, {}),... | custom-call | flops 10000000000 | bytes 1 | tf_op jit(solution)/shard_map/grads_0123_part1/pallas_call | solution.py:422
  45.9 1.3 %collective-permute-start.13 = (bf16[2,128,512]{2,1,0:T(8,128)(2,1)}, bf16[2,128,512]{2,1,0:T(8,128)(2,1)S(1)}, u32[]{:S(2)}, u32[]{:S(2)}) collective-permute-start(bf16[2,128,512]{2,1,0:T(8,128)(2,1)} %get-tuple-element.52), channel_id=1, source_target_pairs={{2,0},{8,2},{6,4},{12,6},{10,8},{16,10},{14,12},{20,14},{18,16},{2... | collective-permute-start | bytes 786440 | tf_op jit(solution)/shard_map/ppermute | solution.py:37
  47.4 1.2 %fusion.1 = bf16[2,128,512]{2,1,0:T(8,128)(2,1)S(1)} fusion(f32[2,128,512]{2,1,0:T(8,128)} %get-tuple-element.46, bf16[2,2,128,512]{3,2,1,0:T(8,128)(2,1)S(1)} %collective-permute-done.10), kind=kLoop, calls=%fused_computation.4 | loop fusion | flops 393216 | bytes 1048576 | tf_op jit(solution)/shard_map/convert_element_type | solution.py:457
  48.6 1.3 %collective-permute-start.14 = (bf16[2,128,512]{2,1,0:T(8,128)(2,1)S(1)}, bf16[2,128,512]{2,1,0:T(8,128)(2,1)S(1)}, u32[]{:S(2)}, u32[]{:S(2)}) collective-permute-start(bf16[2,128,512]{2,1,0:T(8,128)(2,1)S(1)} %fusion.1), channel_id=1, source_target_pairs={{4,0},{6,2},{8,4},{10,6},{12,8},{14,10},{16,12},{18,14},{20,16},{2... | collective-permute-start | bytes 786440 | tf_op jit(solution)/shard_map/ppermute | solution.py:37
  50.0 1.4 %collective-permute-start.12 = (bf16[2,128,512]{2,1,0:T(8,128)(2,1)S(1)}, bf16[2,128,512]{2,1,0:T(8,128)(2,1)S(1)}, u32[]{:S(2)}, u32[]{:S(2)}) collective-permute-start(bf16[2,128,512]{2,1,0:T(8,128)(2,1)S(1)} %fusion), channel_id=1, source_target_pairs={{4,0},{6,2},{8,4},{10,6},{12,8},{14,10},{16,12},{18,14},{20,16},{2... | collective-permute-start | bytes 786440 | tf_op jit(solution)/shard_map/ppermute | solution.py:37
  51.4 1.3 %collective-permute-start.11 = (bf16[2,128,512]{2,1,0:T(8,128)(2,1)S(1)}, bf16[2,128,512]{2,1,0:T(8,128)(2,1)S(1)}, u32[]{:S(2)}, u32[]{:S(2)}) collective-permute-start(bf16[2,128,512]{2,1,0:T(8,128)(2,1)S(1)} %copy-done.11), channel_id=1, source_target_pairs={{2,0},{8,2},{6,4},{12,6},{10,8},{16,10},{14,12},{20,14},{18,16},{2... | collective-permute-start | bytes 786440 | tf_op jit(solution)/shard_map/ppermute | solution.py:37
  52.7 7.1 %collective-permute-done.9.got = bf16[128,2048]{1,0:T(8,128)(2,1)S(1)} collective-permute-done((bf16[128,2048]{1,0:T(8,128)(2,1)}, bf16[128,2048]{1,0:T(8,128)(2,1)S(1)}, u32[]{:S(2)}, u32[]{:S(2)}) %collective-permute-start.9) | collective-permute-done | bytes 524320 | tf_op jit(solution)/shard_map/ppermute | solution.py:29
  61.2 1.9 %fill_in.1 = bf16[128,4096]{1,0:T(8,128)(2,1)} custom-call(s32[1]{0:T(128)} %bitcast.mine.refs_0_, bf16[128,2048]{1,0:T(8,128)(2,1)} %copy-done.10, bf16[128,4096]{1,0:T(8,128)(2,1)} %get-tuple-element.42.before), custom_call_target="tpu_custom_call", output_to_operand_aliasing={{}: (2, {})} | custom-call | flops 1000 | bytes 1 | tf_op jit(solution)/shard_map/fill_in/pallas_call | solution.py:479
  63.1 2.1 %collective-permute-done.12 = bf16[2,128,512]{2,1,0:T(8,128)(2,1)S(1)} collective-permute-done((bf16[2,128,512]{2,1,0:T(8,128)(2,1)S(1)}, bf16[2,128,512]{2,1,0:T(8,128)(2,1)S(1)}, u32[]{:S(2)}, u32[]{:S(2)}) %collective-permute-start.12) | collective-permute-done | bytes 262176 | tf_op jit(solution)/shard_map/ppermute | solution.py:37
  65.4 3.2 %collective-permute-done.15 = bf16[2,128,512]{2,1,0:T(8,128)(2,1)S(1)} collective-permute-done((bf16[2,128,512]{2,1,0:T(8,128)(2,1)S(1)}, bf16[2,128,512]{2,1,0:T(8,128)(2,1)S(1)}, u32[]{:S(2)}, u32[]{:S(2)}) %collective-permute-start.15) | collective-permute-done | bytes 262176 | tf_op jit(solution)/shard_map/ppermute | solution.py:29
  68.7 0.8 %slice_bitcast_fusion = (bf16[128,1024]{1,0:T(8,128)(2,1)}, bf16[128,1024]{1,0:T(8,128)(2,1)}) fusion(bf16[2,128,1024]{2,1,0:T(8,128)(2,1)S(1)} %maximum_select_fusion), kind=kLoop, calls=%fused_computation.7 | loop fusion | bytes 1048576 | tf_op jit(solution)/shard_map/squeeze | solution.py:494
  (46 shorter events, 4.4 us)
Async XLA Ops:
  1.8 10.0 %collective-permute-start.2 = (bf16[2,128,512]{2,1,0:T(8,128)(2,1)S(1)}, bf16[2,128,512]{2,1,0:T(8,128)(2,1)}, u32[]{:S(2)}, u32[]{:S(2)}) collective-permute-start(bf16[2,128,512]{2,1,0:T(8,128)(2,1)S(1)} %pad_maximum_fusion), channel_id=1, source_target_pairs={{0,1},{1,0},{2,3},{3,2},{4,5},{5,4},{6,7},{7,6},{8,9},{9,8},{10,11... | collective-permute-start | bytes 786440 | tf_op jit(solution)/shard_map/ppermute | solution.py:29
  5.6 12.8 %collective-permute-start.3 = (bf16[2,128,512]{2,1,0:T(8,128)(2,1)}, bf16[2,128,512]{2,1,0:T(8,128)(2,1)S(1)}, u32[]{:S(2)}, u32[]{:S(2)}) collective-permute-start(bf16[2,128,512]{2,1,0:T(8,128)(2,1)} %pad_maximum_fusion.1), channel_id=1, source_target_pairs={{0,4},{2,6},{4,8},{6,10},{8,12},{10,14},{12,16},{14,18},{16,20},{1... | collective-permute-start | bytes 786440 | tf_op jit(solution)/shard_map/ppermute | solution.py:37
  11.2 16.6 %copy-start = (bf16[128,4096]{1,0:T(8,128)(2,1)S(1)}, bf16[128,4096]{1,0:T(8,128)(2,1)}, u32[]{:S(2)}) copy-start(bf16[128,4096]{1,0:T(8,128)(2,1)} %refs_3_.3) | copy-start | bytes 3145732
  11.2 16.6 %copy-start.1 = (bf16[128,4096]{1,0:T(8,128)(2,1)S(1)}, bf16[128,4096]{1,0:T(8,128)(2,1)}, u32[]{:S(2)}) copy-start(bf16[128,4096]{1,0:T(8,128)(2,1)} %refs_5_.3) | copy-start | bytes 3145732
  11.2 16.6 %copy-start.2 = (bf16[128,1024]{1,0:T(8,128)(2,1)S(1)}, bf16[128,1024]{1,0:T(8,128)(2,1)}, u32[]{:S(2)}) copy-start(bf16[128,1024]{1,0:T(8,128)(2,1)} %refs_9_.3) | copy-start | bytes 786436
  11.2 16.6 %copy-start.3 = (bf16[128,1024]{1,0:T(8,128)(2,1)S(1)}, bf16[128,1024]{1,0:T(8,128)(2,1)}, u32[]{:S(2)}) copy-start(bf16[128,1024]{1,0:T(8,128)(2,1)} %refs_10_.3) | copy-start | bytes 786436
  11.2 16.5 %collective-permute-start.1 = (bf16[2,144,1024]{2,1,0:T(8,128)(2,1)}, bf16[2,144,1024]{2,1,0:T(8,128)(2,1)S(1)}, u32[]{:S(2)}, u32[]{:S(2)}) collective-permute-start(bf16[2,144,1024]{2,1,0:T(8,128)(2,1)} %get-tuple-element.30), channel_id=1, source_target_pairs={{0,1},{1,0},{2,3},{3,2},{4,5},{5,4},{6,7},{7,6},{8,9},{9,8},{10,11... | collective-permute-start | bytes 1769480 | tf_op jit(solution)/shard_map/ppermute | solution.py:29
  11.8 16.0 %copy-start.4 = (f32[2,1,2048]{2,1,0:T(1,128)S(1)}, f32[2,1,2048]{2,1,0:T(1,128)}, u32[]{:S(2)}) copy-start(f32[2,1,2048]{2,1,0:T(1,128)} %get-tuple-element.29.refs_7_) | copy-start | bytes 49156
  11.8 16.0 %copy-start.5 = (s32[1,4,4,2]{2,3,1,0:T(2,128)S(1)}, s32[1,4,4,2]{2,3,1,0:T(2,128)}, u32[]{:S(2)}) copy-start(s32[1,4,4,2]{2,3,1,0:T(2,128)} %param.14) | copy-start | bytes 388
  11.8 10.2 %collective-permute-start.7 = (bf16[2,128,512]{2,1,0:T(8,128)(2,1)}, bf16[2,128,512]{2,1,0:T(8,128)(2,1)S(1)}, u32[]{:S(2)}, u32[]{:S(2)}) collective-permute-start(bf16[2,128,512]{2,1,0:T(8,128)(2,1)} %pad_maximum_fusion.1), channel_id=1, source_target_pairs={{0,2},{2,8},{4,6},{6,12},{8,10},{10,16},{12,14},{14,20},{16,18},{1... | collective-permute-start | bytes 786440 | tf_op jit(solution)/shard_map/ppermute | solution.py:37
  13.3 9.3 %collective-permute-start.4 = (bf16[2,128,512]{2,1,0:T(8,128)(2,1)}, bf16[2,128,512]{2,1,0:T(8,128)(2,1)S(1)}, u32[]{:S(2)}, u32[]{:S(2)}) collective-permute-start(bf16[2,128,512]{2,1,0:T(8,128)(2,1)} %arrived.1.refs_11_), channel_id=1, source_target_pairs={{0,4},{2,6},{4,8},{6,10},{8,12},{10,14},{12,16},{14,18},{16,20},{1... | collective-permute-start | bytes 786440 | tf_op jit(solution)/shard_map/ppermute | solution.py:37
  16.7 20.5 %collective-permute-start = (bf16[2,128,1024]{2,1,0:T(8,128)(2,1)}, bf16[2,128,1024]{2,1,0:T(8,128)(2,1)S(1)}, u32[]{:S(2)}, u32[]{:S(2)}) collective-permute-start(bf16[2,128,1024]{2,1,0:T(8,128)(2,1)} %get-tuple-element.28), channel_id=1, source_target_pairs={{0,1},{1,0},{2,3},{3,2},{4,5},{5,4},{6,7},{7,6},{8,9},{9,8},{10,11... | collective-permute-start | bytes 1572872 | tf_op jit(solution)/shard_map/ppermute | solution.py:29
  18.3 5.5 %collective-permute-start.8 = (bf16[2,128,512]{2,1,0:T(8,128)(2,1)}, bf16[2,128,512]{2,1,0:T(8,128)(2,1)S(1)}, u32[]{:S(2)}, u32[]{:S(2)}) collective-permute-start(bf16[2,128,512]{2,1,0:T(8,128)(2,1)} %arrived.1.refs_11_), channel_id=1, source_target_pairs={{0,2},{2,8},{4,6},{6,12},{8,10},{10,16},{12,14},{14,20},{16,18},{1... | collective-permute-start | bytes 786440 | tf_op jit(solution)/shard_map/ppermute | solution.py:37
  22.0 1.9 %collective-permute-start.5 = (bf16[2,128,512]{2,1,0:T(8,128)(2,1)S(1)}, bf16[2,128,512]{2,1,0:T(8,128)(2,1)S(1)}, u32[]{:S(2)}, u32[]{:S(2)}) collective-permute-start(bf16[2,128,512]{2,1,0:T(8,128)(2,1)S(1)} %collective-permute-done.3.refs_12_), channel_id=1, source_target_pairs={{0,2},{2,0},{4,6},{6,4},{8,10},{10,8},{12,14},{14,12},{16,18},{18,... | collective-permute-start | bytes 786440 | tf_op jit(solution)/shard_map/ppermute | solution.py:29
  22.6 5.2 %collective-permute-start.6 = (bf16[2,128,512]{2,1,0:T(8,128)(2,1)S(1)}, bf16[2,128,512]{2,1,0:T(8,128)(2,1)S(1)}, u32[]{:S(2)}, u32[]{:S(2)}) collective-permute-start(bf16[2,128,512]{2,1,0:T(8,128)(2,1)S(1)} %collective-permute-done.4.refs_13_), channel_id=1, source_target_pairs={{0,2},{2,0},{4,6},{6,4},{8,10},{10,8},{12,14},{14,12},{16,18},{18,... | collective-permute-start | bytes 786440 | tf_op jit(solution)/shard_map/ppermute | solution.py:29
  45.2 2.2 %collective-permute-start.10 = (bf16[2,2,128,512]{3,2,1,0:T(8,128)(2,1)}, bf16[2,2,128,512]{3,2,1,0:T(8,128)(2,1)S(1)}, u32[]{:S(2)}, u32[]{:S(2)}) collective-permute-start(bf16[2,2,128,512]{3,2,1,0:T(8,128)(2,1)} %get-tuple-element.47), channel_id=1, source_target_pairs={{0,2},{2,0},{4,6},{6,4},{8,10},{10,8},{12,14},{14,12},{16,18},{18,... | collective-permute-start | bytes 1572872 | tf_op jit(solution)/shard_map/ppermute | solution.py:29
  45.3 14.6 %collective-permute-start.9 = (bf16[128,2048]{1,0:T(8,128)(2,1)}, bf16[128,2048]{1,0:T(8,128)(2,1)S(1)}, u32[]{:S(2)}, u32[]{:S(2)}) collective-permute-start(bf16[128,2048]{1,0:T(8,128)(2,1)} %get-tuple-element.41), channel_id=1, source_target_pairs={{0,1},{1,0},{2,3},{3,2},{4,5},{5,4},{6,7},{7,6},{8,9},{9,8},{10,11... | collective-permute-start | bytes 1572872 | tf_op jit(solution)/shard_map/ppermute | solution.py:29
  45.9 14.0 %collective-permute-start.13 = (bf16[2,128,512]{2,1,0:T(8,128)(2,1)}, bf16[2,128,512]{2,1,0:T(8,128)(2,1)S(1)}, u32[]{:S(2)}, u32[]{:S(2)}) collective-permute-start(bf16[2,128,512]{2,1,0:T(8,128)(2,1)} %get-tuple-element.52), channel_id=1, source_target_pairs={{2,0},{8,2},{6,4},{12,6},{10,8},{16,10},{14,12},{20,14},{18,16},{2... | collective-permute-start | bytes 786440 | tf_op jit(solution)/shard_map/ppermute | solution.py:37
  48.6 11.3 %collective-permute-start.14 = (bf16[2,128,512]{2,1,0:T(8,128)(2,1)S(1)}, bf16[2,128,512]{2,1,0:T(8,128)(2,1)S(1)}, u32[]{:S(2)}, u32[]{:S(2)}) collective-permute-start(bf16[2,128,512]{2,1,0:T(8,128)(2,1)S(1)} %fusion.1), channel_id=1, source_target_pairs={{4,0},{6,2},{8,4},{10,6},{12,8},{14,10},{16,12},{18,14},{20,16},{2... | collective-permute-start | bytes 786440 | tf_op jit(solution)/shard_map/ppermute | solution.py:37
  49.9 10.0 %copy-start.8 = (f32[2,128,512]{2,1,0:T(8,128)S(1)}, f32[2,128,512]{2,1,0:T(8,128)}, u32[]{:S(2)}) copy-start(f32[2,128,512]{2,1,0:T(8,128)} %get-tuple-element.51) | copy-start | bytes 1572868
  50.0 15.2 %collective-permute-start.12 = (bf16[2,128,512]{2,1,0:T(8,128)(2,1)S(1)}, bf16[2,128,512]{2,1,0:T(8,128)(2,1)S(1)}, u32[]{:S(2)}, u32[]{:S(2)}) collective-permute-start(bf16[2,128,512]{2,1,0:T(8,128)(2,1)S(1)} %fusion), channel_id=1, source_target_pairs={{4,0},{6,2},{8,4},{10,6},{12,8},{14,10},{16,12},{18,14},{20,16},{2... | collective-permute-start | bytes 786440 | tf_op jit(solution)/shard_map/ppermute | solution.py:37
  51.4 13.8 %collective-permute-start.11 = (bf16[2,128,512]{2,1,0:T(8,128)(2,1)S(1)}, bf16[2,128,512]{2,1,0:T(8,128)(2,1)S(1)}, u32[]{:S(2)}, u32[]{:S(2)}) collective-permute-start(bf16[2,128,512]{2,1,0:T(8,128)(2,1)S(1)} %copy-done.11), channel_id=1, source_target_pairs={{2,0},{8,2},{6,4},{12,6},{10,8},{16,10},{14,12},{20,14},{18,16},{2... | collective-permute-start | bytes 786440 | tf_op jit(solution)/shard_map/ppermute | solution.py:37
  60.7 7.9 %collective-permute-start.15 = (bf16[2,128,512]{2,1,0:T(8,128)(2,1)S(1)}, bf16[2,128,512]{2,1,0:T(8,128)(2,1)S(1)}, u32[]{:S(2)}, u32[]{:S(2)}) collective-permute-start(bf16[2,128,512]{2,1,0:T(8,128)(2,1)S(1)} %add_convert_fusion), channel_id=1, source_target_pairs={{0,1},{1,0},{2,3},{3,2},{4,5},{5,4},{6,7},{7,6},{8,9},{9,8},{10,11... | collective-permute-start | bytes 786440 | tf_op jit(solution)/shard_map/ppermute | solution.py:29
  61.2 4.1 %copy-start.7 = (f32[2,128,512]{2,1,0:T(8,128)S(1)}, f32[2,128,512]{2,1,0:T(8,128)}, u32[]{:S(2)}) copy-start(f32[2,128,512]{2,1,0:T(8,128)} %get-tuple-element.43) | copy-start | bytes 1572868
  (4 other events, 5.5 us)
